TPU v7x, 32 devices: a whole 2x2x4 slice. The times are simulated.
32 devices in a mesh: rep: 4 (over z), fsdp: 4 (over y, x), seq: 2 (over core).
Axes of the slice: x: 2, y: 2, z: 4, core: 2. Of those that a mesh axis runs over, the one named last changes fastest.
Arguments:
- tokens: bfloat16 [32, 1024, 1024], P(('rep', 'fsdp'), 'seq'), may hold values from -6 to 6
- segment_ids: int32 [32, 1024], P(('rep', 'fsdp'), 'seq'), may hold values from 0 to 3, as said below
- padding: int32 [32, 1024], P(('rep', 'fsdp'), 'seq'), may hold values from 0 to 1, as said below
- cotangent: bfloat16 [32, 1024, 1024], P(('rep', 'fsdp'), 'seq'), may hold values from -6 to 6
- w_query: bfloat16 [1024, 1024], P(('fsdp', 'seq')), may hold values from -0.25 to 0.25
- w_key: bfloat16 [1024, 1024], P(('fsdp', 'seq')), may hold values from -0.1875 to 0.1875
- w_value: bfloat16 [1024, 1024], P(('fsdp', 'seq')), may hold values from -0.1875 to 0.1875
- w_out: bfloat16 [1024, 1024], P(('fsdp', 'seq')), may hold values from -0.75 to 0.75
- b_query: bfloat16 [1024], P(('fsdp', 'seq')), may hold values from -3 to 3
- b_value: bfloat16 [1024], P(('fsdp', 'seq')), may hold values from -3 to 3
- b_out: bfloat16 [1024], P(('fsdp', 'seq')), may hold values from -3 to 3
- gain_one: bfloat16 [1024], P(('fsdp', 'seq')), may hold values from 0.099609375 to 1.8984375
- shift_one: bfloat16 [1024], P(('fsdp', 'seq')), may hold values from -3 to 3
- w_up: bfloat16 [1024, 4096], P(('fsdp', 'seq')), may hold values from -0.1875 to 0.1875
- b_up: bfloat16 [4096], P(('fsdp', 'seq')), may hold values from -3 to 3
- w_down: bfloat16 [4096, 1024], P(('fsdp', 'seq')), may hold values from -0.09375 to 0.09375
- b_down: bfloat16 [1024], P(('fsdp', 'seq')), may hold values from -3 to 3
- gain_two: bfloat16 [1024], P(('fsdp', 'seq')), may hold values from 0.099609375 to 1.8984375
- shift_two: bfloat16 [1024], P(('fsdp', 'seq')), may hold values from -3 to 3
Outputs:
- output: bfloat16 [32, 1024, 1024], P(('rep', 'fsdp'), 'seq')
- input_grad: float32 [32, 1024, 1024], P(('rep', 'fsdp'), 'seq')
- grad_w_query: float32 [1024, 1024], P(('fsdp', 'seq'))
- grad_w_key: float32 [1024, 1024], P(('fsdp', 'seq'))
- grad_w_value: float32 [1024, 1024], P(('fsdp', 'seq'))
- grad_w_out: float32 [1024, 1024], P(('fsdp', 'seq'))
- grad_b_query: float32 [1024], P(('fsdp', 'seq'))
- grad_b_value: float32 [1024], P(('fsdp', 'seq'))
- grad_b_out: float32 [1024], P(('fsdp', 'seq'))
- grad_gain_one: float32 [1024], P(('fsdp', 'seq'))
- grad_shift_one: float32 [1024], P(('fsdp', 'seq'))
- grad_w_up: float32 [1024, 4096], P(('fsdp', 'seq'))
- grad_b_up: float32 [4096], P(('fsdp', 'seq'))
- grad_w_down: float32 [4096, 1024], P(('fsdp', 'seq'))
- grad_b_down: float32 [1024], P(('fsdp', 'seq'))
- grad_gain_two: float32 [1024], P(('fsdp', 'seq'))
- grad_shift_two: float32 [1024], P(('fsdp', 'seq'))
Inputs may be any that keep to these rules, and one draw needn't show every extreme that they name: `segment_ids`: along each sequence the ids never fall and start at 0; every document holds a real token; some document of each sequence holds tokens of the first and of the third quarter of the sequence. `padding`: within each sequence the padded tokens form its tail, of 1 to 128 tokens, inside its last document.
All inputs are finite; a program needn't handle non-finite values.
Results may differ from a plain program's by a relative error of at most 0.014.
Values may be sent and summed in bfloat16 or wider, within the bound.
No kernel may reach another device: no remote copies, remote signals or barrier semaphores. Data moves between devices by JAX's collectives and lax.ppermute only.
A program may use at most 320 MiB of HBM per device.

v0:
```python
import jax
import jax.numpy as jnp
from jax import lax
from jax.sharding import PartitionSpec as P

HEAD_DIM = 64


EPSILON = 1e-05
MASKED = -1e30
ROOT_HALF = 0.7071067811865476
INV_ROOT_TAU = 0.3989422804014327


def matmul_rows(left, right):
    return jnp.dot(left, right, preferred_element_type=jnp.float32)


def matmul_left_t(left, right):
    return lax.dot_general(
        left, right, (((0,), (0,)), ((), ())), preferred_element_type=jnp.float32
    )


def matmul_right_t(left, right):
    return lax.dot_general(
        left, right, (((1,), (1,)), ((), ())), preferred_element_type=jnp.float32
    )


def norm_forward(values, gain, shift):
    centred = values - jnp.mean(values, -1, keepdims=True)
    variance = jnp.mean(centred * centred, -1, keepdims=True)
    inverse = lax.rsqrt(variance + EPSILON)
    normed = centred * inverse
    return (normed * gain.astype(jnp.float32) + shift.astype(jnp.float32), normed, inverse)


def norm_backward(incoming, normed, inverse, gain):
    scaled = incoming * gain.astype(jnp.float32)
    return inverse * (
        scaled
        - jnp.mean(scaled, -1, keepdims=True)
        - normed * jnp.mean(scaled * normed, -1, keepdims=True)
    )


def split_heads(matrix):
    return matrix.reshape(matrix.shape[0], matrix.shape[1] // HEAD_DIM, HEAD_DIM)


def score_block(queries, keys_seq, seg_query, seg_key, keep_key):
    scores = jnp.einsum(
        "qhd,khd->hqk",
        split_heads(queries),
        split_heads(keys_seq),
        preferred_element_type=jnp.float32,
    ) * HEAD_DIM ** (-0.5)
    allowed = (seg_query.astype(jnp.float32)[:, None] == seg_key.astype(jnp.float32)[None, :]) & (
        keep_key.astype(jnp.float32)[None, :] > 0.5
    )
    return jnp.where(allowed[None], scores, MASKED)


def attend_forward(inputs):
    queries, keys_seq, values_seq, seg_query, seg_key, keep_key = inputs
    scores = score_block(queries, keys_seq, seg_query, seg_key, keep_key)
    top_score = jnp.max(scores, -1, keepdims=True)
    shifted = jnp.exp(scores - top_score)
    total = jnp.sum(shifted, -1, keepdims=True)
    attn_probs = (shifted / total).astype(jnp.bfloat16)
    mixed_heads = jnp.einsum(
        "hqk,khd->qhd", attn_probs, split_heads(values_seq), preferred_element_type=jnp.float32
    )
    return (
        mixed_heads.reshape(queries.shape).astype(jnp.bfloat16),
        (top_score + jnp.log(total))[..., 0],
    )


def attend_backward(inputs):
    queries, keys_seq, values_seq, seg_query, seg_key, keep_key, log_total, grad_mixed = inputs
    scores = score_block(queries, keys_seq, seg_query, seg_key, keep_key)
    attn_probs = jnp.exp(scores - log_total[..., None])
    grad_probs = jnp.einsum(
        "qhd,khd->hqk",
        split_heads(grad_mixed),
        split_heads(values_seq),
        preferred_element_type=jnp.float32,
    )
    row_dot = jnp.sum(attn_probs * grad_probs, -1, keepdims=True)
    grad_scores = (attn_probs * (grad_probs - row_dot)).astype(jnp.bfloat16)
    scale_factor = HEAD_DIM ** (-0.5)
    grad_query = (
        jnp.einsum(
            "hqk,khd->qhd", grad_scores, split_heads(keys_seq), preferred_element_type=jnp.float32
        )
        * scale_factor
    )
    grad_key = (
        jnp.einsum(
            "hqk,qhd->khd", grad_scores, split_heads(queries), preferred_element_type=jnp.float32
        )
        * scale_factor
    )
    grad_value = jnp.einsum(
        "hqk,qhd->khd",
        attn_probs.astype(jnp.bfloat16),
        split_heads(grad_mixed),
        preferred_element_type=jnp.float32,
    )
    return (
        grad_query.reshape(queries.shape).astype(jnp.bfloat16),
        grad_key.reshape(keys_seq.shape),
        grad_value.reshape(values_seq.shape),
    )


def column_sum(matrix):
    return jnp.sum(matrix.astype(jnp.float32), 0)


def body(
    tokens,
    segment_ids,
    padding,
    cotangent,
    w_query,
    w_key,
    w_value,
    w_out,
    b_query,
    b_value,
    b_out,
    gain_one,
    shift_one,
    w_up,
    b_up,
    w_down,
    b_down,
    gain_two,
    shift_two,
):
    seq_count, part_len, width = tokens.shape
    tok_count = seq_count * part_len
    tok_rows = tokens.reshape(tok_count, width)
    inputs_f = tok_rows.astype(jnp.float32)
    (
        full_query,
        full_key,
        full_value,
        full_out,
        bias_query,
        bias_value,
        bias_out,
        gain_first,
        shift_first,
    ) = (
        lax.all_gather(w_query, ("fsdp", "seq"), axis=0, tiled=True),
        lax.all_gather(w_key, ("fsdp", "seq"), axis=0, tiled=True),
        lax.all_gather(w_value, ("fsdp", "seq"), axis=0, tiled=True),
        lax.all_gather(w_out, ("fsdp", "seq"), axis=0, tiled=True),
        lax.all_gather(b_query, ("fsdp", "seq"), axis=0, tiled=True),
        lax.all_gather(b_value, ("fsdp", "seq"), axis=0, tiled=True),
        lax.all_gather(b_out, ("fsdp", "seq"), axis=0, tiled=True),
        lax.all_gather(gain_one, ("fsdp", "seq"), axis=0, tiled=True),
        lax.all_gather(shift_one, ("fsdp", "seq"), axis=0, tiled=True),
    )
    query_rows = (matmul_rows(tok_rows, full_query) + bias_query.astype(jnp.float32)).astype(
        jnp.bfloat16
    )
    key_rows = matmul_rows(tok_rows, full_key).astype(jnp.bfloat16)
    value_rows = (matmul_rows(tok_rows, full_value) + bias_value.astype(jnp.float32)).astype(
        jnp.bfloat16
    )
    query_parts = query_rows.reshape(seq_count, part_len, width)
    key_parts = key_rows.reshape(seq_count, part_len, width)
    value_parts = value_rows.reshape(seq_count, part_len, width)
    key_seq, value_seq, seg_keys, keep_keys = (
        lax.all_gather(key_parts, "seq", axis=1, tiled=True),
        lax.all_gather(value_parts, "seq", axis=1, tiled=True),
        lax.all_gather(segment_ids.astype(jnp.bfloat16), "seq", axis=1, tiled=True),
        lax.all_gather(padding.astype(jnp.bfloat16), "seq", axis=1, tiled=True),
    )
    mixed_parts, log_totals = lax.map(
        attend_forward, (query_parts, key_seq, value_seq, segment_ids, seg_keys, keep_keys)
    )
    mixed_rows = mixed_parts.reshape(tok_count, width)
    branch = matmul_rows(mixed_rows, full_out) + bias_out.astype(jnp.float32)
    first, normed_one, inverse_one = norm_forward(inputs_f + branch, gain_first, shift_first)
    first_low = first.astype(jnp.bfloat16)
    full_up, full_down, bias_up, bias_down, gain_second, shift_second = (
        lax.all_gather(w_up, ("fsdp", "seq"), axis=0, tiled=True),
        lax.all_gather(w_down, ("fsdp", "seq"), axis=0, tiled=True),
        lax.all_gather(b_up, ("fsdp", "seq"), axis=0, tiled=True),
        lax.all_gather(b_down, ("fsdp", "seq"), axis=0, tiled=True),
        lax.all_gather(gain_two, ("fsdp", "seq"), axis=0, tiled=True),
        lax.all_gather(shift_two, ("fsdp", "seq"), axis=0, tiled=True),
    )
    hidden = matmul_rows(first_low, full_up) + bias_up.astype(jnp.float32)
    cumulative = 0.5 * (1.0 + lax.erf(hidden * ROOT_HALF))
    activated = (hidden * cumulative).astype(jnp.bfloat16)
    second = matmul_rows(activated, full_down) + bias_down.astype(jnp.float32)
    result, normed_two, inverse_two = norm_forward(first + second, gain_second, shift_second)
    output = result.astype(jnp.bfloat16).reshape(tokens.shape)
    grad_result = cotangent.reshape(tok_count, width).astype(jnp.float32)
    grad_gain_two = jnp.sum(grad_result * normed_two, 0)
    grad_shift_two = jnp.sum(grad_result, 0)
    grad_sum_two = norm_backward(grad_result, normed_two, inverse_two, gain_second)
    back_up, back_down = (
        lax.all_gather(w_up, ("fsdp", "seq"), axis=0, tiled=True),
        lax.all_gather(w_down, ("fsdp", "seq"), axis=0, tiled=True),
    )
    grad_second = grad_sum_two.astype(jnp.bfloat16)
    grad_bias_down = column_sum(grad_second)
    grad_down = matmul_left_t(activated, grad_second)
    grad_act = matmul_right_t(grad_second, back_down)
    density = jnp.exp(-0.5 * hidden * hidden) * INV_ROOT_TAU
    grad_hidden = (grad_act * (cumulative + hidden * density)).astype(jnp.bfloat16)
    grad_bias_up = column_sum(grad_hidden)
    grad_up = matmul_left_t(first_low, grad_hidden)
    grad_first = grad_sum_two + matmul_right_t(grad_hidden, back_up)
    grad_gain_one = jnp.sum(grad_first * normed_one, 0)
    grad_shift_one = jnp.sum(grad_first, 0)
    grad_sum_one = norm_backward(grad_first, normed_one, inverse_one, gain_first)
    grad_branch = grad_sum_one.astype(jnp.bfloat16)
    grad_bias_out = column_sum(grad_branch)
    grad_out_weight = matmul_left_t(mixed_rows, grad_branch)
    back_query, back_key, back_value, back_out = (
        lax.all_gather(w_query, ("fsdp", "seq"), axis=0, tiled=True),
        lax.all_gather(w_key, ("fsdp", "seq"), axis=0, tiled=True),
        lax.all_gather(w_value, ("fsdp", "seq"), axis=0, tiled=True),
        lax.all_gather(w_out, ("fsdp", "seq"), axis=0, tiled=True),
    )
    grad_mixed = matmul_right_t(grad_branch, back_out).astype(jnp.bfloat16)
    grad_mixed_parts = grad_mixed.reshape(seq_count, part_len, width)
    key_again, value_again = (
        lax.all_gather(key_parts, "seq", axis=1, tiled=True),
        lax.all_gather(value_parts, "seq", axis=1, tiled=True),
    )
    grad_query_parts, grad_key_seq, grad_value_seq = lax.map(
        attend_backward,
        (
            query_parts,
            key_again,
            value_again,
            segment_ids,
            seg_keys,
            keep_keys,
            log_totals,
            grad_mixed_parts,
        ),
    )
    grad_key_own, grad_value_own = (
        lax.psum_scatter(grad_key_seq, "seq", scatter_dimension=1, tiled=True),
        lax.psum_scatter(grad_value_seq, "seq", scatter_dimension=1, tiled=True),
    )
    grad_query_rows = grad_query_parts.reshape(tok_count, width)
    grad_key_rows = grad_key_own.reshape(tok_count, width).astype(jnp.bfloat16)
    grad_value_rows = grad_value_own.reshape(tok_count, width).astype(jnp.bfloat16)
    grad_bias_query = column_sum(grad_query_rows)
    grad_bias_value = column_sum(grad_value_rows)
    grad_wquery = matmul_left_t(tok_rows, grad_query_rows)
    grad_wkey = matmul_left_t(tok_rows, grad_key_rows)
    grad_wvalue = matmul_left_t(tok_rows, grad_value_rows)
    grad_input = (
        grad_sum_one
        + matmul_right_t(grad_query_rows, back_query)
        + matmul_right_t(grad_key_rows, back_key)
        + matmul_right_t(grad_value_rows, back_value)
    )
    input_grad = grad_input.reshape(tokens.shape)
    (
        shard_query,
        shard_key,
        shard_value,
        shard_out,
        shard_bquery,
        shard_bvalue,
        shard_bout,
        shard_gone,
        shard_sone,
        shard_up,
        shard_down,
        shard_bup,
        shard_bdown,
        shard_gtwo,
        shard_stwo,
    ) = (
        lax.psum_scatter(grad_wquery, ("fsdp", "seq"), scatter_dimension=0, tiled=True),
        lax.psum_scatter(grad_wkey, ("fsdp", "seq"), scatter_dimension=0, tiled=True),
        lax.psum_scatter(grad_wvalue, ("fsdp", "seq"), scatter_dimension=0, tiled=True),
        lax.psum_scatter(grad_out_weight, ("fsdp", "seq"), scatter_dimension=0, tiled=True),
        lax.psum_scatter(grad_bias_query, ("fsdp", "seq"), scatter_dimension=0, tiled=True),
        lax.psum_scatter(grad_bias_value, ("fsdp", "seq"), scatter_dimension=0, tiled=True),
        lax.psum_scatter(grad_bias_out, ("fsdp", "seq"), scatter_dimension=0, tiled=True),
        lax.psum_scatter(grad_gain_one, ("fsdp", "seq"), scatter_dimension=0, tiled=True),
        lax.psum_scatter(grad_shift_one, ("fsdp", "seq"), scatter_dimension=0, tiled=True),
        lax.psum_scatter(grad_up, ("fsdp", "seq"), scatter_dimension=0, tiled=True),
        lax.psum_scatter(grad_down, ("fsdp", "seq"), scatter_dimension=0, tiled=True),
        lax.psum_scatter(grad_bias_up, ("fsdp", "seq"), scatter_dimension=0, tiled=True),
        lax.psum_scatter(grad_bias_down, ("fsdp", "seq"), scatter_dimension=0, tiled=True),
        lax.psum_scatter(grad_gain_two, ("fsdp", "seq"), scatter_dimension=0, tiled=True),
        lax.psum_scatter(grad_shift_two, ("fsdp", "seq"), scatter_dimension=0, tiled=True),
    )
    (
        final_query,
        final_key,
        final_value,
        final_out,
        final_bquery,
        final_bvalue,
        final_bout,
        final_gone,
        final_sone,
        final_up,
        final_down,
        final_bup,
        final_bdown,
        final_gtwo,
        final_stwo,
    ) = lax.psum(
        (
            shard_query,
            shard_key,
            shard_value,
            shard_out,
            shard_bquery,
            shard_bvalue,
            shard_bout,
            shard_gone,
            shard_sone,
            shard_up,
            shard_down,
            shard_bup,
            shard_bdown,
            shard_gtwo,
            shard_stwo,
        ),
        "rep",
    )
    return (
        output,
        input_grad,
        final_query,
        final_key,
        final_value,
        final_out,
        final_bquery,
        final_bvalue,
        final_bout,
        final_gone,
        final_sone,
        final_up,
        final_bup,
        final_down,
        final_bdown,
        final_gtwo,
        final_stwo,
    )


def solution(mesh):
    placed = (
        P(("rep", "fsdp"), "seq", None),
        P(("rep", "fsdp"), "seq"),
        P(("rep", "fsdp"), "seq"),
        P(("rep", "fsdp"), "seq", None),
        P(("fsdp", "seq"), None),
        P(("fsdp", "seq"), None),
        P(("fsdp", "seq"), None),
        P(("fsdp", "seq"), None),
        P(("fsdp", "seq")),
        P(("fsdp", "seq")),
        P(("fsdp", "seq")),
        P(("fsdp", "seq")),
        P(("fsdp", "seq")),
        P(("fsdp", "seq"), None),
        P(("fsdp", "seq")),
        P(("fsdp", "seq"), None),
        P(("fsdp", "seq")),
        P(("fsdp", "seq")),
        P(("fsdp", "seq")),
    )
    return jax.shard_map(
        body,
        mesh=mesh,
        in_specs=placed,
        out_specs=(
            P(("rep", "fsdp"), "seq", None),
            P(("rep", "fsdp"), "seq", None),
            P(("fsdp", "seq"), None),
            P(("fsdp", "seq"), None),
            P(("fsdp", "seq"), None),
            P(("fsdp", "seq"), None),
            P(("fsdp", "seq")),
            P(("fsdp", "seq")),
            P(("fsdp", "seq")),
            P(("fsdp", "seq")),
            P(("fsdp", "seq")),
            P(("fsdp", "seq"), None),
            P(("fsdp", "seq")),
            P(("fsdp", "seq"), None),
            P(("fsdp", "seq")),
            P(("fsdp", "seq")),
            P(("fsdp", "seq")),
        ),
        check_vma=False,
    )
```

profile of v0, /device:TPU:0, one launch (start us, length us, event | category | flops | bytes accessed | tf_op | source)
XLA Modules:
  0.0 1375.5 jit_solution(3362333839241295329)
XLA Ops:
  19.8 20.8 %all-gather.18.cloned.1.call-done = bf16[1024,1024]{1,0:T(8,128)(2,1)} async-done(((bf16[128,1024]{1,0:T(8,128)(2,1)}), bf16[1024,1024]{1,0:T(8,128)(2,1)}) %all-gather.18.cloned.1.call-update) | async-done | bytes 2097168 | tf_op jit(solution)/shard_map/all_gather | solution.py:161
  47.7 22.6 %all-gather.24.cloned.1.call-done = bf16[1024,1024]{1,0:T(8,128)(2,1)} async-done(((bf16[128,1024]{1,0:T(8,128)(2,1)}), bf16[1024,1024]{1,0:T(8,128)(2,1)}) %all-gather.24.cloned.1.call-update) | async-done | bytes 2097168 | tf_op jit(solution)/shard_map/all_gather | solution.py:160
  165.4 102.2 %while.26 = (s32[]{:T(128)}, bf16[2,512,1024]{2,1,0:T(8,128)(2,1)}, f32[2,16,512]{2,1,0:T(8,128)}, bf16[2,1024,1024]{1,2,0:T(8,128)(2,1)}, s32[2,512]{1,0:T(2,12...) while((s32[]{:T(128)}, bf16[2,512,1024]{2,1,0:T(8,128)(2,1)}, ...), condition=%wide.region_3.4_spmd, body=%wide.region_0.3_spmd.sunk | while | flops 2249715200 | bytes 124015736 | solution.py:185
  184.0 15.7 %fusion.111 = f32[16,512]{1,0:T(8,128)S(1)} fusion(f32[16,512,1024]{2,1,0:T(8,128)} %get-tuple-element.474, f32[16,512]{1,0:T(8,128)S(1)} %get-tuple-element.475, pred[512,1024]{1,0:T(8,128)(4,1)S(1)} %compare_and_fusion.4), kind=kLoop, calls=%fused_computation.4.clone.1 | loop fusion | flops 33546240 | bytes 34144256 | tf_op jit(solution)/shard_map/while/body/eval_jaxpr/reduce_sum | solution.py:70
  235.8 14.9 %fusion.111 = f32[16,512]{1,0:T(8,128)S(1)} fusion(f32[16,512,1024]{2,1,0:T(8,128)} %get-tuple-element.474, f32[16,512]{1,0:T(8,128)S(1)} %get-tuple-element.475, pred[512,1024]{1,0:T(8,128)(4,1)S(1)} %compare_and_fusion.4), kind=kLoop, calls=%fused_computation.4.clone.1 | loop fusion | flops 33546240 | bytes 34144256 | tf_op jit(solution)/shard_map/while/body/eval_jaxpr/reduce_sum | solution.py:70
  275.6 18.4 %multiply_convert_fusion.2 = (bf16[1024,4096]{1,0:T(8,128)(2,1)}, f32[1024,4096]{1,0:T(8,128)}) fusion(f32[4096]{0:T(1024)S(1)} %bitcast.224, bf16[1024,4096]{1,0:T(8,128)(2,1)} %all-gather.30.cloned.1.call-done, f32[1024,1024]{1,0:T(8,128)} %copy-done.7, f32[1024]{0:T(1024)S(1)} %bitcast.226, f32[1024]{0:T(1024)S(1)} %bitcast.219, ...), kind=kOutput, calls=%fused_computation.50 | convolution fusion | flops 8620343296 | bytes 37781504 | tf_op jit(solution)/shard_map/dot_general | solution.py:16
  316.4 20.2 %convert_reduce_fusion = (f32[4096]{0:T(1024)}, bf16[1024,4096]{1,0:T(8,128)(2,1)}) fusion(f32[1024,4096]{1,0:T(8,128)} %get-tuple-element.340, f32[4096]{0:T(1024)S(1)} %bitcast.225, bf16[4096,1024]{1,0:T(8,128)(2,1)S(1)} %bitcast.242, f32[1024,1024]{1,0:T(8,128)S(1)} %get-tuple-element.323), kind=kOutput, calls=%fused_computation.49 | convolution fusion | flops 8645505024 | bytes 37781504 | tf_op jit(solution)/shard_map/dot_general | solution.py:26
  336.6 16.0 %multiply_reduce_fusion.1 = (f32[1024]{0:T(1024)}, f32[1024]{0:T(1024)S(1)}, f32[1024]{0:T(1024)S(1)}, f32[1024]{0:T(1024)}, f32[1024,1024]{1,0:T(8,128)S(1)}) fusion(f32[1024,1024]{1,0:T(8,128)S(1)} %copy-done.8, f32[1024]{0:T(1024)S(1)} %add_rsqrt_fusion.1, f32[1024]{0:T(1024)S(1)} %broadcast_multiply_fusion.4, f32[1024]{0:T(1024)S(1)} %bitcast.221, ...), kind=kOutput, calls=%fused_computation.64 | convolution fusion | flops 8600416256 | bytes 29388800 | tf_op jit(solution)/shard_map/dot_general | solution.py:26
  358.3 273.2 %while.27 = (s32[]{:T(128)}, bf16[2,512,1024]{1,2,0:T(8,128)(2,1)}, f32[2,1024,1024]{2,1,0:T(8,128)}, f32[2,1024,1024]{2,1,0:T(8,128)}, bf16[2,1024,1024]{1,2,0:...) while((s32[]{:T(128)}, bf16[2,512,1024]{1,2,0:T(8,128)(2,1)}, ...), condition=%wide.region_14.15_spmd, body=%wide.region_12.14_spmd.sunk | while | flops 5497679360 | bytes 341038336 | solution.py:241
  382.0 25.6 %multiply_reduce_fusion.7 = (f32[16,512]{1,0:T(8,128)S(1)}, f32[16,512,1024]{2,1,0:T(8,128)}) fusion(f32[16,512,1024]{2,1,0:T(8,128)} %fusion.123, f32[16,512]{1,0:T(8,128)S(1)} %dynamic-slice_bitcast_fusion.2, pred[512,1024]{1,0:T(8,128)(4,1)S(1)} %copy-done, bf16[512,16,64]{0,2,1:T(8,128)(2,1)S(1)} %bitcast.196, ...), kind=kOutput, calls=%fused_computation.20.clone.1 | convolution fusion | flops 1115676672 | bytes 70844416 | tf_op jit(solution)/shard_map/while/body/eval_jaxpr/qhd,khd->hqk/dot_general | solution.py:85
  407.6 28.0 %multiply_convert_fusion.5 = bf16[16,512,1024]{2,1,0:T(8,128)(2,1)} fusion(f32[16,512,1024]{2,1,0:T(8,128)} %get-tuple-element.488, f32[16,512,1024]{2,1,0:T(8,128)} %fusion.123, f32[16,512]{1,0:T(8,128)S(1)} %get-tuple-element.489, f32[16,512]{1,0:T(8,128)S(1)} %dynamic-slice_bitcast_fusion.2, pred[512,1024]{1,0:T(8,128)(4,1)} %compare_and_fusion.5), kind=kLoop, calls=%fused_computation.19.clone.1 | loop fusion | flops 50331648 | bytes 84475904 | tf_op jit(solution)/shard_map/while/body/eval_jaxpr/convert_element_type | solution.py:92
  451.8 17.1 %fusion.125 = f32[16,64,1024]{2,1,0:T(8,128)} fusion(bf16[512,16,64]{0,2,1:T(8,128)(2,1)} %bitcast.195, f32[16,512,1024]{2,1,0:T(8,128)} %fusion.123, f32[16,512]{1,0:T(8,128)S(1)} %dynamic-slice_bitcast_fusion.2, pred[512,1024]{1,0:T(8,128)(4,1)S(1)} %copy-done.1), kind=kOutput, calls=%fused_computation.23.clone.1 | convolution fusion | flops 1107296256 | bytes 39354368 | tf_op jit(solution)/shard_map/while/body/eval_jaxpr/hqk,qhd->khd/dot_general | solution.py:106
  518.3 25.6 %multiply_reduce_fusion.7 = (f32[16,512]{1,0:T(8,128)S(1)}, f32[16,512,1024]{2,1,0:T(8,128)}) fusion(f32[16,512,1024]{2,1,0:T(8,128)} %fusion.123, f32[16,512]{1,0:T(8,128)S(1)} %dynamic-slice_bitcast_fusion.2, pred[512,1024]{1,0:T(8,128)(4,1)S(1)} %copy-done, bf16[512,16,64]{0,2,1:T(8,128)(2,1)S(1)} %bitcast.196, ...), kind=kOutput, calls=%fused_computation.20.clone.1 | convolution fusion | flops 1115676672 | bytes 70844416 | tf_op jit(solution)/shard_map/while/body/eval_jaxpr/qhd,khd->hqk/dot_general | solution.py:85
  543.9 28.0 %multiply_convert_fusion.5 = bf16[16,512,1024]{2,1,0:T(8,128)(2,1)} fusion(f32[16,512,1024]{2,1,0:T(8,128)} %get-tuple-element.488, f32[16,512,1024]{2,1,0:T(8,128)} %fusion.123, f32[16,512]{1,0:T(8,128)S(1)} %get-tuple-element.489, f32[16,512]{1,0:T(8,128)S(1)} %dynamic-slice_bitcast_fusion.2, pred[512,1024]{1,0:T(8,128)(4,1)} %compare_and_fusion.5), kind=kLoop, calls=%fused_computation.19.clone.1 | loop fusion | flops 50331648 | bytes 84475904 | tf_op jit(solution)/shard_map/while/body/eval_jaxpr/convert_element_type | solution.py:92
  588.1 17.1 %fusion.125 = f32[16,64,1024]{2,1,0:T(8,128)} fusion(bf16[512,16,64]{0,2,1:T(8,128)(2,1)} %bitcast.195, f32[16,512,1024]{2,1,0:T(8,128)} %fusion.123, f32[16,512]{1,0:T(8,128)S(1)} %dynamic-slice_bitcast_fusion.2, pred[512,1024]{1,0:T(8,128)(4,1)S(1)} %copy-done.1), kind=kOutput, calls=%fused_computation.23.clone.1 | convolution fusion | flops 1107296256 | bytes 39354368 | tf_op jit(solution)/shard_map/while/body/eval_jaxpr/hqk,qhd->khd/dot_general | solution.py:106
  678.1 17.7 %fusion.34 = f32[1024,4096]{1,0:T(8,128)} fusion(bf16[1024,4096]{1,0:T(8,128)(2,1)} %get-tuple-element.345, f32[1024,1024]{1,0:T(8,128)} %copy-done.7, f32[1024]{0:T(1024)S(1)} %bitcast.228, f32[1024]{0:T(1024)S(1)} %bitcast.223, f32[1024]{0:T(1024)S(1)} %copy-done.32, f32[1024]{0:T(1024)S(1)} %copy-done.23), kind=kOutput, calls=%fused_computation.103 | convolution fusion | flops 8595177472 | bytes 29376512 | tf_op jit(solution)/shard_map/dot_general | solution.py:20
  695.9 16.6 %fusion.31 = f32[4096,1024]{1,0:T(8,128)} fusion(bf16[1024,4096]{1,0:T(8,128)(2,1)} %get-tuple-element.339, f32[1024,1024]{1,0:T(8,128)} %copy-done.14), kind=kOutput, calls=%fused_computation.100 | convolution fusion | flops 8590983168 | bytes 29360128 | tf_op jit(solution)/shard_map/dot_general | solution.py:20
  725.0 54.9 %reduce-scatter.19.cloned.1.call-done = f32[128,1024]{1,0:T(8,128)} async-done(((f32[1024,1024]{1,0:T(8,128)}), f32[128,1024]{1,0:T(8,128)}) %reduce-scatter.19.cloned.1.call-update) | async-done | bytes 524304 | tf_op jit(solution)/shard_map/reduce_scatter | solution.py:293
  779.9 54.7 %reduce-scatter.17.cloned.1.call-done = f32[128,1024]{0,1:T(8,128)} async-done(((f32[1024,1024]{0,1:T(8,128)}), f32[128,1024]{0,1:T(8,128)}) %reduce-scatter.17.cloned.1.call-update) | async-done | bytes 524304 | tf_op jit(solution)/shard_map/reduce_scatter | solution.py:292
  834.6 54.9 %reduce-scatter.15.cloned.1.call-done = f32[128,1024]{0,1:T(8,128)} async-done(((f32[1024,1024]{0,1:T(8,128)}), f32[128,1024]{0,1:T(8,128)}) %reduce-scatter.15.cloned.1.call-update) | async-done | bytes 524304 | tf_op jit(solution)/shard_map/reduce_scatter | solution.py:291
  889.6 119.4 %reduce-scatter.21.cloned.1.call-done = f32[128,4096]{1,0:T(8,128)} async-done(((f32[1024,4096]{1,0:T(8,128)}), f32[128,4096]{1,0:T(8,128)}) %reduce-scatter.21.cloned.1.call-update) | async-done | bytes 2097168 | tf_op jit(solution)/shard_map/reduce_scatter | solution.py:299
  1009.0 119.4 %reduce-scatter.23.cloned.1.call-done = f32[512,1024]{1,0:T(8,128)} async-done(((f32[4096,1024]{1,0:T(8,128)}), f32[512,1024]{1,0:T(8,128)}) %reduce-scatter.23.cloned.1.call-update) | async-done | bytes 2097168 | tf_op jit(solution)/shard_map/reduce_scatter | solution.py:300
  1139.9 25.6 %all-reduce.9 = (f32[1024]{0:T(1024)S(1)}, f32[1024]{0:T(1024)S(1)}, f32[1024]{0:T(1024)S(1)}, f32[1024]{0:T(1024)S(1)}, f32[1024]{0:T(1024)S(1)}, /*index=5*/f3...) all-reduce(f32[1024]{0:T(1024)S(1)} %convert_reduce_fusion.5, ...), channel_id=8, replica_groups=mesh['rep'=4,'fsdp'=4,'seq'=2] {'fsdp','seq'}, use_global_device_ids=true, to_apply=%region_26.27.clone | all-reduce | flops 12288 | bytes 98304
  1189.4 166.7 %all-reduce.14.cloned.1.call-done = (f32[128,1024]{0,1:T(8,128)}, f32[128,1024]{0,1:T(8,128)}, f32[128,1024]{0,1:T(8,128)}, f32[128,1024]{1,0:T(8,128)}, f32[128,4096]{1,0:T(8,128)}, /*index=5*/f32[512,1024]{1,0:T(8,128)}) async-done(((f32[128,1024]{0,1:T(8,128)}, f32[128,1024]{0,1:T(8,128)}, f32[128,1024]{0,1:T(8,128)}, f32[128,1024]{1,0:T(8,128)}, f32[128,4096]{1,0:T(8,128)}, ...) | async-done | bytes 6291472 | tf_op jit(solution)/shard_map/psum | solution.py:322
  (301 shorter events, 458.7 us)
Async XLA Ops:
  7.2 33.4 %all-gather.18.cloned.1.call-start = ((), (), s32[]{:S(2)}) async-start(), calls=%async_computation.8 | async-start | bytes 2359296 | tf_op jit(solution)/shard_map/all_gather | solution.py:161
  7.9 62.4 %all-gather.24.cloned.1.call-start = ((), (), s32[]{:S(2)}) async-start(), calls=%async_computation.11 | async-start | bytes 2359296 | tf_op jit(solution)/shard_map/all_gather | solution.py:160
  8.7 149.3 %all-gather.22.cloned.1.call-start = ((), (), s32[]{:S(2)}) async-start(), calls=%async_computation.10 | async-start | bytes 2359296 | tf_op jit(solution)/shard_map/all_gather | solution.py:159
  9.4 155.9 %all-gather.20.cloned.1.call-start = ((), (), s32[]{:S(2)}) async-start(), calls=%async_computation.9 | async-start | bytes 6291456 | tf_op jit(solution)/shard_map/all_gather | solution.py:181
  47.7 117.7 %all-gather.26.cloned.1.call-start = ((), (), s32[]{:S(2)}) async-start(), calls=%async_computation.12 | async-start | bytes 6291456 | tf_op jit(solution)/shard_map/all_gather | solution.py:180
  76.3 62.6 %copy-start.49 = (bf16[128]{0:T(256)(128)(2,1)S(1)}, bf16[128]{0:T(256)(128)(2,1)}, u32[]{:S(2)}) copy-start(bf16[128]{0:T(256)(128)(2,1)} %param.40) | copy-start | bytes 772
  76.3 71.3 %copy-start.3 = (bf16[2,512,1024]{2,1,0:T(8,128)(2,1)S(1)}, bf16[2,512,1024]{2,1,0:T(8,128)(2,1)}, u32[]{:S(2)}) copy-start(bf16[2,512,1024]{2,1,0:T(8,128)(2,1)} %param.26) | copy-start | bytes 6291460
  80.4 69.2 %copy-start.50 = (bf16[128]{0:T(256)(128)(2,1)S(1)}, bf16[128]{0:T(256)(128)(2,1)}, u32[]{:S(2)}) copy-start(bf16[128]{0:T(256)(128)(2,1)} %param.41) | copy-start | bytes 772
  80.4 187.1 %all-gather.28.cloned.1.call-start = ((), (), s32[]{:S(2)}) async-start(), calls=%async_computation.13 | async-start | bytes 2359296 | tf_op jit(solution)/shard_map/all_gather | solution.py:162
  81.0 194.6 %all-gather.30.cloned.1.call-start = ((), (), s32[]{:S(2)}) async-start(), calls=%async_computation.14 | async-start | bytes 9437184 | tf_op jit(solution)/shard_map/all_gather | solution.py:193
  81.8 212.3 %all-gather.32.cloned.1.call-start = ((), (), s32[]{:S(2)}) async-start(), calls=%async_computation.15 | async-start | bytes 9437184 | tf_op jit(solution)/shard_map/all_gather | solution.py:194
  82.5 566.1 %reduce-scatter.11.cloned.1.call-start = ((), (), s32[]{:S(2)}) async-start(), calls=%async_computation.17 | async-start | bytes 12582912 | tf_op jit(solution)/shard_map/reduce_scatter | solution.py:256
  165.4 102.2 %copy-start.42 = (f32[8,1,128]{2,1,0:T(1,128)S(1)}, f32[8,1,128]{2,1,0:T(1,128)}, u32[]{:S(2)}) copy-start(f32[8,1,128]{2,1,0:T(1,128)} %convert_element_type.230) | copy-start | bytes 12292
  273.0 79.6 %copy-start.22 = (f32[1024]{0:T(1024)}, f32[1024]{0:T(1024)S(1)}, u32[]{:S(2)}) copy-start(f32[1024]{0:T(1024)S(1)} %broadcast_multiply_fusion.4) | copy-start | bytes 12292
  275.6 77.0 %copy-start.31 = (f32[1024]{0:T(1024)}, f32[1024]{0:T(1024)S(1)}, u32[]{:S(2)}) copy-start(f32[1024]{0:T(1024)S(1)} %add_rsqrt_fusion.1) | copy-start | bytes 12292
  631.5 37.5 %reduce-scatter.9.cloned.1.call-start = ((), (), s32[]{:S(2)}) async-start(), calls=%async_computation.16 | async-start | bytes 12582912 | tf_op jit(solution)/shard_map/reduce_scatter | solution.py:255
  632.1 92.9 %reduce-scatter.13.cloned.1.call-start = ((), (), s32[]{:S(2)}) async-start(), calls=%async_computation.18 | async-start | bytes 4718592 | tf_op jit(solution)/shard_map/reduce_scatter | solution.py:290
  639.1 140.8 %reduce-scatter.19.cloned.1.call-start = ((), (), s32[]{:S(2)}) async-start(), calls=%async_computation.21 | async-start | bytes 4718592 | tf_op jit(solution)/shard_map/reduce_scatter | solution.py:293
  647.8 186.8 %reduce-scatter.17.cloned.1.call-start = ((), (), s32[]{:S(2)}) async-start(), calls=%async_computation.20 | async-start | bytes 4718592 | tf_op jit(solution)/shard_map/reduce_scatter | solution.py:292
  657.2 232.3 %reduce-scatter.15.cloned.1.call-start = ((), (), s32[]{:S(2)}) async-start(), calls=%async_computation.19 | async-start | bytes 4718592 | tf_op jit(solution)/shard_map/reduce_scatter | solution.py:291
  677.4 331.6 %reduce-scatter.21.cloned.1.call-start = ((), (), s32[]{:S(2)}) async-start(), calls=%async_computation.22 | async-start | bytes 18874368 | tf_op jit(solution)/shard_map/reduce_scatter | solution.py:299
  695.8 432.5 %reduce-scatter.23.cloned.1.call-start = ((), (), s32[]{:S(2)}) async-start(), calls=%async_computation.23 | async-start | bytes 18874368 | tf_op jit(solution)/shard_map/reduce_scatter | solution.py:300
  712.6 415.8 %copy-start.54 = (u32[32]{0:T(128)S(1)}, u32[32]{0:T(128)}, u32[]{:S(2)}) copy-start(u32[32]{0:T(128)} %constant.93) | copy-start | bytes 388
  712.6 643.6 %all-reduce.14.cloned.1.call-start = ((), (), s32[]{:S(2)}) async-start(), calls=%async_computation.24 | async-start | bytes 12582912 | tf_op jit(solution)/shard_map/psum | solution.py:322
  (54 other events, 514.7 us)
Sparse Core Ops, SparseCore 0:
  9.9 30.5 all-gather.17
  42.4 27.8 all-gather.23
  72.2 27.8 all-gather.21
  102.2 13.6 all-gather.19
  117.8 14.8 all-gather.25
  134.4 29.0 all-gather.27
  165.4 54.3 all-gather.29
  221.7 54.3 all-gather.31
  631.6 16.9 reduce-scatter.10
  650.9 18.0 reduce-scatter.8
  672.4 52.5 reduce-scatter.12
  728.5 51.3 reduce-scatter.18
  783.3 51.3 reduce-scatter.16
  838.2 51.3 reduce-scatter.14
  893.0 115.9 reduce-scatter.20
  1012.4 115.8 reduce-scatter.22
  1131.0 225.0 all-reduce.13
where the time goes:
time: 1380 us
  waiting for transfers between devices  643 us (47%)
  matrix products  380 us (28%)
  blocking collectives  119 us (9%)
  other arithmetic  111 us (8%)
  local copies, waits for them, and re-layouts  105 us (8%)
  between operations  16.1 us (1%)
    psum x1, waiting for transfers between devices, body(): lax.psum((shard_query, shard_key, shard_value, shard_out, shard_bquery, s...  167 us
    reduce_scatter x1, waiting for transfers between devices, body(): lax.psum_scatter(grad_up, ('fsdp', 'seq'), scatter_dimension=0, tiled=True)  119 us
    reduce_scatter x1, waiting for transfers between devices, body(): lax.psum_scatter(grad_down, ('fsdp', 'seq'), scatter_dimension=0, tiled=T...  119 us
    dot_general x6, matrix products, matmul_left_t(): lax.dot_general(left, right, (((0,), (0,)), ((), ())), preferred_element_...  57.7 us
    convert_element_type x2, other arithmetic, attend_backward(): grad_scores = (attn_probs * (grad_probs - row_dot)).astype(jnp.bfloat16)  55.9 us
    dot_general x6, matrix products, matmul_right_t(): lax.dot_general(left, right, (((1,), (1,)), ((), ())), preferred_element_...  55.3 us
    dot_general x4, matrix products, score_block(): jnp.einsum('qhd,khd->hqk', split_heads(queries), split_heads(keys_seq), p...  55.3 us
    reduce_scatter x1, waiting for transfers between devices, body(): lax.psum_scatter(grad_out_weight, ('fsdp', 'seq'), scatter_dimension=0, t...  54.9 us
  transfers between devices with their start and end apart: 17, of which 11 were waited for; matrix products, arithmetic and copies ran while one was open for 17% of the time, Pallas kernels for 0%

commit v1 on v0

v1 whole, which is shorter than its diff:
```python
import functools
import math
import jax
import jax.numpy as jnp
from jax import lax
from jax.experimental import pallas as pl
from jax.experimental.pallas import tpu as pltpu
from jax.sharding import PartitionSpec as P

F32 = jnp.float32
BF = jnp.bfloat16
HEAD_DIM = 64
LANES = 128
EPSILON = 1e-05
ROOT_HALF = 0.7071067811865476
INV_ROOT_TAU = 0.3989422804014327
NT = (((1,), (1,)), ((), ()))
TN = (((0,), (0,)), ((), ()))
NN = (((1,), (0,)), ((), ()))
VMEM = 58 << 20
ANY = pl.BlockSpec(memory_space=pl.ANY)


def dg(a, b, dims):
    return lax.dot_general(a, b, dims, preferred_element_type=F32)


def params(limit=VMEM):
    return pltpu.CompilerParams(vmem_limit_bytes=limit)


def cost(flops, bytes_accessed, trans=0):
    return pl.CostEstimate(flops=flops, bytes_accessed=bytes_accessed, transcendentals=trans)


def swap(x, axis, size, xor):
    return lax.ppermute(x, axis, [(i, i ^ xor) for i in range(size)])


class Gathered:
    def __init__(self, arrays, entries, half):
        self.arrays, self.entries, self.half = arrays, entries, half

    def copies(self, refs, ids, targets, sems):
        out = []
        for which, index, half, slot in self.entries:
            low = half * self.half
            for first, rows, dest, stride, offset in targets:
                a, b = max(first, low), min(first + rows, low + self.half)
                if a >= b:
                    continue
                src = refs[which].at[(*index, pl.ds(a - low, b - a))]
                start = pl.multiple_of(ids[slot] * stride + (offset + a - first), 16)
                out.append(pltpu.make_async_copy(src, dest.at[pl.ds(start, b - a)], sems.at[len(out)]))
        return out

    def count(self, targets):
        n = 0
        for _, _, half, _ in self.entries:
            low = half * self.half
            n += sum(max(t[0], low) < min(t[0] + t[1], low + self.half) for t in targets)
        return n


def gather_start(halves, nf):
    if nf == 4:
        one, two = halves
        return {
            "xa": swap(one, "fsdp", nf, 1),
            "yb": swap(two, "fsdp", nf, 2),
            "ya": swap(one, "fsdp", nf, 2),
            "xb": swap(two, "fsdp", nf, 1),
        }
    return {"all": [lax.all_gather(h, "fsdp", axis=0) for h in halves]}


def gather_far(first, nf):
    if nf == 4:
        return swap(first["xa"], "fsdp", nf, 2), swap(first["yb"], "fsdp", nf, 1)
    return ()


def gather_end(halves, first, far, nf, ns):
    half = halves[0].shape[0]
    if nf == 4:
        arrays = [halves[0], halves[1], first["xa"], first["xb"], first["ya"], first["yb"], far[0], far[1]]
        entries = [(w, (), w % 2, 2 * (w // 2)) for w in range(8)]
    else:
        arrays = list(first["all"])
        entries = [(h, (f,), h, 2 * nf + 2 * f) for f in range(nf) for h in range(2)]
    n = len(arrays)
    arrays = arrays + [swap(a, "seq", ns, 1) for a in arrays]
    entries = entries + [(w + n, i, h, s + 1) for w, i, h, s in entries]
    return Gathered(arrays, entries, half)


BIAS_ROWS = 32


def split_kernel(moves, nin, nout, *refs):
    ins, outs, sems = refs[:nin], refs[len(refs) - nout - 1 : -1], refs[-1]
    copies = [
        pltpu.make_async_copy(ins[s].at[pl.ds(first, rows)], outs[d].at[pl.ds(to, rows)], sems.at[i])
        for i, (s, first, rows, d, to) in enumerate(moves)
    ]
    for m in copies:
        m.start()
    for m in copies:
        m.wait()


def split_rows(ins, moves, out_shapes, deps, name):
    return pl.pallas_call(
        functools.partial(split_kernel, moves, len(ins), len(out_shapes)),
        in_specs=[ANY] * (len(ins) + len(deps)),
        out_specs=[ANY] * len(out_shapes),
        out_shape=[jax.ShapeDtypeStruct(o, BF) for o in out_shapes],
        scratch_shapes=[pltpu.SemaphoreType.DMA((len(moves),))],
        compiler_params=params(4 << 20),
        name=name,
    )(*ins, *deps)


def bias_kernel(nvec, *refs):
    vecs, out, tile = refs[:nvec], refs[nvec], refs[nvec + 1]
    part = vecs[0].shape[-1]
    tile[...] = jnp.zeros_like(tile)
    for i in range(8):
        tile[0:1, i * part : (i + 1) * part] = vecs[i][...].astype(F32).reshape(1, part)
    tile[1:2, 0 : 4 * part] = vecs[8][...].astype(F32).reshape(1, 4 * part)
    out[...] = tile[...].astype(BF)


def pack_bias(vecs, width):
    return pl.pallas_call(
        functools.partial(bias_kernel, len(vecs)),
        in_specs=[pl.BlockSpec(memory_space=pltpu.VMEM)] * len(vecs),
        out_specs=pl.BlockSpec(memory_space=pltpu.VMEM),
        out_shape=jax.ShapeDtypeStruct((BIAS_ROWS, width), BF),
        scratch_shapes=[pltpu.VMEM((BIAS_ROWS, width), F32)],
        compiler_params=params(4 << 20),
        name="pack_bias",
    )(*vecs)


def qkv_kernel(got, ids, x_ref, *rest):
    n = len(got.arrays)
    pieces, (q_ref, k_ref, v_ref, p_ref, b_ref, wq, wk, wv, wb, sems) = rest[:n], rest[n:]
    width = x_ref.shape[1]
    nb = wb.shape[0] // BIAS_ROWS
    part = width // nb
    targets = qkv_targets(part, wq, wk, wv, wb)

    @pl.when(pl.program_id(0) == 0)
    def _():
        moves = got.copies(pieces, ids, targets, sems)
        for m in moves:
            m.start()
        for m in moves:
            m.wait()
        for b in range(nb):
            rows = wb[b * BIAS_ROWS : b * BIAS_ROWS + 16, :].astype(F32)
            for vec in range(8):
                p_ref[vec : vec + 1, b * part : (b + 1) * part] = rows[0:1, vec * part : (vec + 1) * part]
            b_ref[0:1, b * 4 * part : (b + 1) * 4 * part] = rows[1:2, 0 : 4 * part]

    x = x_ref[...]
    q_ref[...] = (dg(x, wq[...], NN) + p_ref[0:1, :]).astype(BF)
    k_ref[...] = dg(x, wk[...], NN).astype(BF)
    v_ref[...] = (dg(x, wv[...], NN) + p_ref[1:2, :]).astype(BF)


def qkv_targets(part, wq, wk, wv, wb):
    t = [(0, part, wq, part, 0), (part, part, wk, part, 0), (2 * part, part, wv, part, 0)]
    if wb is not None:
        t.append((3 * part, BIAS_ROWS, wb, BIAS_ROWS, 0))
    return t


def project(x, got, ids, nb, block=256):
    n, width = x.shape
    grid = n // block
    rows = pl.BlockSpec((block, width), lambda i, ids: (i, 0))
    whole = lambda shape: pl.BlockSpec(shape, lambda i, ids: (0, 0))
    count = got.count(qkv_targets(width // nb, 0, 0, 0, 0))
    return pl.pallas_call(
        functools.partial(qkv_kernel, got),
        grid_spec=pltpu.PrefetchScalarGridSpec(
            num_scalar_prefetch=1,
            grid=(grid,),
            in_specs=[rows] + [ANY] * len(got.arrays),
            out_specs=[rows, rows, rows, whole((8, width)), whole((1, 4 * width))],
            scratch_shapes=[pltpu.VMEM((width, width), BF)] * 3
            + [pltpu.VMEM((nb * BIAS_ROWS, width), BF), pltpu.SemaphoreType.DMA((count,))],
        ),
        out_shape=[jax.ShapeDtypeStruct((n, width), BF)] * 3
        + [jax.ShapeDtypeStruct((8, width), F32), jax.ShapeDtypeStruct((1, 4 * width), F32)],
        compiler_params=params(),
        cost_estimate=cost(6 * n * width * width, 2 * n * width * 4 + 6 * width * width),
        name="project",
    )(ids, x, *got.arrays)


def split3(v):
    hi=v.astype(BF); r=v-hi.astype(F32); mid=r.astype(BF); lo=(r-mid.astype(F32)).astype(BF)
    return hi,mid,lo
def attn_fwd_kernel(qb, q_ref,k_ref,v_ref,qf_ref,kf_ref,*rest):
    a_ref,lf_ref=rest[-2:]
    n=q_ref.shape[0]
    lane=lax.broadcasted_iota(jnp.int32,(n,LANES),1)
    left=lane<HEAD_DIM
    q=q_ref[...]*jnp.asarray(0.125,BF); k=k_ref[...]; v=v_ref[...]
    qf=qf_ref[...]; kf=kf_ref[...]
    one=jnp.ones_like(v)
    sides=[]
    for h in range(2):
        own=left if h==0 else ~left
        sides.append((jnp.where(own,q,qf),jnp.where(own,k,kf),jnp.where(own,v,one)))
    lq=lax.broadcasted_iota(jnp.int32,(qb,LANES),1)
    leftq=lq<HEAD_DIM
    for c in range(n//qb):
        rows=slice(c*qb,(c+1)*qb)
        res=[]; lse=[]
        for h in range(2):
            qa,ka,va=sides[h]
            s=dg(qa[rows],ka,NT)
            m=jnp.max(s,-1,keepdims=True)
            p=jnp.exp(s-m).astype(BF)
            o=dg(p,va,NN)
            tot=o[:,64:65] if h==0 else o[:,0:1]
            res.append(o/tot)
            lse.append(m+jnp.log(tot))
        a_ref[rows,:]=jnp.where(leftq,res[0],res[1]).astype(BF)
        lm=jnp.where(leftq,lse[1],lse[0])
        hi,mid,lo=split3(lm)
        j=lq%HEAD_DIM
        base=qf[rows]
        lf_ref[rows,:]=jnp.where(j==4,hi,jnp.where(j==5,mid,jnp.where(j==6,lo,base)))
def attn_fwd(q,k,v,qf,kf,first,npair,deps=(),qb=512):
    n=q.shape[0]
    blk=pl.BlockSpec((n,LANES),lambda i:(0,i+first))
    whole=pl.BlockSpec((n,LANES),lambda i:(0,0))
    out=pl.BlockSpec((n,LANES),lambda i:(0,i))
    return pl.pallas_call(functools.partial(attn_fwd_kernel,qb),grid=(npair,),
        in_specs=[blk,blk,blk,whole,whole]+[ANY]*len(deps),out_specs=[out,out],
        out_shape=[jax.ShapeDtypeStruct((n,npair*LANES),BF)]*2,
        compiler_params=pltpu.CompilerParams(vmem_limit_bytes=50<<20),
        cost_estimate=pl.CostEstimate(flops=npair*2*2*2*n*n*256,bytes_accessed=npair*n*LANES*2*5,transcendentals=npair*2*n*n),
        name="attend_forward")(q,k,v,qf,kf,*deps)
def attn_bwd_kernel(qb,q_ref,k_ref,v_ref,da_ref,a_ref,lf_ref,kf_ref,*rest):
    d_ref,dka,dva=rest[-3:]
    n=q_ref.shape[0]
    lane=lax.broadcasted_iota(jnp.int32,(n,LANES),1)
    left=lane<HEAD_DIM
    q=q_ref[...]*jnp.asarray(0.125,BF); k=k_ref[...]; v=v_ref[...]; da=da_ref[...]
    lf=lf_ref[...]; kf=kf_ref[...]
    prod=da.astype(F32)*a_ref[...].astype(F32)
    j=lane%HEAD_DIM
    zero=jnp.zeros_like(q)
    minus=jnp.where((j>=4)&(j<7),jnp.asarray(-1,BF),jnp.asarray(0,BF))
    sides=[]
    for h in range(2):
        own=left if h==0 else ~left
        d=jnp.sum(jnp.where(own,prod,0.0),-1,keepdims=True)
        hi,mid,lo=split3(d)
        df=jnp.where(j==4,hi,jnp.where(j==5,mid,jnp.where(j==6,lo,zero)))
        sides.append((jnp.where(own,q,lf),jnp.where(own,k,kf),jnp.where(own,v,minus),jnp.where(own,da,df),
                      jnp.where(own,q,zero),jnp.where(own,da,zero)))
    kt=k.T
    for c in range(n//qb):
        rows=slice(c*qb,(c+1)*qb)
        dqs=[]; dk=None; dv=None
        for h in range(2):
            qa,ka,va,daa,qz,daz=sides[h]
            s=dg(ka,qa[rows],NT)
            p=jnp.exp(s)
            dp=dg(va,daa[rows],NT)
            ds=(p*dp).astype(BF)
            pb=p.astype(BF)
            x=dg(pb,daz[rows],NN); dv=x if dv is None else dv+x
            y=dg(ds,qz[rows],NN); dk=y if dk is None else dk+y
            dqs.append(dg(kt[h*64:(h+1)*64],ds,NN))
        d_ref[0,rows,:]=(jnp.concatenate(dqs,0).T*0.125).astype(BF)
        if c==0: dka[...]=dk; dva[...]=dv
        else: dka[...]+=dk; dva[...]+=dv
    d_ref[1]=dka[...].astype(BF)
    d_ref[2]=dva[...].astype(BF)
def attn_bwd(q,k,v,da,a,lf,kf,first,npair,deps=(),qb=256):
    n=q.shape[0]
    blk=pl.BlockSpec((n,LANES),lambda i:(0,i+first))
    whole=pl.BlockSpec((n,LANES),lambda i:(0,0))
    own=pl.BlockSpec((n,LANES),lambda i:(0,i))
    out=pl.BlockSpec((3,n,LANES),lambda i:(0,0,i))
    return pl.pallas_call(functools.partial(attn_bwd_kernel,qb),grid=(npair,),
        in_specs=[blk]*5+[own,whole]+[ANY]*len(deps),out_specs=out,
        out_shape=jax.ShapeDtypeStruct((3,n,npair*LANES),BF),
        scratch_shapes=[pltpu.VMEM((n,LANES),F32)]*2,
        compiler_params=pltpu.CompilerParams(vmem_limit_bytes=50<<20),
        cost_estimate=pl.CostEstimate(flops=npair*2*5*2*n*n*256,bytes_accessed=npair*n*LANES*2*9,transcendentals=npair*2*n*n),
        name="attend_backward")(q,k,v,da,a,lf,kf,*deps)
def seg_features(seg,pad):
    n=seg.shape[0]
    j=lax.broadcasted_iota(jnp.int32,(n,LANES),1)%HEAD_DIM
    same=(seg[:,None]==j)
    qf=jnp.where((j<4)&same,1.0,0.0).astype(BF)
    kf=jnp.where(j<4,jnp.where(same&(pad[:,None]>0),0.0,-1e30),jnp.where(j<7,-1.0,0.0)).astype(BF)
    return qf,kf


def up_kernel(got, part, ids, x_ref, p_ref, bup_ref, *rest):
    n = len(got.arrays)
    *a_refs, wo = rest[: len(rest) - n - 9]
    pieces = rest[len(rest) - n - 9 : len(rest) - 9]
    a_all, y_ref, yb_ref, n_ref, s_ref, g_ref, gp_ref, wu, sems = rest[-9:]
    width = x_ref.shape[1]
    targets = [(0, part, wu, part, 0)]

    @pl.when(pl.program_id(0) == 0)
    def _():
        for m in got.copies(pieces, ids, targets, sems):
            m.start()

    a = jnp.concatenate([r[...] for r in a_refs], 1)
    a_all[...] = a
    r = x_ref[...].astype(F32) + dg(a, wo[...], NN) + p_ref[2:3, :]
    c = r - jnp.mean(r, -1, keepdims=True)
    s = lax.rsqrt(jnp.mean(c * c, -1, keepdims=True) + EPSILON)
    normed = c * s
    y = normed * p_ref[3:4, :] + p_ref[4:5, :]
    y_ref[...] = y
    n_ref[...] = normed.astype(BF)
    s_ref[...] = s
    yb = y.astype(BF)
    yb_ref[...] = yb

    @pl.when(pl.program_id(0) == 0)
    def _():
        for m in got.copies(pieces, ids, targets, sems):
            m.wait()

    step = 512
    for k in range(0, 4 * width, step):
        h = dg(yb, wu[:, k : k + step], NN) + bup_ref[:, k : k + step]
        phi = 0.5 + 0.5 * lax.erf(h * ROOT_HALF)
        g_ref[:, k : k + step] = (h * phi).astype(BF)
        gp_ref[:, k : k + step] = (phi + h * (jnp.exp(-0.5 * h * h) * INV_ROOT_TAU)).astype(BF)


def up_part(x, vecs, bup, a_parts, w_out, got, ids, nb, block=256):
    n, width = x.shape
    part = width // nb
    rows = lambda w: pl.BlockSpec((block, w), lambda i, ids: (i, 0))
    whole = lambda shape: pl.BlockSpec(shape, lambda i, ids: (0, 0))
    count = got.count([(0, part, 0, 0, 0)])
    sds = jax.ShapeDtypeStruct
    return pl.pallas_call(
        functools.partial(up_kernel, got, part),
        grid_spec=pltpu.PrefetchScalarGridSpec(
            num_scalar_prefetch=1,
            grid=(n // block,),
            in_specs=[rows(width), whole((8, width)), whole((1, 4 * width))]
            + [rows(a.shape[1]) for a in a_parts]
            + [whole((width, width))]
            + [ANY] * len(got.arrays),
            out_specs=[rows(width), rows(width), rows(width), rows(width), rows(1), rows(4 * width), rows(4 * width)],
            scratch_shapes=[pltpu.VMEM((width, 4 * width), BF), pltpu.SemaphoreType.DMA((count,))],
        ),
        out_shape=[
            sds((n, width), BF),
            sds((n, width), F32),
            sds((n, width), BF),
            sds((n, width), BF),
            sds((n, 1), F32),
            sds((n, 4 * width), BF),
            sds((n, 4 * width), BF),
        ],
        compiler_params=params(),
        cost_estimate=cost(10 * n * width * width, 28 * n * width + 10 * width * width, 8 * n * width),
        name="out_norm_up",
    )(ids, x, vecs, bup, *a_parts, w_out, *got.arrays)


def down_kernel(g_ref, y_ref, c_ref, p_ref, wd, o_ref, df_ref, dr_ref, sum_ref):
    @pl.when(pl.program_id(0) == 0)
    def _():
        sum_ref[...] = jnp.zeros_like(sum_ref)

    r = y_ref[...] + dg(g_ref[...], wd[...], NN) + p_ref[5:6, :]
    c = r - jnp.mean(r, -1, keepdims=True)
    s = lax.rsqrt(jnp.mean(c * c, -1, keepdims=True) + EPSILON)
    normed = c * s
    gain = p_ref[6:7, :]
    o_ref[...] = (normed * gain + p_ref[7:8, :]).astype(BF)
    ct = c_ref[...].astype(F32)
    e = ct * gain
    dr = s * (e - jnp.mean(e, -1, keepdims=True) - normed * jnp.mean(e * normed, -1, keepdims=True))
    dr_ref[...] = dr
    df = dr.astype(BF)
    df_ref[...] = df
    sum_ref[0:1, :] += jnp.sum(ct * normed, 0, keepdims=True)
    sum_ref[1:2, :] += jnp.sum(ct, 0, keepdims=True)
    sum_ref[2:3, :] += jnp.sum(df.astype(F32), 0, keepdims=True)


def down_part(g, y, ct, vecs, w_down, block=256):
    n, width = y.shape
    rows = lambda w: pl.BlockSpec((block, w), lambda i: (i, 0))
    whole = lambda shape: pl.BlockSpec(shape, lambda i: (0, 0))
    sds = jax.ShapeDtypeStruct
    return pl.pallas_call(
        down_kernel,
        grid=(n // block,),
        in_specs=[rows(4 * width), rows(width), rows(width), whole((8, width)), whole((4 * width, width))],
        out_specs=[rows(width), rows(width), rows(width), whole((8, width))],
        out_shape=[sds((n, width), BF), sds((n, width), BF), sds((n, width), F32), sds((8, width), F32)],
        compiler_params=params(),
        cost_estimate=cost(8 * n * width * width, 22 * n * width + 8 * width * width),
        name="down_norm",
    )(g, y, ct, vecs, w_down)


def hidden_kernel(df_ref, gp_ref, wd, dh_ref, bup_ref):
    @pl.when(pl.program_id(0) == 0)
    def _():
        bup_ref[...] = jnp.zeros_like(bup_ref)

    df = df_ref[...]
    step = 512
    for k in range(0, dh_ref.shape[1], step):
        dh = (dg(df, wd[k : k + step, :], NT) * gp_ref[:, k : k + step].astype(F32)).astype(BF)
        dh_ref[:, k : k + step] = dh
        bup_ref[:, k : k + step] += jnp.sum(dh.astype(F32), 0, keepdims=True)


def hidden_part(df, gp, w_down, block=256):
    n, width = df.shape
    rows = lambda w: pl.BlockSpec((block, w), lambda i: (i, 0))
    whole = lambda shape: pl.BlockSpec(shape, lambda i: (0, 0))
    return pl.pallas_call(
        hidden_kernel,
        grid=(n // block,),
        in_specs=[rows(width), rows(4 * width), whole((4 * width, width))],
        out_specs=[rows(4 * width), whole((1, 4 * width))],
        out_shape=[jax.ShapeDtypeStruct((n, 4 * width), BF), jax.ShapeDtypeStruct((1, 4 * width), F32)],
        compiler_params=params(),
        cost_estimate=cost(8 * n * width * width, 18 * n * width + 8 * width * width),
        name="hidden_gradient",
    )(df, gp, w_down)


def back_kernel(up, part, ids, dh_ref, dr_ref, n_ref, s_ref, p_ref, wo, *rest):
    nu = len(up.arrays)
    pu = rest[:nu]
    dr1_ref, do_ref, da_ref, sum_ref, wu, su = rest[-6:]
    tu = [(0, part, wu, part, 0)]

    @pl.when(pl.program_id(0) == 0)
    def _():
        moves = up.copies(pu, ids, tu, su)
        for m in moves:
            m.start()
        sum_ref[...] = jnp.zeros_like(sum_ref)
        for m in moves:
            m.wait()

    dy = dr_ref[...] + dg(dh_ref[...], wu[...], NT)
    normed = n_ref[...].astype(F32)
    e = dy * p_ref[3:4, :]
    dr = s_ref[...] * (e - jnp.mean(e, -1, keepdims=True) - normed * jnp.mean(e * normed, -1, keepdims=True))
    dr1_ref[...] = dr
    do = dr.astype(BF)
    do_ref[...] = do
    da_ref[...] = dg(do, wo[...], NT).astype(BF)
    sum_ref[0:1, :] += jnp.sum(dy * normed, 0, keepdims=True)
    sum_ref[1:2, :] += jnp.sum(dy, 0, keepdims=True)
    sum_ref[2:3, :] += jnp.sum(do.astype(F32), 0, keepdims=True)


def back_part(dh, dr, normed, inverse, vecs, w_out, up, ids, nb, deps=(), block=256):
    n, width = dr.shape
    part = width // nb
    rows = lambda w: pl.BlockSpec((block, w), lambda i, ids: (i, 0))
    whole = lambda shape: pl.BlockSpec(shape, lambda i, ids: (0, 0))
    sds = jax.ShapeDtypeStruct
    return pl.pallas_call(
        functools.partial(back_kernel, up, part),
        grid_spec=pltpu.PrefetchScalarGridSpec(
            num_scalar_prefetch=1,
            grid=(n // block,),
            in_specs=[rows(4 * width), rows(width), rows(width), rows(1), whole((8, width)), whole((width, width))]
            + [ANY] * (len(up.arrays) + len(deps)),
            out_specs=[rows(width), rows(width), rows(width), whole((8, width))],
            scratch_shapes=[pltpu.VMEM((width, 4 * width), BF), pltpu.SemaphoreType.DMA((up.count([(0, part, 0, 0, 0)]),))],
        ),
        out_shape=[sds((n, width), F32), sds((n, width), BF), sds((n, width), BF), sds((8, width), F32)],
        compiler_params=params(),
        cost_estimate=cost(10 * n * width * width, 22 * n * width + 10 * width * width),
        name="norm_backward",
    )(ids, dh, dr, normed, inverse, vecs, w_out, *up.arrays, *deps)


def grad_rows_kernel(jb, lo, ls, ro, rs, *rest):
    rest[-1][0] = (dg(lo[...], ro[...], TN) + dg(ls[...], rs[...], TN)).astype(BF)


def grad_down(g_own, g_sib, df_own, df_sib, jb, nf, deps=()):
    n, hidden = g_own.shape
    width = df_own.shape[1]
    part = hidden // (2 * nf)
    left = pl.BlockSpec((n, part), lambda j, jb: (0, jb[j]))
    right = pl.BlockSpec((n, width), lambda j, jb: (0, 0))
    return pl.pallas_call(
        grad_rows_kernel,
        grid_spec=pltpu.PrefetchScalarGridSpec(
            num_scalar_prefetch=1,
            grid=(nf,),
            in_specs=[left, left, right, right] + [ANY] * len(deps),
            out_specs=pl.BlockSpec((1, part, width), lambda j, jb: (j, 0, 0)),
        ),
        out_shape=jax.ShapeDtypeStruct((nf, part, width), BF),
        compiler_params=params(),
        cost_estimate=cost(2 * n * hidden * width, 2 * n * hidden + 4 * n * width + hidden * width),
        name="grad_down",
    )(jb, g_own, g_sib, df_own, df_sib, *deps)


def grad_cols_kernel(nl, nr, nf, want_sum, *refs):
    los, lss = refs[1 : 1 + nl], refs[1 + nl : 1 + 2 * nl]
    ros, rss = refs[1 + 2 * nl : 1 + 2 * nl + nr], refs[1 + 2 * nl + nr : 1 + 2 * nl + 2 * nr]
    outs = refs[-3:-1] if want_sum else refs[-2:-1]
    lt = refs[-1]
    n, wide = los[0].shape
    part = nl * wide // nf

    @pl.when(pl.program_id(0) == 0)
    def _():
        for j in range(nl):
            lt[j * wide : (j + 1) * wide, 0:n] = los[j][...].T
            lt[j * wide : (j + 1) * wide, n : 2 * n] = lss[j][...].T

    left = lt[...]
    at = 0
    for k in range(nr):
        planes = ros[k].shape[0]
        for m in range(planes):
            both = jnp.concatenate([ros[k][m], rss[k][m]], 0)
            cols = both.shape[1]
            got = dg(left, both, NN).astype(BF)
            for j in range(nf):
                outs[0][j, :, at : at + cols] = got[j * part : (j + 1) * part]
            if want_sum:
                outs[1][:, at : at + cols] = jnp.broadcast_to(jnp.sum(both.astype(F32), 0, keepdims=True), (8, cols))
            at += cols


def grad_cols(l_own, l_sib, r_own, r_sib, jb, nf, block, name, want_sum=False, deps=(), into=None, at=0, total=None):
    n, width = l_own.shape
    part = width // (2 * nf)
    nr = len(r_own)
    steps = r_own[0].shape[2] // block
    planes = sum(r.shape[0] for r in r_own)
    here = planes * block
    assert steps == 1 or (nr == 1 and planes == 1)
    if part % LANES == 0:
        nl = nf
        lefts = [pl.BlockSpec((n, part), lambda i, jb, j=j: (0, jb[j])) for j in range(nf)]
    else:
        nl = 1
        pick = lambda z: z.reshape(n, 2 * nf, part)[:, jb].reshape(n, nf * part)
        l_own, l_sib = pick(l_own), pick(l_sib)
        lefts = [pl.BlockSpec((n, nf * part), lambda i, jb: (0, 0))]
    rights = [pl.BlockSpec((r.shape[0], n, block), lambda i, jb: (0, 0, i)) for r in r_own]
    shift = at // here
    out_specs = [pl.BlockSpec((nf, part, here), lambda i, jb: (0, 0, i + shift))]
    total = total or here * steps
    out_shape = [jax.ShapeDtypeStruct((nf, part, total), BF)]
    if want_sum:
        out_specs.append(pl.BlockSpec((8, here), lambda i, jb: (0, 0)))
        out_shape.append(jax.ShapeDtypeStruct((8, here), F32))
    alias = {}
    if into is not None:
        alias = {1 + 2 * nl + 2 * nr: 0}
        deps = (into,) + tuple(deps)
    return pl.pallas_call(
        functools.partial(grad_cols_kernel, nl, nr, nf, want_sum),
        grid_spec=pltpu.PrefetchScalarGridSpec(
            num_scalar_prefetch=1,
            grid=(steps,),
            in_specs=lefts * 2 + rights * 2 + [ANY] * len(deps),
            out_specs=out_specs,
            scratch_shapes=[pltpu.VMEM((nf * part, 2 * n), BF)],
        ),
        out_shape=out_shape,
        input_output_aliases=alias,
        compiler_params=params(),
        cost_estimate=cost(2 * n * width * here * steps, 4 * n * (here * steps + width // 2)),
        name=name,
    )(jb, *([l_own] * nl), *([l_sib] * nl), *r_own, *r_sib, *deps)


def input_kernel(got, part, groups, ids, dr_ref, *rest):
    n = len(got.arrays)
    d_refs, pieces = rest[:groups], rest[groups : groups + n]
    out_ref, wq, wk, wv, sems = rest[-5:]
    targets = qkv_targets(part, wq, wk, wv, None)

    @pl.when(pl.program_id(0) == 0)
    def _():
        moves = got.copies(pieces, ids, targets, sems)
        for c in moves:
            c.start()
        for c in moves:
            c.wait()

    total = dr_ref[...]
    for k, w in enumerate((wq, wk, wv)):
        d = jnp.concatenate([r[k] for r in d_refs], 1)
        total += dg(d, w[...], NT)
    out_ref[...] = total


def input_part(dr, grads, got, ids, nb, deps=(), block=256):
    n, width = dr.shape
    rows = pl.BlockSpec((block, width), lambda i, ids: (i, 0))
    three = lambda w: pl.BlockSpec((3, block, w), lambda i, ids: (0, i, 0))
    count = got.count(qkv_targets(width // nb, 0, 0, 0, None))
    return pl.pallas_call(
        functools.partial(input_kernel, got, width // nb, len(grads)),
        grid_spec=pltpu.PrefetchScalarGridSpec(
            num_scalar_prefetch=1,
            grid=(n // block,),
            in_specs=[rows] + [three(a.shape[2]) for a in grads] + [ANY] * (len(got.arrays) + len(deps)),
            out_specs=rows,
            scratch_shapes=[pltpu.VMEM((width, width), BF)] * 3 + [pltpu.SemaphoreType.DMA((count,))],
        ),
        out_shape=jax.ShapeDtypeStruct((n, width), F32),
        compiler_params=params(),
        cost_estimate=cost(6 * n * width * width, 14 * n * width + 6 * width * width),
        name="input_gradient",
    )(ids, dr, *grads, *got.arrays, *deps)


def add_low(a, b):
    return lax.optimization_barrier((a.astype(F32) + b.astype(F32)).astype(BF))


class Chain:
    def __init__(self, parts, nf, nr, extra=None):
        self.nf, self.nr, self.rows = nf, nr, parts.shape[1]
        self.extra = 0 if extra is None else extra.shape[1]
        self.bits = nf.bit_length() - 1
        a, b = parts[:, : self.rows // 2], parts[:, self.rows // 2 :]
        if extra is not None:
            a = jnp.concatenate([a, extra], 1)
        box = lambda z: z.reshape((2,) * self.bits + z.shape[1:])
        self.cur = [box(a), box(b)]
        self.axes = [list(range(self.bits - 1, -1, -1)) for _ in range(2)]
        self.level = 0

    def plane(self):
        for i in range(2):
            level = self.level if i == 0 else self.bits - 1 - self.level
            axes = self.axes[i]
            ax = axes[level]
            keep = lax.index_in_dim(self.cur[i], 0, ax, keepdims=False)
            send = lax.index_in_dim(self.cur[i], 1, ax, keepdims=False)
            self.cur[i] = add_low(keep, swap(send, "fsdp", self.nf, 1 << level))
            self.axes[i] = [z - (z > ax) for z in axes]
        self.level += 1
        return tuple(self.cur)

    def rest(self):
        while self.level < self.bits:
            self.plane()
        return self

    def cur_deps(self):
        return tuple(self.cur)

    def rep_first(self):
        v = jnp.concatenate([self.cur[1], self.cur[0]], 0)
        self.odd = (lax.axis_index("rep") & 1) == 1
        n = v.shape[0] // 2
        low, high = v[:n], v[n:]
        self.kept = add_low(jnp.where(self.odd, high, low), swap(jnp.where(self.odd, low, high), "rep", self.nr, 1))
        return (self.kept,)

    def rep_middle(self):
        xor = 2
        while xor < self.nr:
            self.kept = add_low(self.kept, swap(self.kept, "rep", self.nr, xor))
            xor *= 2
        return (self.kept,)

    def rep_last(self):
        self.other = swap(self.kept, "rep", self.nr, 1)
        return (self.other,)

    def result(self):
        v = jnp.concatenate([jnp.where(self.odd, self.other, self.kept), jnp.where(self.odd, self.kept, self.other)], 0)
        rows, cut = self.rows, self.rows - self.rows // 2
        main = jnp.concatenate([v[cut : cut + rows // 2], v[:cut]], 0).astype(F32)
        return main, v[rows:].astype(F32)


def body(tokens, segment_ids, padding, cotangent, w_query, w_key, w_value, w_out, b_query, b_value, b_out,
         gain_one, shift_one, w_up, b_up, w_down, b_down, gain_two, shift_two, *, nr, nf, ns):
    _, part_len, width = tokens.shape
    f, c = lax.axis_index("fsdp"), lax.axis_index("seq")
    rel = [((f ^ j) * 2 + (c ^ p)) for j in range(nf) for p in range(2)]
    absolute = [(j * 2 + (c ^ p)) for j in range(nf) for p in range(2)]
    ids = jnp.stack(rel + absolute).astype(jnp.int32)
    jb = jnp.stack(rel[::2]).astype(jnp.int32)
    jb_abs = jnp.stack(absolute[::2]).astype(jnp.int32)
    first_core = c == 0

    def both(x):
        y = swap(x, "seq", ns, 1)
        own = jnp.where(first_core, jnp.concatenate([x[0], y[0]]), jnp.concatenate([y[1], x[1]]))
        sib = jnp.where(first_core, jnp.concatenate([x[1], y[1]]), jnp.concatenate([y[0], x[0]]))
        return own, sib

    def unpair(z):
        low, high = z[:part_len], z[part_len:]
        mine, theirs = jnp.where(first_core, low, high), jnp.where(first_core, high, low)
        got = swap(theirs, "seq", ns, 1)
        return jnp.stack([jnp.where(first_core, mine, got), jnp.where(first_core, got, mine)])

    sib_of = lambda z: swap(z, "seq", ns, 1)

    nb = 2 * nf
    part = width // nb
    bias = pack_bias([b_query, b_value, b_out, gain_one, shift_one, b_down, gain_two, shift_two, b_up], width)
    total = 3 * part + BIAS_ROWS
    half = total // 2
    moves = []
    at = 0
    for src, rows in enumerate((part, part, part, BIAS_ROWS)):
        for side in range(2):
            lo, hi = max(at, side * half), min(at + rows, (side + 1) * half)
            if lo < hi:
                moves.append((src, lo - at, hi - lo, side, lo - side * half))
        at += rows
    qkv_halves = split_rows([w_query, w_key, w_value, bias], moves, [(half, width)] * 2, (), "pack_projections")
    first = gather_start(qkv_halves, nf)
    x, x_sib = both(tokens)
    marks, _ = both(jnp.stack([segment_ids, padding], -1))
    qf, kf = seg_features(marks[:, 0], marks[:, 1])
    far = gather_far(first, nf)
    got_qkv = gather_end(qkv_halves, first, far, nf, ns)
    gate = far if far else tuple(first["all"])
    h = part // 2
    up_halves = split_rows(
        [w_up, w_out, w_down],
        [(0, 0, h, 0, 0), (0, h, h, 1, 0), (1, 0, part, 2, 0), (2, 0, 4 * part, 3, 0)],
        [(h, 4 * width), (h, 4 * width), (part, width), (4 * part, width)],
        gate,
        "split_up",
    )
    first_up = gather_start(up_halves[:2], nf)
    full_out = lax.all_gather(up_halves[2], ("fsdp", "seq"), axis=0, tiled=True)
    full_down = lax.all_gather(up_halves[3], ("fsdp", "seq"), axis=0, tiled=True)
    q, k, v, vecs, bup = project(x, got_qkv, ids, nb)
    pairs = width // LANES
    groups = 4
    each = pairs // groups
    fwd = [attn_fwd(q, k, v, qf, kf, 0, each)]
    arrived = tuple(first_up.values()) if nf == 4 else tuple(first_up["all"])
    far_up = gather_far(first_up, nf)
    fwd.append(attn_fwd(q, k, v, qf, kf, each, each, (fwd[0][0],) + arrived))
    got_up = gather_end(up_halves[:2], first_up, far_up, nf, ns)
    fwd.append(attn_fwd(q, k, v, qf, kf, 2 * each, each, (fwd[1][0],)))
    fwd.append(attn_fwd(q, k, v, qf, kf, 3 * each, each, (fwd[2][0],) + tuple(far_up)))
    ct, _ = both(cotangent)
    a_all, y, yb, normed, inverse, g, gp = up_part(x, vecs, bup, [r[0] for r in fwd], full_out, got_up, ids, nb)
    a_sib, yb_sib, g_sib = sib_of(a_all), sib_of(yb), sib_of(g)
    out, df, dr, sums_two = down_part(g, y, ct, vecs, full_down)
    output = unpair(out)
    df_sib = sib_of(df)
    dh, sum_up = hidden_part(df, gp, full_down)
    dh_sib = sib_of(dh)
    g_down = grad_down(g, g_sib, df, df_sib, jb_abs, nf, (dh,))
    down_sum = lax.psum_scatter(g_down.reshape(nf * 4 * part, width), "fsdp", scatter_dimension=0, tiled=True)
    final_down = lax.psum(down_sum, "rep").astype(F32)
    dr1, do, da, sums_one = back_part(dh, dr, normed, inverse, vecs, full_out, got_up, ids, nb, (g_down,))
    do_sib = sib_of(do)
    (g_up,) = grad_cols(yb, yb_sib, [dh[None]], [dh_sib[None]], jb, nf, 512, "grad_up", deps=(da,), total=5 * width)
    (g_up,) = grad_cols(a_all, a_sib, [do[None]], [do_sib[None]], jb, nf, 512, "grad_out", into=g_up, at=4 * width, total=5 * width)
    chain_up = Chain(g_up, nf, nr)

    def back(i, deps):
        return attn_bwd(q, k, v, da, a_all, fwd[i][1], kf, i * each, each, deps)

    grads = [back(0, (g_up,))]
    sibs = [sib_of(grads[0])]
    grads.append(back(1, (grads[0],)))
    sibs.append(sib_of(grads[1]))
    grads.append(back(2, (grads[1],) + chain_up.plane()))
    sibs.append(sib_of(grads[2]))
    g_one, sum_one = grad_cols(x, x_sib, grads[:2], sibs[:2], jb, nf, each * LANES, "grad_qkv", True, (grads[2],) + chain_up.rest().cur_deps())
    chain_one = Chain(g_one, nf, nr)
    grads.append(back(3, (g_one,) + chain_up.rep_first()))
    sibs.append(sib_of(grads[3]))
    vec_sums = jnp.concatenate([sums_one[2:3], sums_one[0:2], sums_two[2:3], sums_two[0:2], sum_up.reshape(4, width)], 0)
    vec_sums = vec_sums + sib_of(vec_sums)
    deps = chain_one.plane() + chain_up.rep_middle()
    g_two, sum_two = grad_cols(x, x_sib, grads[2:], sibs[2:], jb, nf, each * LANES, "grad_qkv", True, (grads[3],) + deps)

    sums = jnp.concatenate([sum_one[0].reshape(2, 3, -1), sum_two[0].reshape(2, 3, -1)], 0)
    bq, bv = sums[:, 0].reshape(-1), sums[:, 2].reshape(-1)
    eight = jnp.concatenate([bq[None], bv[None], vec_sums[:6]], 0)
    by_block = jnp.concatenate(
        [eight.reshape(8, nb, part).transpose(1, 0, 2).reshape(nb, 8 * part), vec_sums[6:].reshape(nb, 4 * part)], 1
    )
    cols = g_two.shape[2]
    lines16 = -(-12 * part // (cols * 16)) * 16
    mine = jnp.pad(by_block[jb], ((0, 0), (0, lines16 * cols - 12 * part))).reshape(nf, lines16, cols).astype(BF)
    chain_two = Chain(g_two, nf, nr, mine)
    input_grad = unpair(input_part(dr1, grads, got_qkv, ids, nb, (g_two,)))
    chain_up.rep_last()
    chain_one.rest().rep_first()
    chain_one.rep_middle()
    chain_one.rep_last()
    chain_two.rest().rep_first()
    chain_two.rep_middle()
    chain_two.rep_last()
    both_up, _ = chain_up.result()
    final_up, final_out = both_up[:, : 4 * width], both_up[:, 4 * width :]
    one, _ = chain_one.result()
    two, small = chain_two.result()
    wide = each * LANES
    pieces = [z[:, (3 * i + m) * wide : (3 * i + m + 1) * wide] for m in range(3) for z in (one, two) for i in range(2)]
    final_q, final_k, final_v = (jnp.concatenate(pieces[4 * m : 4 * m + 4], 1) for m in range(3))
    small = small.reshape(-1)
    v8 = [small[i * part : (i + 1) * part] for i in range(8)]
    final_bup = small[8 * part : 12 * part]
    return (output, input_grad, final_q, final_k, final_v, final_out, v8[0], v8[1], v8[2], v8[3], v8[4],
            final_up, final_bup, final_down, v8[5], v8[6], v8[7])


def solution(mesh):
    tok = P(("rep", "fsdp"), "seq", None)
    ids = P(("rep", "fsdp"), "seq")
    mat = P(("fsdp", "seq"), None)
    vec = P(("fsdp", "seq"))
    sizes = mesh.shape
    return jax.shard_map(
        functools.partial(body, nr=sizes["rep"], nf=sizes["fsdp"], ns=sizes["seq"]),
        mesh=mesh,
        in_specs=(tok, ids, ids, tok) + (mat,) * 4 + (vec,) * 5 + (mat, vec, mat) + (vec,) * 3,
        out_specs=(tok, tok) + (mat,) * 4 + (vec,) * 5 + (mat, vec, mat) + (vec,) * 3,
        check_vma=False,
    )
```

time: 1380 us -> 588 us (0.43)
  waiting for transfers between devices: 643 us -> 164 us
  matrix products: 380 us -> 0 us
  Pallas kernels: 0 us -> 255 us
  blocking collectives: 119 us -> 0 us
  other arithmetic: 111 us -> 48.2 us
  local copies, waits for them, and re-layouts: 105 us -> 47.8 us
  starting transfers between devices: 0.68 us -> 52.9 us
    reduce_scatter x8 -> x1, waiting for transfers between devices: 428 us -> 0.01 us  [body(): lax.psum_scatter(g_down.reshape(nf * 4 * part, width), 'fsdp', scatter_di...]
    dot_general x32 -> x0, matrix products: 380 us -> none  [the longest x6 57.7 us: matmul_left_t(): lax.dot_general(left, right, (((0,), (0,)), ((), ())), preferred_element_...]
    pallas_call x0 -> x22, Pallas kernels: none -> 255 us  [the longest x4 51.9 us: attn_bwd(): pl.pallas_call(functools.partial(attn_bwd_kernel, qb), grid=(npair,), in_...]
    psum x1, waiting for transfers between devices: 167 us -> 0.02 us  [body(): final_down = lax.psum(down_sum, 'rep').astype(F32)]
    ppermute x0 -> x65, waiting for transfers between devices: none -> 163 us  [swap(): return lax.ppermute(x, axis, [(i, i ^ xor) for i in range(size)])]
    all_gather x11 -> x0, blocking collectives: 80 us -> none  [the longest x1 10.3 us: body(): lax.all_gather(b_value, ('fsdp', 'seq'), axis=0, tiled=True)]
    ppermute x0 -> x65, starting transfers between devices: none -> 52.8 us  [swap(): return lax.ppermute(x, axis, [(i, i ^ xor) for i in range(size)])]
    reduce_sum x10 -> x0, other arithmetic: 44.2 us -> none  [the longest x2 30.6 us: attend_forward(): total = jnp.sum(shifted, -1, keepdims=True)]
  transfers between devices with their start and end apart: 17 -> 69, of which waited for: 11 -> 24; matrix products, arithmetic and copies ran while one was open for 17% -> 12% of each run, Pallas kernels for 0% -> 42%
where the time goes in v1:
time: 588 us; the launch traced here: 583 us
  Pallas kernels  255 us (43%)
  waiting for transfers between devices  164 us (28%)
  starting transfers between devices  52.9 us (9%)
  other arithmetic  48.2 us (8%)
  local copies, waits for them, and re-layouts  47.8 us (8%)
  between operations  15.2 us (3%)
    ppermute x65, waiting for transfers between devices, swap(): return lax.ppermute(x, axis, [(i, i ^ xor) for i in range(size)])  163 us
    ppermute x65, starting transfers between devices, swap(): return lax.ppermute(x, axis, [(i, i ^ xor) for i in range(size)])  52.8 us
    pallas_call x4, Pallas kernels, attn_bwd(): pl.pallas_call(functools.partial(attn_bwd_kernel, qb), grid=(npair,), in_...  51.9 us
    pallas_call x4, Pallas kernels, grad_cols(): pl.pallas_call(functools.partial(grad_cols_kernel, nl, nr, nf, want_sum),...  41.3 us
    pallas_call x4, Pallas kernels, attn_fwd(): pl.pallas_call(functools.partial(attn_fwd_kernel, qb), grid=(npair,), in_...  32.6 us
    pallas_call x1, Pallas kernels, up_part(): pl.pallas_call(functools.partial(up_kernel, got, part), grid_spec=pltpu.P...  28.6 us
    pallas_call x1, Pallas kernels, back_part(): pl.pallas_call(functools.partial(back_kernel, up, part), grid_spec=pltpu....  22.1 us
    unnamed x154, local copies, waits for them, and re-layouts  20.5 us
  transfers between devices with their start and end apart: 69, of which 24 were waited for; matrix products, arithmetic and copies ran while one was open for 12% of the time, Pallas kernels for 42%

profile of v1, /device:TPU:0, one launch (start us, length us, event | category | flops | bytes accessed | tf_op | source)
XLA Modules:
  0.0 583.2 jit_solution(3911241433382919043)
XLA Ops:
  21.1 8.3 %collective-permute-done.1.rest_2_.rest_6_ = bf16[208,1024]{1,0:T(8,128)(2,1)S(1)} collective-permute-done((bf16[208,1024]{1,0:T(8,128)(2,1)S(1)}, bf16[208,1024]{1,0:T(8,128)(2,1)S(1)}, u32[]{:S(2)}, u32[]{:S(2)}) %collective-permute-start.1) | collective-permute-done | bytes 426016 | tf_op jit(solution)/shard_map/ppermute | solution.py:37
  73.8 13.1 %project.1 = (bf16[1024,1024]{1,0:T(8,128)(2,1)}, bf16[1024,1024]{1,0:T(8,128)(2,1)}, bf16[1024,1024]{1,0:T(8,128)(2,1)}, f32[8,1024]{1,0:T(8,128)}, f32[1,4096]{1,0:T(1,128)}) custom-call(s32[16]{0:T(128)} %stack.118.ids, bf16[1024,1024]{1,0:T(8,128)(2,1)} %get-tuple-element.100.x_ref.refs_1_.refs_2_.refs_3_.refs_4_, bf16[208,1024]{1,0:T(8,128)(2,1)} %copy-done.27, ...), custom_call_target="tpu_custom_call" | custom-call | flops 6442450944 | bytes 14680064 | tf_op jit(solution)/shard_map/project/pallas_call | solution.py:186
  87.4 14.1 %collective-permute-done.17.rest_2_.rest_10_.rest_5_ = bf16[64,4096]{1,0:T(8,128)(2,1)S(1)} collective-permute-done((bf16[64,4096]{1,0:T(8,128)(2,1)S(1)}, bf16[64,4096]{1,0:T(8,128)(2,1)S(1)}, u32[]{:S(2)}, u32[]{:S(2)}) %collective-permute-start.17) | collective-permute-done | bytes 524320 | tf_op jit(solution)/shard_map/ppermute | solution.py:37
  113.4 8.3 %attend_forward.5 = (bf16[1024,256]{1,0:T(8,128)(2,1)S(1)}, bf16[1024,256]{1,0:T(8,128)(2,1)S(1)}) custom-call(bf16[1024,1024]{1,0:T(8,128)(2,1)} %get-tuple-element.61.q_ref, bf16[1024,1024]{1,0:T(8,128)(2,1)} %get-tuple-element.62.k_ref, bf16[1024,1024]{1,0:T(8,128)(2,1)} %get-tuple-element.63.v_ref, bf16[1024,128]{1,0:T(8,128)(2,1)S(1)} %get-tuple-element.142.qf_ref, ...), custom_call_target="tpu_custom_call" | custom-call | flops 4294967296 | bytes 2621440 | tf_op jit(solution)/shard_map/attend_forward/pallas_call | solution.py:244
  122.9 8.3 %attend_forward.6 = (bf16[1024,256]{1,0:T(8,128)(2,1)S(1)}, bf16[1024,256]{1,0:T(8,128)(2,1)S(1)}) custom-call(bf16[1024,1024]{1,0:T(8,128)(2,1)} %get-tuple-element.61.q_ref, bf16[1024,1024]{1,0:T(8,128)(2,1)} %get-tuple-element.62.k_ref, bf16[1024,1024]{1,0:T(8,128)(2,1)} %get-tuple-element.63.v_ref, bf16[1024,128]{1,0:T(8,128)(2,1)S(1)} %get-tuple-element.142.qf_ref, ...), custom_call_target="tpu_custom_call" | custom-call | flops 4294967296 | bytes 2621440 | tf_op jit(solution)/shard_map/attend_forward/pallas_call | solution.py:244
  132.3 8.1 %attend_forward.7 = (bf16[1024,256]{1,0:T(8,128)(2,1)S(1)}, bf16[1024,256]{1,0:T(8,128)(2,1)S(1)}) custom-call(bf16[1024,1024]{1,0:T(8,128)(2,1)} %get-tuple-element.61.q_ref, bf16[1024,1024]{1,0:T(8,128)(2,1)} %get-tuple-element.62.k_ref, bf16[1024,1024]{1,0:T(8,128)(2,1)} %get-tuple-element.63.v_ref, bf16[1024,128]{1,0:T(8,128)(2,1)S(1)} %get-tuple-element.142.qf_ref, ...), custom_call_target="tpu_custom_call" | custom-call | flops 4294967296 | bytes 2621440 | tf_op jit(solution)/shard_map/attend_forward/pallas_call | solution.py:244
  143.0 28.6 %out_norm_up.1 = (bf16[1024,1024]{1,0:T(8,128)(2,1)}, f32[1024,1024]{1,0:T(8,128)}, bf16[1024,1024]{1,0:T(8,128)(2,1)}, bf16[1024,1024]{1,0:T(8,128)(2,1)}, f32[...) custom-call(s32[16]{0:T(128)} %stack.118.ids, ...), custom_call_target="tpu_custom_call" | custom-call | flops 10737418240 | bytes 39845888 | tf_op jit(solution)/shard_map/out_norm_up/pallas_call | solution.py:356
  176.3 18.9 %down_norm.1 = (bf16[1024,1024]{1,0:T(8,128)(2,1)}, bf16[1024,1024]{1,0:T(8,128)(2,1)}, f32[1024,1024]{1,0:T(8,128)}, f32[8,1024]{1,0:T(8,128)}) custom-call(bf16[1024,4096]{1,0:T(8,128)(2,1)} %get-tuple-element.71.g_ref.lo, f32[1024,1024]{1,0:T(8,128)} %get-tuple-element.72.y_ref, bf16[1024,1024]{1,0:T(8,128)(2,1)} %maximum_select_fusion.1.c_ref, ...), custom_call_target="tpu_custom_call" | custom-call | flops 8589934592 | bytes 31457280 | tf_op jit(solution)/shard_map/down_norm/pallas_call | solution.py:410
  195.3 16.3 %hidden_gradient.1 = (bf16[1024,4096]{1,0:T(8,128)(2,1)}, f32[1,4096]{1,0:T(1,128)}) custom-call(bf16[1024,1024]{1,0:T(8,128)(2,1)} %get-tuple-element.75.df_ref.ro, bf16[1024,4096]{1,0:T(8,128)(2,1)} %get-tuple-element.76.gp_ref, bf16[4096,1024]{1,0:T(8,128)(2,1)} %all-gather.5.cloned.1.call-done.wd), custom_call_target="tpu_custom_call" | custom-call | flops 8589934592 | bytes 27262976 | tf_op jit(solution)/shard_map/hidden_gradient/pallas_call | solution.py:439
  214.6 16.5 %collective-permute-done.33.rs = bf16[1024,1024]{1,0:T(8,128)(2,1)} collective-permute-done((bf16[1024,1024]{1,0:T(8,128)(2,1)}, bf16[1024,1024]{1,0:T(8,128)(2,1)}, u32[]{:S(2)}, u32[]{:S(2)}) %collective-permute-start.33) | collective-permute-done | bytes 2097184 | tf_op jit(solution)/shard_map/ppermute | solution.py:37
  231.1 14.1 %grad_down.1.rest_16_ = bf16[4,512,1024]{2,1,0:T(8,128)(2,1)} custom-call(s32[4]{0:T(128)} %pad_add_fusion.1.jb, bf16[1024,4096]{1,0:T(8,128)(2,1)} %get-tuple-element.71.g_ref.lo, bf16[1024,4096]{1,0:T(8,128)(2,1)} %collective-permute-done.32.ls, bf16[1024,1024]{1,0:T(8,128)(2,1)} %get-tuple-element.75.df_ref.ro, ...), custom_call_target="tpu_custom_call" | custom-call | flops 8589934592 | bytes 16777216 | tf_op jit(solution)/shard_map/grad_down/pallas_call | solution.py:512
  245.2 22.1 %norm_backward.1 = (f32[1024,1024]{1,0:T(8,128)}, bf16[1024,1024]{1,0:T(8,128)(2,1)}, bf16[1024,1024]{1,0:T(8,128)(2,1)}, f32[8,1024]{1,0:T(8,128)}) custom-call(s32[16]{0:T(128)} %stack.118.ids, bf16[1024,4096]{1,0:T(8,128)(2,1)} %get-tuple-element.77.rest_0_.dh_ref, f32[1024,1024]{1,0:T(8,128)} %get-tuple-element.78.dr_ref, ...), custom_call_target="tpu_custom_call" | custom-call | flops 10737418240 | bytes 33554432 | tf_op jit(solution)/shard_map/norm_backward/pallas_call | solution.py:485
  280.2 16.5 %grad_up.1.refs_11_ = bf16[4,128,5120]{2,1,0:T(8,128)(2,1)} custom-call(s32[4]{0:T(128)} %pad_add_fusion.2.refs_0_, bf16[1024,1024]{1,0:T(8,128)(2,1)} %get-tuple-element.86.refs_1_.refs_2_.refs_3_.refs_4_, bf16[1024,1024]{1,0:T(8,128)(2,1)} %get-tuple-element.86.refs_1_.refs_2_.refs_3_.refs_4_, ...), custom_call_target="tpu_custom_call" | custom-call | flops 8589934592 | bytes 18874368 | tf_op jit(solution)/shard_map/grad_up/pallas_call | solution.py:584
  310.2 12.5 %attend_backward.4.rest_0_.refs_9_ = bf16[3,1024,256]{2,1,0:T(8,128)(2,1)S(1)} custom-call(bf16[1024,1024]{1,0:T(8,128)(2,1)} %get-tuple-element.61.q_ref, bf16[1024,1024]{1,0:T(8,128)(2,1)} %get-tuple-element.62.k_ref, bf16[1024,1024]{1,0:T(8,128)(2,1)} %get-tuple-element.63.v_ref, bf16[1024,1024]{1,0:T(8,128)(2,1)} %get-tuple-element.82.refs_11_.da_ref, ...), custom_call_target="tpu_custom_call" | custom-call | flops 10737418240 | bytes 4718592 | tf_op jit(solution)/shard_map/attend_backward/pallas_call | solution.py:294
  322.8 13.0 %attend_backward.5.rest_0_.refs_10_.rest_1_ = bf16[3,1024,256]{2,1,0:T(8,128)(2,1)S(1)} custom-call(bf16[1024,1024]{1,0:T(8,128)(2,1)} %get-tuple-element.61.q_ref, bf16[1024,1024]{1,0:T(8,128)(2,1)} %get-tuple-element.62.k_ref, bf16[1024,1024]{1,0:T(8,128)(2,1)} %get-tuple-element.63.v_ref, bf16[1024,1024]{1,0:T(8,128)(2,1)} %get-tuple-element.82.refs_11_.da_ref, ...), custom_call_target="tpu_custom_call" | custom-call | flops 10737418240 | bytes 4718592 | tf_op jit(solution)/shard_map/attend_backward/pallas_call | solution.py:294
  336.2 14.4 %collective-permute-done.39 = bf16[2,64,5120]{2,1,0:T(8,128)(2,1)} collective-permute-done((bf16[2,64,5120]{2,1,0:T(8,128)(2,1)S(1)}, bf16[2,64,5120]{2,1,0:T(8,128)(2,1)}, u32[]{:S(2)}, u32[]{:S(2)}) %collective-permute-start.39) | collective-permute-done | bytes 1310752 | tf_op jit(solution)/shard_map/ppermute | solution.py:37
  356.5 13.6 %attend_backward.6.refs_13_.refs_9_.rest_2_ = bf16[3,1024,256]{2,1,0:T(8,128)(2,1)} custom-call(bf16[1024,1024]{1,0:T(8,128)(2,1)} %get-tuple-element.61.q_ref, bf16[1024,1024]{1,0:T(8,128)(2,1)} %get-tuple-element.62.k_ref, bf16[1024,1024]{1,0:T(8,128)(2,1)} %get-tuple-element.63.v_ref, bf16[1024,1024]{1,0:T(8,128)(2,1)} %get-tuple-element.82.refs_11_.da_ref, ...), custom_call_target="tpu_custom_call" | custom-call | flops 10737418240 | bytes 4718592 | tf_op jit(solution)/shard_map/attend_backward/pallas_call | solution.py:294
  375.0 8.8 %grad_qkv.2 = (bf16[4,128,1536]{2,1,0:T(8,128)(2,1)}, f32[8,1536]{1,0:T(8,128)}) custom-call(s32[4]{0:T(128)} %pad_add_fusion.2.refs_0_, bf16[1024,1024]{1,0:T(8,128)(2,1)} %get-tuple-element.100.x_ref.refs_1_.refs_2_.refs_3_.refs_4_, bf16[1024,1024]{1,0:T(8,128)(2,1)} %get-tuple-element.100.x_ref.refs_1_.refs_2_.refs_3_.refs_4_, ...), custom_call_target="tpu_custom_call" | custom-call | flops 3221225472 | bytes 8388608 | tf_op jit(solution)/shard_map/grad_qkv/pallas_call | solution.py:584
  409.1 10.0 %collective-permute-done.44 = bf16[64,5120]{1,0:T(8,128)(2,1)} collective-permute-done((bf16[64,5120]{1,0:T(8,128)(2,1)}, bf16[64,5120]{1,0:T(8,128)(2,1)}, u32[]{:S(2)}, u32[]{:S(2)}) %collective-permute-start.44) | collective-permute-done | bytes 655392 | tf_op jit(solution)/shard_map/ppermute | solution.py:37
  429.2 12.7 %attend_backward.7.refs_10_.refs_13_.rest_3_ = bf16[3,1024,256]{2,1,0:T(8,128)(2,1)S(1)} custom-call(bf16[1024,1024]{1,0:T(8,128)(2,1)} %get-tuple-element.61.q_ref, bf16[1024,1024]{1,0:T(8,128)(2,1)} %get-tuple-element.62.k_ref, bf16[1024,1024]{1,0:T(8,128)(2,1)} %get-tuple-element.63.v_ref, bf16[1024,1024]{1,0:T(8,128)(2,1)} %get-tuple-element.82.refs_11_.da_ref, ...), custom_call_target="tpu_custom_call" | custom-call | flops 10737418240 | bytes 4718592 | tf_op jit(solution)/shard_map/attend_backward/pallas_call | solution.py:294
  442.0 37.2 %collective-permute-done.54 = bf16[64,1536]{1,0:T(8,128)(2,1)S(1)} collective-permute-done((bf16[64,1536]{1,0:T(8,128)(2,1)S(1)}, bf16[64,1536]{1,0:T(8,128)(2,1)S(1)}, u32[]{:S(2)}, u32[]{:S(2)}) %collective-permute-start.54) | collective-permute-done | bytes 196640 | tf_op jit(solution)/shard_map/ppermute | solution.py:37
  486.4 12.7 %collective-permute-done.64 = bf16[64,5120]{1,0:T(8,128)(2,1)S(1)} collective-permute-done((bf16[64,5120]{1,0:T(8,128)(2,1)S(1)}, bf16[64,5120]{1,0:T(8,128)(2,1)S(1)}, u32[]{:S(2)}, u32[]{:S(2)}) %collective-permute-start.64) | collective-permute-done | bytes 655392 | tf_op jit(solution)/shard_map/ppermute | solution.py:37
  500.0 8.8 %grad_qkv.3 = (bf16[4,128,1536]{2,1,0:T(8,128)(2,1)}, f32[8,1536]{1,0:T(8,128)}) custom-call(s32[4]{0:T(128)} %pad_add_fusion.2.refs_0_, bf16[1024,1024]{1,0:T(8,128)(2,1)} %get-tuple-element.100.x_ref.refs_1_.refs_2_.refs_3_.refs_4_, bf16[1024,1024]{1,0:T(8,128)(2,1)} %get-tuple-element.100.x_ref.refs_1_.refs_2_.refs_3_.refs_4_, ...), custom_call_target="tpu_custom_call" | custom-call | flops 3221225472 | bytes 8388608 | tf_op jit(solution)/shard_map/grad_qkv/pallas_call | solution.py:584
  543.7 14.1 %input_gradient.1 = f32[1024,1024]{1,0:T(8,128)} custom-call(s32[16]{0:T(128)} %stack.118.ids, f32[1024,1024]{1,0:T(8,128)} %get-tuple-element.81.dr_ref, bf16[3,1024,256]{2,1,0:T(8,128)(2,1)} %copy-done.1, bf16[3,1024,256]{2,1,0:T(8,128)(2,1)} %copy-done.2, bf16[3,1024,256]{2,1,0:T(8,128)(2,1)} %attend_backward.6.refs_13_.refs_9_.rest_2_, ...), custom_call_target="tpu_custom_call" | custom-call | flops 6442450944 | bytes 20971520 | tf_op jit(solution)/shard_map/input_gradient/pallas_call | solution.py:627
  (398 shorter events, 216.9 us)
Async XLA Ops:
  7.2 135.8 %all-gather.3.cloned.1.call-start = ((), (), s32[]{:S(2)}) async-start(), calls=%async_computation.1 | async-start | bytes 2359296 | tf_op jit(solution)/shard_map/all_gather | solution.py:761
  46.3 130.0 %all-gather.5.cloned.1.call-start = ((), (), s32[]{:S(2)}) async-start(), calls=%async_computation.2 | async-start | bytes 9437184 | tf_op jit(solution)/shard_map/all_gather | solution.py:762
  47.1 345.8 %reduce-scatter.2.cloned.1.call-start = ((), (), s32[]{:S(2)}) async-start(), calls=%async_computation.3 | async-start | bytes 5242880 | tf_op jit(solution)/shard_map/reduce_scatter | solution.py:783
  69.6 32.2 %collective-permute-start.18 = (bf16[64,4096]{1,0:T(8,128)(2,1)S(1)}, bf16[64,4096]{1,0:T(8,128)(2,1)S(1)}, u32[]{:S(2)}, u32[]{:S(2)}) collective-permute-start(bf16[64,4096]{1,0:T(8,128)(2,1)S(1)} %get-tuple-element.65.rest_5_.rest_0_), channel_id=1, source_target_pairs={{0,4},{2,6},{4,0},{6,2},{1,5},{3,7},{5,1},{7,3},{8,12},{10,14},{12... | collective-permute-start | bytes 1572872 | tf_op jit(solution)/shard_map/ppermute | solution.py:37
  70.7 30.9 %collective-permute-start.17 = (bf16[64,4096]{1,0:T(8,128)(2,1)S(1)}, bf16[64,4096]{1,0:T(8,128)(2,1)S(1)}, u32[]{:S(2)}, u32[]{:S(2)}) collective-permute-start(bf16[64,4096]{1,0:T(8,128)(2,1)S(1)} %get-tuple-element.66.rest_6_.rest_1_), channel_id=1, source_target_pairs={{0,4},{2,6},{4,0},{6,2},{1,5},{3,7},{5,1},{7,3},{8,12},{10,14},{12... | collective-permute-start | bytes 1572872 | tf_op jit(solution)/shard_map/ppermute | solution.py:37
  71.6 30.4 %collective-permute-start.19 = (bf16[64,4096]{1,0:T(8,128)(2,1)S(1)}, bf16[64,4096]{1,0:T(8,128)(2,1)S(1)}, u32[]{:S(2)}, u32[]{:S(2)}) collective-permute-start(bf16[64,4096]{1,0:T(8,128)(2,1)S(1)} %get-tuple-element.66.rest_6_.rest_1_), channel_id=1, source_target_pairs={{0,2},{2,0},{4,6},{6,4},{1,3},{3,1},{5,7},{7,5},{8,10},{10,8},{12,... | collective-permute-start | bytes 1572872 | tf_op jit(solution)/shard_map/ppermute | solution.py:37
  73.0 40.1 %collective-permute-start.22 = (bf16[64,4096]{1,0:T(8,128)(2,1)S(1)}, bf16[64,4096]{1,0:T(8,128)(2,1)S(1)}, u32[]{:S(2)}, u32[]{:S(2)}) collective-permute-start(bf16[64,4096]{1,0:T(8,128)(2,1)S(1)} %get-tuple-element.65.rest_5_.rest_0_), channel_id=1, source_target_pairs={{0,1},{1,0},{2,3},{3,2},{4,5},{5,4},{6,7},{7,6},{8,9},{9,8},{10,11... | collective-permute-start | bytes 1572872 | tf_op jit(solution)/shard_map/ppermute | solution.py:37
  87.4 34.3 %collective-permute-start.23 = (bf16[64,4096]{1,0:T(8,128)(2,1)S(1)}, bf16[64,4096]{1,0:T(8,128)(2,1)S(1)}, u32[]{:S(2)}, u32[]{:S(2)}) collective-permute-start(bf16[64,4096]{1,0:T(8,128)(2,1)S(1)} %get-tuple-element.66.rest_6_.rest_1_), channel_id=1, source_target_pairs={{0,1},{1,0},{2,3},{3,2},{4,5},{5,4},{6,7},{7,6},{8,9},{9,8},{10,11... | collective-permute-start | bytes 1572872 | tf_op jit(solution)/shard_map/ppermute | solution.py:37
  132.1 40.1 %collective-permute-start.30 = (bf16[2,512,1024]{2,1,0:T(8,128)(2,1)S(1)}, bf16[2,512,1024]{2,1,0:T(8,128)(2,1)}, u32[]{:S(2)}, u32[]{:S(2)}) collective-permute-start(bf16[2,512,1024]{2,1,0:T(8,128)(2,1)S(1)} %copy-done.49), channel_id=1, source_target_pairs={{0,1},{1,0},{2,3},{3,2},{4,5},{5,4},{6,7},{7,6},{8,9},{9,8},{10,11... | collective-permute-start | bytes 6291464 | tf_op jit(solution)/shard_map/ppermute | solution.py:37
  171.7 42.6 %collective-permute-start.32 = (bf16[1024,4096]{1,0:T(8,128)(2,1)}, bf16[1024,4096]{1,0:T(8,128)(2,1)}, u32[]{:S(2)}, u32[]{:S(2)}) collective-permute-start(bf16[1024,4096]{1,0:T(8,128)(2,1)} %get-tuple-element.71.g_ref.lo), channel_id=1, source_target_pairs={{0,1},{1,0},{2,3},{3,2},{4,5},{5,4},{6,7},{7,6},{8,9},{9,8},{10,11... | collective-permute-start | bytes 25165832 | tf_op jit(solution)/shard_map/ppermute | solution.py:37
  211.6 68.6 %collective-permute-start.37 = (bf16[1024,4096]{1,0:T(8,128)(2,1)}, bf16[1024,4096]{1,0:T(8,128)(2,1)}, u32[]{:S(2)}, u32[]{:S(2)}) collective-permute-start(bf16[1024,4096]{1,0:T(8,128)(2,1)} %get-tuple-element.77.rest_0_.dh_ref), channel_id=1, source_target_pairs={{0,1},{1,0},{2,3},{3,2},{4,5},{5,4},{6,7},{7,6},{8,9},{9,8},{10,11... | collective-permute-start | bytes 25165832 | tf_op jit(solution)/shard_map/ppermute | solution.py:37
  212.7 67.5 %collective-permute-start.36 = (bf16[1024,1024]{1,0:T(8,128)(2,1)}, bf16[1024,1024]{1,0:T(8,128)(2,1)}, u32[]{:S(2)}, u32[]{:S(2)}) collective-permute-start(bf16[1024,1024]{1,0:T(8,128)(2,1)} %get-tuple-element.86.refs_1_.refs_2_.refs_3_.refs_4_), channel_id=1, source_target_pairs={{0,1},{1,0},{2,3},{3,2},{4,5},{5,4},{6,7},{7,6},{8,9},{9,8},{10,11... | collective-permute-start | bytes 6291464 | tf_op jit(solution)/shard_map/ppermute | solution.py:37
  213.0 83.7 %collective-permute-start.34 = (bf16[1024,1024]{1,0:T(8,128)(2,1)S(1)}, bf16[1024,1024]{1,0:T(8,128)(2,1)}, u32[]{:S(2)}, u32[]{:S(2)}) collective-permute-start(bf16[1024,1024]{1,0:T(8,128)(2,1)S(1)} %copy-done.38), channel_id=1, source_target_pairs={{0,1},{1,0},{2,3},{3,2},{4,5},{5,4},{6,7},{7,6},{8,9},{9,8},{10,11... | collective-permute-start | bytes 6291464 | tf_op jit(solution)/shard_map/ppermute | solution.py:37
  214.3 56.8 %collective-permute-start.31 = (bf16[512,1024]{1,0:T(8,128)(2,1)}, bf16[512,1024]{1,0:T(8,128)(2,1)}, u32[]{:S(2)}, u32[]{:S(2)}) collective-permute-start(bf16[512,1024]{1,0:T(8,128)(2,1)} %broadcast_select_fusion), channel_id=1, source_target_pairs={{0,1},{1,0},{2,3},{3,2},{4,5},{5,4},{6,7},{7,6},{8,9},{9,8},{10,11... | collective-permute-start | bytes 3145736 | tf_op jit(solution)/shard_map/ppermute | solution.py:37
  279.5 199.9 %all-reduce.3.cloned.1.call-start = ((), (), s32[]{:S(2)}) async-start(), calls=%async_computation.4 | async-start | bytes 2097152 | tf_op jit(solution)/shard_map/psum | solution.py:784
  307.3 43.3 %collective-permute-start.39 = (bf16[2,64,5120]{2,1,0:T(8,128)(2,1)S(1)}, bf16[2,64,5120]{2,1,0:T(8,128)(2,1)}, u32[]{:S(2)}, u32[]{:S(2)}) collective-permute-start(bf16[2,64,5120]{2,1,0:T(8,128)(2,1)S(1)} %slice.368), channel_id=1, source_target_pairs={{0,4},{2,6},{4,0},{6,2},{1,5},{3,7},{5,1},{7,3},{8,12},{10,14},{12... | collective-permute-start | bytes 3932168 | tf_op jit(solution)/shard_map/ppermute | solution.py:37
  309.0 45.2 %collective-permute-start.38 = (bf16[2,64,5120]{2,1,0:T(8,128)(2,1)S(1)}, bf16[2,64,5120]{2,1,0:T(8,128)(2,1)}, u32[]{:S(2)}, u32[]{:S(2)}) collective-permute-start(bf16[2,64,5120]{2,1,0:T(8,128)(2,1)S(1)} %slice_bitcast_fusion), channel_id=1, source_target_pairs={{0,2},{2,0},{4,6},{6,4},{1,3},{3,1},{5,7},{7,5},{8,10},{10,8},{12,... | collective-permute-start | bytes 3932168 | tf_op jit(solution)/shard_map/ppermute | solution.py:37
  322.8 50.6 %collective-permute-start.40 = (bf16[3,1024,256]{2,1,0:T(8,128)(2,1)S(1)}, bf16[3,1024,256]{2,1,0:T(8,128)(2,1)S(1)}, u32[]{:S(2)}, u32[]{:S(2)}) collective-permute-start(bf16[3,1024,256]{2,1,0:T(8,128)(2,1)S(1)} %attend_backward.4.rest_0_.refs_9_), channel_id=1, source_target_pairs={{0,1},{1,0},{2,3},{3,2},{4,5},{5,4},{6,7},{7,6},{8,9},{9,8},{10,11... | collective-permute-start | bytes 4718600 | tf_op jit(solution)/shard_map/ppermute | solution.py:37
  335.9 37.5 %collective-permute-start.41 = (bf16[3,1024,256]{2,1,0:T(8,128)(2,1)S(1)}, bf16[3,1024,256]{2,1,0:T(8,128)(2,1)S(1)}, u32[]{:S(2)}, u32[]{:S(2)}) collective-permute-start(bf16[3,1024,256]{2,1,0:T(8,128)(2,1)S(1)} %attend_backward.5.rest_0_.refs_10_.rest_1_), channel_id=1, source_target_pairs={{0,1},{1,0},{2,3},{3,2},{4,5},{5,4},{6,7},{7,6},{8,9},{9,8},{10,11... | collective-permute-start | bytes 4718600 | tf_op jit(solution)/shard_map/ppermute | solution.py:37
  370.2 129.8 %collective-permute-start.45 = (bf16[3,1024,256]{2,1,0:T(8,128)(2,1)}, bf16[3,1024,256]{2,1,0:T(8,128)(2,1)}, u32[]{:S(2)}, u32[]{:S(2)}) collective-permute-start(bf16[3,1024,256]{2,1,0:T(8,128)(2,1)} %attend_backward.6.refs_13_.refs_9_.rest_2_), channel_id=1, source_target_pairs={{0,1},{1,0},{2,3},{3,2},{4,5},{5,4},{6,7},{7,6},{8,9},{9,8},{10,11... | collective-permute-start | bytes 4718600 | tf_op jit(solution)/shard_map/ppermute | solution.py:37
  388.5 30.6 %collective-permute-start.44 = (bf16[64,5120]{1,0:T(8,128)(2,1)}, bf16[64,5120]{1,0:T(8,128)(2,1)}, u32[]{:S(2)}, u32[]{:S(2)}) collective-permute-start(bf16[64,5120]{1,0:T(8,128)(2,1)} %broadcast_select_fusion.4), channel_id=1, source_target_pairs={{0,8},{8,0},{16,24},{24,16},{1,9},{9,1},{17,25},{25,17},{2,10},{10... | collective-permute-start | bytes 1966088 | tf_op jit(solution)/shard_map/ppermute | solution.py:37
  420.4 61.7 %collective-permute-start.49 = (bf16[64,5120]{1,0:T(8,128)(2,1)S(1)}, bf16[64,5120]{1,0:T(8,128)(2,1)}, u32[]{:S(2)}, u32[]{:S(2)}) collective-permute-start(bf16[64,5120]{1,0:T(8,128)(2,1)S(1)} %add_convert_fusion.2.rest_1_), channel_id=1, source_target_pairs={{0,16},{8,24},{16,0},{24,8},{1,17},{9,25},{17,1},{25,9},{2,18},{10... | collective-permute-start | bytes 1966088 | tf_op jit(solution)/shard_map/ppermute | solution.py:37
  427.8 51.4 %collective-permute-start.54 = (bf16[64,1536]{1,0:T(8,128)(2,1)S(1)}, bf16[64,1536]{1,0:T(8,128)(2,1)S(1)}, u32[]{:S(2)}, u32[]{:S(2)}) collective-permute-start(bf16[64,1536]{1,0:T(8,128)(2,1)S(1)} %add_convert_fusion.8), channel_id=1, source_target_pairs={{0,16},{8,24},{16,0},{24,8},{1,17},{9,25},{17,1},{25,9},{2,18},{10... | collective-permute-start | bytes 589832 | tf_op jit(solution)/shard_map/ppermute | solution.py:37
  442.0 58.1 %collective-permute-start.46 = (bf16[3,1024,256]{2,1,0:T(8,128)(2,1)S(1)}, bf16[3,1024,256]{2,1,0:T(8,128)(2,1)}, u32[]{:S(2)}, u32[]{:S(2)}) collective-permute-start(bf16[3,1024,256]{2,1,0:T(8,128)(2,1)S(1)} %attend_backward.7.refs_10_.refs_13_.rest_3_), channel_id=1, source_target_pairs={{0,1},{1,0},{2,3},{3,2},{4,5},{5,4},{6,7},{7,6},{8,9},{9,8},{10,11... | collective-permute-start | bytes 4718600 | tf_op jit(solution)/shard_map/ppermute | solution.py:37
  (120 other events, 1311.1 us)
Sparse Core Ops, SparseCore 0:
  46.4 35.1 all-gather.2
  83.5 63.9 all-gather.4
  279.6 65.5 reduce-scatter.1
  393.0 79.4 all-reduce.2

commit v2 on v1

--- a/solution.py
+++ b/solution.py
@@ -43,54 +43,50 @@
 
     def copies(self, refs, ids, targets, sems):
         out = []
-        for which, index, half, slot in self.entries:
+        for which, index, base, half, slot in self.entries:
             low = half * self.half
             for first, rows, dest, stride, offset in targets:
                 a, b = max(first, low), min(first + rows, low + self.half)
                 if a >= b:
                     continue
-                src = refs[which].at[(*index, pl.ds(a - low, b - a))]
+                src = refs[which].at[(*index, pl.ds(base + a - low, b - a))]
                 start = pl.multiple_of(ids[slot] * stride + (offset + a - first), 16)
                 out.append(pltpu.make_async_copy(src, dest.at[pl.ds(start, b - a)], sems.at[len(out)]))
         return out
 
     def count(self, targets):
         n = 0
-        for _, _, half, _ in self.entries:
+        for _, _, _, half, _ in self.entries:
             low = half * self.half
             n += sum(max(t[0], low) < min(t[0] + t[1], low + self.half) for t in targets)
         return n
 
 
-def gather_start(halves, nf):
+def gather_start(shard, nf):
     if nf == 4:
-        one, two = halves
-        return {
-            "xa": swap(one, "fsdp", nf, 1),
-            "yb": swap(two, "fsdp", nf, 2),
-            "ya": swap(one, "fsdp", nf, 2),
-            "xb": swap(two, "fsdp", nf, 1),
-        }
-    return {"all": [lax.all_gather(h, "fsdp", axis=0) for h in halves]}
+        return [swap(shard, "fsdp", nf, 1), swap(shard, "fsdp", nf, 2)]
+    return [lax.all_gather(shard, "fsdp", axis=0)]
 
 
 def gather_far(first, nf):
     if nf == 4:
-        return swap(first["xa"], "fsdp", nf, 2), swap(first["yb"], "fsdp", nf, 1)
-    return ()
-
-
-def gather_end(halves, first, far, nf, ns):
-    half = halves[0].shape[0]
+        half = first[0].shape[0] // 2
+        return [swap(first[0][:half], "fsdp", nf, 2), swap(first[1][half:], "fsdp", nf, 1)]
+    return []
+
+
+def gather_end(shard, first, far, nf, ns):
+    half = shard.shape[0] // 2
     if nf == 4:
-        arrays = [halves[0], halves[1], first["xa"], first["xb"], first["ya"], first["yb"], far[0], far[1]]
-        entries = [(w, (), w % 2, 2 * (w // 2)) for w in range(8)]
+        arrays = [shard, *first, *far]
+        entries = [(w, (), h * half, h, 2 * w) for w in range(3) for h in range(2)]
+        entries += [(3, (), 0, 0, 6), (4, (), 0, 1, 6)]
     else:
-        arrays = list(first["all"])
-        entries = [(h, (f,), h, 2 * nf + 2 * f) for f in range(nf) for h in range(2)]
+        arrays = list(first)
+        entries = [(0, (f,), h * half, h, 2 * nf + 2 * f) for f in range(nf) for h in range(2)]
     n = len(arrays)
     arrays = arrays + [swap(a, "seq", ns, 1) for a in arrays]
-    entries = entries + [(w + n, i, h, s + 1) for w, i, h, s in entries]
+    entries = entries + [(w + n, i, r, h, s + 1) for w, i, r, h, s in entries]
     return Gathered(arrays, entries, half)
 
 
@@ -113,10 +109,10 @@
     return pl.pallas_call(
         functools.partial(split_kernel, moves, len(ins), len(out_shapes)),
         in_specs=[ANY] * (len(ins) + len(deps)),
-        out_specs=[ANY] * len(out_shapes),
+        out_specs=[pl.BlockSpec(memory_space=pltpu.VMEM)] * len(out_shapes),
         out_shape=[jax.ShapeDtypeStruct(o, BF) for o in out_shapes],
         scratch_shapes=[pltpu.SemaphoreType.DMA((len(moves),))],
-        compiler_params=params(4 << 20),
+        compiler_params=params(),
         name=name,
     )(*ins, *deps)
 
@@ -143,9 +139,78 @@
     )(*vecs)
 
 
+def pair_kernel(count, core, *refs):
+    ins, outs, sems = refs[: 2 * len(count)], refs[len(refs) - 1 - sum(count) : -1], refs[-1]
+    c = core[0]
+    at, moves = 0, []
+    for i, n in enumerate(count):
+        mine, theirs = ins[2 * i], ins[2 * i + 1]
+        half = mine.shape[1]
+        for k in range(n):
+            which = c if k == 0 else 1 - c
+            for src, place in ((mine, c), (theirs, 1 - c)):
+                start = pl.multiple_of(place * half, half)
+                moves.append(pltpu.make_async_copy(src.at[which], outs[at].at[pl.ds(start, half)], sems.at[len(moves)]))
+            at += 1
+    for m in moves:
+        m.start()
+    for m in moves:
+        m.wait()
+
+
+def pair_up(core, items, deps=()):
+    count = [n for _, _, n in items]
+    flat = [z for a, b, _ in items for z in (a, b)]
+    shapes = [jax.ShapeDtypeStruct((2 * a.shape[1], a.shape[2]), a.dtype) for a, _, n in items for _ in range(n)]
+    return pl.pallas_call(
+        functools.partial(pair_kernel, count),
+        grid_spec=pltpu.PrefetchScalarGridSpec(
+            num_scalar_prefetch=1,
+            grid=(1,),
+            in_specs=[ANY] * (len(flat) + len(deps)),
+            out_specs=[pl.BlockSpec(z.shape, lambda i, core: (0, 0)) for z in shapes],
+            scratch_shapes=[pltpu.SemaphoreType.DMA((2 * len(shapes),))],
+        ),
+        out_shape=shapes,
+        compiler_params=params(),
+        name="pair_up",
+    )(core, *flat, *deps)
+
+
+def unpair_kernel(core, own, theirs, *rest):
+    out, sems = rest[-2:]
+    c = core[0]
+    half = out.shape[1]
+    start = pl.multiple_of(c * half, half)
+    cut = lambda z: z.at[pl.ds(start, half)] if z.shape[0] > half else z
+    one = pltpu.make_async_copy(cut(own), out.at[c], sems.at[0])
+    two = pltpu.make_async_copy(cut(theirs), out.at[1 - c], sems.at[1])
+    one.start()
+    two.start()
+    one.wait()
+    two.wait()
+
+
+def unpair_up(core, own, theirs, half, deps=()):
+    width = own.shape[1]
+    return pl.pallas_call(
+        unpair_kernel,
+        grid_spec=pltpu.PrefetchScalarGridSpec(
+            num_scalar_prefetch=1,
+            grid=(1,),
+            in_specs=[ANY] * (2 + len(deps)),
+            out_specs=pl.BlockSpec((2, half, width), lambda i, core: (0, 0, 0)),
+            scratch_shapes=[pltpu.SemaphoreType.DMA((2,))],
+        ),
+        out_shape=jax.ShapeDtypeStruct((2, half, width), own.dtype),
+        compiler_params=params(),
+        name="unpair",
+    )(core, own, theirs, *deps)
+
+
 def qkv_kernel(got, ids, x_ref, *rest):
     n = len(got.arrays)
-    pieces, (q_ref, k_ref, v_ref, p_ref, b_ref, wq, wk, wv, wb, sems) = rest[:n], rest[n:]
+    pieces, (q_ref, k_ref, v_ref, p_ref, b_ref, wq, wk, wv, wb, sems) = rest[:n], rest[-10:]
     width = x_ref.shape[1]
     nb = wb.shape[0] // BIAS_ROWS
     part = width // nb
@@ -177,7 +242,7 @@
     return t
 
 
-def project(x, got, ids, nb, block=256):
+def project(x, got, ids, nb, deps=(), block=256):
     n, width = x.shape
     grid = n // block
     rows = pl.BlockSpec((block, width), lambda i, ids: (i, 0))
@@ -188,7 +253,7 @@
         grid_spec=pltpu.PrefetchScalarGridSpec(
             num_scalar_prefetch=1,
             grid=(grid,),
-            in_specs=[rows] + [ANY] * len(got.arrays),
+            in_specs=[rows] + [ANY] * (len(got.arrays) + len(deps)),
             out_specs=[rows, rows, rows, whole((8, width)), whole((1, 4 * width))],
             scratch_shapes=[pltpu.VMEM((width, width), BF)] * 3
             + [pltpu.VMEM((nb * BIAS_ROWS, width), BF), pltpu.SemaphoreType.DMA((count,))],
@@ -198,7 +263,7 @@
         compiler_params=params(),
         cost_estimate=cost(6 * n * width * width, 2 * n * width * 4 + 6 * width * width),
         name="project",
-    )(ids, x, *got.arrays)
+    )(ids, x, *got.arrays, *deps)
 
 
 def split3(v):
@@ -248,7 +313,7 @@
         cost_estimate=pl.CostEstimate(flops=npair*2*2*2*n*n*256,bytes_accessed=npair*n*LANES*2*5,transcendentals=npair*2*n*n),
         name="attend_forward")(q,k,v,qf,kf,*deps)
 def attn_bwd_kernel(qb,q_ref,k_ref,v_ref,da_ref,a_ref,lf_ref,kf_ref,*rest):
-    d_ref,dka,dva=rest[-3:]
+    d_ref,s_ref,dka,dva=rest[-4:]
     n=q_ref.shape[0]
     lane=lax.broadcasted_iota(jnp.int32,(n,LANES),1)
     left=lane<HEAD_DIM
@@ -267,6 +332,7 @@
         sides.append((jnp.where(own,q,lf),jnp.where(own,k,kf),jnp.where(own,v,minus),jnp.where(own,da,df),
                       jnp.where(own,q,zero),jnp.where(own,da,zero)))
     kt=k.T
+    sq=jnp.zeros((1,LANES),F32)
     for c in range(n//qb):
         rows=slice(c*qb,(c+1)*qb)
         dqs=[]; dk=None; dv=None
@@ -280,11 +346,16 @@
             x=dg(pb,daz[rows],NN); dv=x if dv is None else dv+x
             y=dg(ds,qz[rows],NN); dk=y if dk is None else dk+y
             dqs.append(dg(kt[h*64:(h+1)*64],ds,NN))
-        d_ref[0,rows,:]=(jnp.concatenate(dqs,0).T*0.125).astype(BF)
+        dqb=(jnp.concatenate(dqs,0).T*0.125).astype(BF)
+        d_ref[0,rows,:]=dqb
+        sq=sq+jnp.sum(dqb.astype(F32),0,keepdims=True)
         if c==0: dka[...]=dk; dva[...]=dv
         else: dka[...]+=dk; dva[...]+=dv
     d_ref[1]=dka[...].astype(BF)
-    d_ref[2]=dva[...].astype(BF)
+    dvb=dva[...].astype(BF)
+    d_ref[2]=dvb
+    s_ref[0:1,:]=sq
+    s_ref[1:2,:]=jnp.sum(dvb.astype(F32),0,keepdims=True)
 def attn_bwd(q,k,v,da,a,lf,kf,first,npair,deps=(),qb=256):
     n=q.shape[0]
     blk=pl.BlockSpec((n,LANES),lambda i:(0,i+first))
@@ -292,8 +363,8 @@
     own=pl.BlockSpec((n,LANES),lambda i:(0,i))
     out=pl.BlockSpec((3,n,LANES),lambda i:(0,0,i))
     return pl.pallas_call(functools.partial(attn_bwd_kernel,qb),grid=(npair,),
-        in_specs=[blk]*5+[own,whole]+[ANY]*len(deps),out_specs=out,
-        out_shape=jax.ShapeDtypeStruct((3,n,npair*LANES),BF),
+        in_specs=[blk]*5+[own,whole]+[ANY]*len(deps),out_specs=[out,pl.BlockSpec((8,LANES),lambda i:(0,i))],
+        out_shape=[jax.ShapeDtypeStruct((3,n,npair*LANES),BF),jax.ShapeDtypeStruct((8,npair*LANES),F32)],
         scratch_shapes=[pltpu.VMEM((n,LANES),F32)]*2,
         compiler_params=pltpu.CompilerParams(vmem_limit_bytes=50<<20),
         cost_estimate=pl.CostEstimate(flops=npair*2*5*2*n*n*256,bytes_accessed=npair*n*LANES*2*9,transcendentals=npair*2*n*n),
@@ -524,83 +595,105 @@
     )(jb, g_own, g_sib, df_own, df_sib, *deps)
 
 
-def grad_cols_kernel(nl, nr, nf, want_sum, *refs):
-    los, lss = refs[1 : 1 + nl], refs[1 + nl : 1 + 2 * nl]
-    ros, rss = refs[1 + 2 * nl : 1 + 2 * nl + nr], refs[1 + 2 * nl + nr : 1 + 2 * nl + 2 * nr]
-    outs = refs[-3:-1] if want_sum else refs[-2:-1]
-    lt = refs[-1]
-    n, wide = los[0].shape
+class Job:
+    def __init__(self, left, rights):
+        self.left, self.rights = left, rights
+
+
+def grad_cols_kernel(jobs, nl, nf, block, keeps, *refs):
+    pos = 1
+    step = pl.program_id(0)
+    lefts, rights = [], []
+    for spans in jobs:
+        lefts.append((refs[pos : pos + nl], refs[pos + nl : pos + 2 * nl]))
+        pos += 2 * nl
+    for spans in jobs:
+        for _ in spans:
+            rights.append((refs[pos], refs[pos + 1]))
+            pos += 2
+    outs = refs[len(refs) - len(jobs) - 4 : len(refs) - len(jobs)]
+    lts = refs[len(refs) - len(jobs) :]
+    n, wide = lefts[0][0][0].shape
     part = nl * wide // nf
-
-    @pl.when(pl.program_id(0) == 0)
-    def _():
-        for j in range(nl):
-            lt[j * wide : (j + 1) * wide, 0:n] = los[j][...].T
-            lt[j * wide : (j + 1) * wide, n : 2 * n] = lss[j][...].T
-
-    left = lt[...]
+    half = part // 2
     at = 0
-    for k in range(nr):
-        planes = ros[k].shape[0]
-        for m in range(planes):
-            both = jnp.concatenate([ros[k][m], rss[k][m]], 0)
-            cols = both.shape[1]
-            got = dg(left, both, NN).astype(BF)
-            for j in range(nf):
-                outs[0][j, :, at : at + cols] = got[j * part : (j + 1) * part]
-            if want_sum:
-                outs[1][:, at : at + cols] = jnp.broadcast_to(jnp.sum(both.astype(F32), 0, keepdims=True), (8, cols))
-            at += cols
-
-
-def grad_cols(l_own, l_sib, r_own, r_sib, jb, nf, block, name, want_sum=False, deps=(), into=None, at=0, total=None):
-    n, width = l_own.shape
+    for (los, lss), spans, lt in zip(lefts, jobs, lts):
+
+        @pl.when(step == spans[0][0])
+        def _():
+            for j in range(nl):
+                lt[j * wide : (j + 1) * wide, 0:n] = los[j][...].T
+                lt[j * wide : (j + 1) * wide, n : 2 * n] = lss[j][...].T
+
+        for begin, count in spans:
+            own, sib = rights[at]
+            at += 1
+
+            @pl.when((step >= begin) & (step < begin + count))
+            def _():
+                both = jnp.concatenate([own[0], sib[0]], 0)
+                got = dg(lt[...], both, NN).astype(BF)
+                for out, (which, side) in zip(outs, keeps):
+                    for m, j in enumerate(which):
+                        out[m, 0:half, :] = got[j * part + side * half : j * part + (side + 1) * half]
+
+
+def grad_cols(jobs, jb, nf, block, name, deps=()):
+    n, width = jobs[0].left[0].shape
     part = width // (2 * nf)
-    nr = len(r_own)
-    steps = r_own[0].shape[2] // block
-    planes = sum(r.shape[0] for r in r_own)
-    here = planes * block
-    assert steps == 1 or (nr == 1 and planes == 1)
-    if part % LANES == 0:
-        nl = nf
-        lefts = [pl.BlockSpec((n, part), lambda i, jb, j=j: (0, jb[j])) for j in range(nf)]
-    else:
-        nl = 1
+    spans, step = [], 0
+    in_specs, operands, right_specs, right_ops = [], [], [], []
+    for job in jobs:
+        mine = []
         pick = lambda z: z.reshape(n, 2 * nf, part)[:, jb].reshape(n, nf * part)
-        l_own, l_sib = pick(l_own), pick(l_sib)
-        lefts = [pl.BlockSpec((n, nf * part), lambda i, jb: (0, 0))]
-    rights = [pl.BlockSpec((r.shape[0], n, block), lambda i, jb: (0, 0, i)) for r in r_own]
-    shift = at // here
-    out_specs = [pl.BlockSpec((nf, part, here), lambda i, jb: (0, 0, i + shift))]
-    total = total or here * steps
-    out_shape = [jax.ShapeDtypeStruct((nf, part, total), BF)]
-    if want_sum:
-        out_specs.append(pl.BlockSpec((8, here), lambda i, jb: (0, 0)))
-        out_shape.append(jax.ShapeDtypeStruct((8, here), F32))
-    alias = {}
-    if into is not None:
-        alias = {1 + 2 * nl + 2 * nr: 0}
-        deps = (into,) + tuple(deps)
-    return pl.pallas_call(
-        functools.partial(grad_cols_kernel, nl, nr, nf, want_sum),
+        for z in job.left:
+            if part % LANES == 0:
+                nl = nf
+                in_specs += [pl.BlockSpec((n, part), lambda i, jb, j=j: (0, jb[j])) for j in range(nf)]
+                operands += [z] * nf
+            else:
+                nl = 1
+                in_specs += [pl.BlockSpec((n, nf * part), lambda i, jb: (0, 0))]
+                operands += [pick(z)]
+        for own, sib in job.rights:
+            planes, _, cols = own.shape
+            per = cols // block
+            count = planes * per
+
+            def at(i, jb, step=step, count=count, per=per):
+                k = jnp.clip(i - step, 0, count - 1)
+                return (k // per, 0, k % per)
+
+            right_specs += [pl.BlockSpec((1, n, block), at)] * 2
+            right_ops += [own, sib]
+            mine.append((step, count))
+            step += count
+        spans.append(mine)
+    half = part // 2
+    js = list(range(nf))
+    top = nf // 2
+    keeps = [([j for j in js if not j & 1], 0), ([j for j in js if j & 1], 0), ([j for j in js if j < top], 1), ([j for j in js if j >= top], 1)]
+    out_spec = pl.BlockSpec((nf // 2, half, block), lambda i, jb: (0, 0, i))
+    out_shape = jax.ShapeDtypeStruct((nf // 2, half, step * block), BF)
+    return pl.pallas_call(
+        functools.partial(grad_cols_kernel, spans, nl, nf, block, keeps),
         grid_spec=pltpu.PrefetchScalarGridSpec(
             num_scalar_prefetch=1,
-            grid=(steps,),
-            in_specs=lefts * 2 + rights * 2 + [ANY] * len(deps),
-            out_specs=out_specs,
-            scratch_shapes=[pltpu.VMEM((nf * part, 2 * n), BF)],
+            grid=(step,),
+            in_specs=in_specs + right_specs + [ANY] * len(deps),
+            out_specs=[out_spec] * 4,
+            scratch_shapes=[pltpu.VMEM((nf * part, 2 * n), BF)] * len(jobs),
         ),
-        out_shape=out_shape,
-        input_output_aliases=alias,
-        compiler_params=params(),
-        cost_estimate=cost(2 * n * width * here * steps, 4 * n * (here * steps + width // 2)),
+        out_shape=[out_shape] * 4,
+        compiler_params=params(),
+        cost_estimate=cost(2 * n * width * step * block, 4 * n * (step * block + width // 2)),
         name=name,
-    )(jb, *([l_own] * nl), *([l_sib] * nl), *r_own, *r_sib, *deps)
-
-
-def input_kernel(got, part, groups, ids, dr_ref, *rest):
+    )(jb, *operands, *right_ops, *deps)
+
+
+def input_kernel(got, part, groups, place, ids, dr_ref, *rest):
     n = len(got.arrays)
-    d_refs, pieces = rest[:groups], rest[groups : groups + n]
+    d_refs, pieces = rest[1 : 1 + groups], rest[1 + groups : 1 + groups + n]
     out_ref, wq, wk, wv, sems = rest[-5:]
     targets = qkv_targets(part, wq, wk, wv, None)
 
@@ -619,70 +712,98 @@
     out_ref[...] = total
 
 
-def input_part(dr, grads, got, ids, nb, deps=(), block=256):
+def input_part(dr, grads, got, ids, place, nb, deps=(), block=256):
     n, width = dr.shape
-    rows = pl.BlockSpec((block, width), lambda i, ids: (i, 0))
-    three = lambda w: pl.BlockSpec((3, block, w), lambda i, ids: (0, i, 0))
+    steps = n // 2 // block
+    rows = pl.BlockSpec((block, width), lambda i, ids: (i + ids[ids.shape[0] - 2 + place] * steps, 0))
+    three = lambda w: pl.BlockSpec((3, block, w), lambda i, ids: (0, i + ids[ids.shape[0] - 2 + place] * steps, 0))
     count = got.count(qkv_targets(width // nb, 0, 0, 0, None))
     return pl.pallas_call(
-        functools.partial(input_kernel, got, width // nb, len(grads)),
+        functools.partial(input_kernel, got, width // nb, len(grads), place),
         grid_spec=pltpu.PrefetchScalarGridSpec(
             num_scalar_prefetch=1,
-            grid=(n // block,),
-            in_specs=[rows] + [three(a.shape[2]) for a in grads] + [ANY] * (len(got.arrays) + len(deps)),
-            out_specs=rows,
+            grid=(steps,),
+            in_specs=[rows, ANY] + [three(a.shape[2]) for a in grads] + [ANY] * (len(got.arrays) + len(deps)),
+            out_specs=pl.BlockSpec((block, width), lambda i, ids: (i, 0)),
             scratch_shapes=[pltpu.VMEM((width, width), BF)] * 3 + [pltpu.SemaphoreType.DMA((count,))],
         ),
-        out_shape=jax.ShapeDtypeStruct((n, width), F32),
-        compiler_params=params(),
-        cost_estimate=cost(6 * n * width * width, 14 * n * width + 6 * width * width),
+        out_shape=jax.ShapeDtypeStruct((n // 2, width), F32),
+        compiler_params=params(),
+        cost_estimate=cost(3 * n * width * width, 7 * n * width + 6 * width * width),
         name="input_gradient",
-    )(ids, dr, *grads, *got.arrays, *deps)
+    )(ids, dr, dr, *grads, *got.arrays, *deps)
 
 
 def add_low(a, b):
     return lax.optimization_barrier((a.astype(F32) + b.astype(F32)).astype(BF))
 
 
+def stage_kernel(last, odd, ka, ra, kb, rb, *outs):
+    add = lambda a, b: (a[...].astype(F32) + b[...].astype(F32)).astype(BF)
+    a, b = add(ka, ra), add(kb, rb)
+    m = a.shape[0]
+    if last:
+        swapped = odd[0] == 1
+        outs[0][...] = jnp.where(swapped, b, a)
+        outs[1][...] = jnp.where(swapped, a, b)
+    else:
+        for i in range(m // 2):
+            outs[0][i], outs[1][i] = a[2 * i], a[2 * i + 1]
+            outs[2][i], outs[3][i] = b[i], b[m // 2 + i]
+
+
+def stage(odd, ka, ra, kb, rb, name, block=512):
+    m, rows, cols = ka.shape
+    block = min(block, cols)
+    while cols % block:
+        block //= 2
+    last = m == 1
+    into = pl.BlockSpec((m, rows, block), lambda i, odd: (0, 0, i))
+    mo = max(m // 2, 1)
+    out = pl.BlockSpec((mo, rows, block), lambda i, odd: (0, 0, i))
+    return pl.pallas_call(
+        functools.partial(stage_kernel, last),
+        grid_spec=pltpu.PrefetchScalarGridSpec(
+            num_scalar_prefetch=1,
+            grid=(cols // block,),
+            in_specs=[into] * 4,
+            out_specs=[out] * (2 if last else 4),
+        ),
+        out_shape=[jax.ShapeDtypeStruct((mo, rows, cols), BF)] * (2 if last else 4),
+        compiler_params=params(16 << 20),
+        cost_estimate=cost(0, 12 * m * rows * cols),
+        name=name,
+    )(odd, ka, ra, kb, rb)
+
+
 class Chain:
-    def __init__(self, parts, nf, nr, extra=None):
-        self.nf, self.nr, self.rows = nf, nr, parts.shape[1]
-        self.extra = 0 if extra is None else extra.shape[1]
-        self.bits = nf.bit_length() - 1
-        a, b = parts[:, : self.rows // 2], parts[:, self.rows // 2 :]
-        if extra is not None:
-            a = jnp.concatenate([a, extra], 1)
-        box = lambda z: z.reshape((2,) * self.bits + z.shape[1:])
-        self.cur = [box(a), box(b)]
-        self.axes = [list(range(self.bits - 1, -1, -1)) for _ in range(2)]
-        self.level = 0
+    def __init__(self, parts, nf, nr, odd):
+        self.nf, self.nr, self.odd = nf, nr, odd
+        self.ka, self.sa, self.kb, self.sb = parts
+        self.level, self.bits = 0, nf.bit_length() - 1
 
     def plane(self):
-        for i in range(2):
-            level = self.level if i == 0 else self.bits - 1 - self.level
-            axes = self.axes[i]
-            ax = axes[level]
-            keep = lax.index_in_dim(self.cur[i], 0, ax, keepdims=False)
-            send = lax.index_in_dim(self.cur[i], 1, ax, keepdims=False)
-            self.cur[i] = add_low(keep, swap(send, "fsdp", self.nf, 1 << level))
-            self.axes[i] = [z - (z > ax) for z in axes]
+        a, b = self.level, self.bits - 1 - self.level
+        ra, rb = swap(self.sa, "fsdp", self.nf, 1 << a), swap(self.sb, "fsdp", self.nf, 1 << b)
         self.level += 1
-        return tuple(self.cur)
+        out = stage(self.odd, self.ka, ra, self.kb, rb, "sum_plane")
+        if self.level == self.bits:
+            self.kept, self.sent = out[0][0], out[1][0]
+        else:
+            self.ka, self.sa, self.kb, self.sb = out
+        return tuple(out)
+
+    def kept_deps(self):
+        return (self.kept,)
 
     def rest(self):
+        out = ()
         while self.level < self.bits:
-            self.plane()
-        return self
-
-    def cur_deps(self):
-        return tuple(self.cur)
+            out = self.plane()
+        return out
 
     def rep_first(self):
-        v = jnp.concatenate([self.cur[1], self.cur[0]], 0)
-        self.odd = (lax.axis_index("rep") & 1) == 1
-        n = v.shape[0] // 2
-        low, high = v[:n], v[n:]
-        self.kept = add_low(jnp.where(self.odd, high, low), swap(jnp.where(self.odd, low, high), "rep", self.nr, 1))
+        self.kept = add_low(self.kept, swap(self.sent, "rep", self.nr, 1))
         return (self.kept,)
 
     def rep_middle(self):
@@ -697,10 +818,8 @@
         return (self.other,)
 
     def result(self):
-        v = jnp.concatenate([jnp.where(self.odd, self.other, self.kept), jnp.where(self.odd, self.kept, self.other)], 0)
-        rows, cut = self.rows, self.rows - self.rows // 2
-        main = jnp.concatenate([v[cut : cut + rows // 2], v[:cut]], 0).astype(F32)
-        return main, v[rows:].astype(F32)
+        odd = self.odd[0] == 1
+        return jnp.concatenate([jnp.where(odd, self.other, self.kept), jnp.where(odd, self.kept, self.other)], 0).astype(F32)
 
 
 def body(tokens, segment_ids, padding, cotangent, w_query, w_key, w_value, w_out, b_query, b_value, b_out,
@@ -709,131 +828,130 @@
     f, c = lax.axis_index("fsdp"), lax.axis_index("seq")
     rel = [((f ^ j) * 2 + (c ^ p)) for j in range(nf) for p in range(2)]
     absolute = [(j * 2 + (c ^ p)) for j in range(nf) for p in range(2)]
-    ids = jnp.stack(rel + absolute).astype(jnp.int32)
+    ids = jnp.stack(rel + absolute + [1 - c, c]).astype(jnp.int32)
     jb = jnp.stack(rel[::2]).astype(jnp.int32)
     jb_abs = jnp.stack(absolute[::2]).astype(jnp.int32)
-    first_core = c == 0
-
-    def both(x):
-        y = swap(x, "seq", ns, 1)
-        own = jnp.where(first_core, jnp.concatenate([x[0], y[0]]), jnp.concatenate([y[1], x[1]]))
-        sib = jnp.where(first_core, jnp.concatenate([x[1], y[1]]), jnp.concatenate([y[0], x[0]]))
-        return own, sib
-
-    def unpair(z):
-        low, high = z[:part_len], z[part_len:]
-        mine, theirs = jnp.where(first_core, low, high), jnp.where(first_core, high, low)
-        got = swap(theirs, "seq", ns, 1)
-        return jnp.stack([jnp.where(first_core, mine, got), jnp.where(first_core, got, mine)])
-
+    core = c.astype(jnp.int32).reshape(1)
+    odd = (lax.axis_index("rep") & 1).astype(jnp.int32).reshape(1)
     sib_of = lambda z: swap(z, "seq", ns, 1)
-
     nb = 2 * nf
     part = width // nb
+
     bias = pack_bias([b_query, b_value, b_out, gain_one, shift_one, b_down, gain_two, shift_two, b_up], width)
-    total = 3 * part + BIAS_ROWS
-    half = total // 2
-    moves = []
-    at = 0
+    moves, at = [], 0
     for src, rows in enumerate((part, part, part, BIAS_ROWS)):
-        for side in range(2):
-            lo, hi = max(at, side * half), min(at + rows, (side + 1) * half)
-            if lo < hi:
-                moves.append((src, lo - at, hi - lo, side, lo - side * half))
+        moves.append((src, 0, rows, 0, at))
         at += rows
-    qkv_halves = split_rows([w_query, w_key, w_value, bias], moves, [(half, width)] * 2, (), "pack_projections")
-    first = gather_start(qkv_halves, nf)
-    x, x_sib = both(tokens)
-    marks, _ = both(jnp.stack([segment_ids, padding], -1))
-    qf, kf = seg_features(marks[:, 0], marks[:, 1])
+    (qkv_shard,) = split_rows([w_query, w_key, w_value, bias], moves, [(at, width)], (), "pack_projections")
+    first = gather_start(qkv_shard, nf)
+    x, x_sib, ct = pair_up(core, [(tokens, sib_of(tokens), 2), (cotangent, sib_of(cotangent), 1)])
+    marks = jnp.stack([segment_ids, padding])
+    theirs = sib_of(marks)
+    own = c == 0
+    mine_m, their_m = jnp.where(own, marks[:, 0], marks[:, 1]), jnp.where(own, theirs[:, 0], theirs[:, 1])
+    whole = jnp.where(own, jnp.concatenate([mine_m, their_m], 1), jnp.concatenate([their_m, mine_m], 1))
+    qf, kf = seg_features(whole[0], whole[1])
     far = gather_far(first, nf)
-    got_qkv = gather_end(qkv_halves, first, far, nf, ns)
-    gate = far if far else tuple(first["all"])
-    h = part // 2
-    up_halves = split_rows(
+    got_qkv = gather_end(qkv_shard, first, far, nf, ns)
+    up_shard, out_shard, down_shard = split_rows(
         [w_up, w_out, w_down],
-        [(0, 0, h, 0, 0), (0, h, h, 1, 0), (1, 0, part, 2, 0), (2, 0, 4 * part, 3, 0)],
-        [(h, 4 * width), (h, 4 * width), (part, width), (4 * part, width)],
-        gate,
-        "split_up",
+        [(0, 0, part, 0, 0), (1, 0, part, 1, 0), (2, 0, 4 * part, 2, 0)],
+        [w_up.shape, w_out.shape, w_down.shape],
+        (x, ct, qf, kf) + tuple(first) + tuple(far),
+        "hold_weights",
     )
-    first_up = gather_start(up_halves[:2], nf)
-    full_out = lax.all_gather(up_halves[2], ("fsdp", "seq"), axis=0, tiled=True)
-    full_down = lax.all_gather(up_halves[3], ("fsdp", "seq"), axis=0, tiled=True)
+    full_out = lax.all_gather(out_shard, ("fsdp", "seq"), axis=0, tiled=True)
+    full_down = lax.all_gather(down_shard, ("fsdp", "seq"), axis=0, tiled=True)
+    first_up = gather_start(up_shard, nf)
     q, k, v, vecs, bup = project(x, got_qkv, ids, nb)
+
     pairs = width // LANES
     groups = 4
     each = pairs // groups
     fwd = [attn_fwd(q, k, v, qf, kf, 0, each)]
-    arrived = tuple(first_up.values()) if nf == 4 else tuple(first_up["all"])
+    fwd.append(attn_fwd(q, k, v, qf, kf, each, each, (fwd[0][0],)))
     far_up = gather_far(first_up, nf)
-    fwd.append(attn_fwd(q, k, v, qf, kf, each, each, (fwd[0][0],) + arrived))
-    got_up = gather_end(up_halves[:2], first_up, far_up, nf, ns)
-    fwd.append(attn_fwd(q, k, v, qf, kf, 2 * each, each, (fwd[1][0],)))
-    fwd.append(attn_fwd(q, k, v, qf, kf, 3 * each, each, (fwd[2][0],) + tuple(far_up)))
-    ct, _ = both(cotangent)
+    got_up = gather_end(up_shard, first_up, far_up, nf, ns)
+    fwd.append(attn_fwd(q, k, v, qf, kf, 2 * each, each, (fwd[1][0],) + tuple(first_up)))
+    fwd.append(attn_fwd(q, k, v, qf, kf, 3 * each, each, (fwd[2][0],)))
+
     a_all, y, yb, normed, inverse, g, gp = up_part(x, vecs, bup, [r[0] for r in fwd], full_out, got_up, ids, nb)
     a_sib, yb_sib, g_sib = sib_of(a_all), sib_of(yb), sib_of(g)
     out, df, dr, sums_two = down_part(g, y, ct, vecs, full_down)
-    output = unpair(out)
     df_sib = sib_of(df)
     dh, sum_up = hidden_part(df, gp, full_down)
     dh_sib = sib_of(dh)
+    out_sib = sib_of(out)
     g_down = grad_down(g, g_sib, df, df_sib, jb_abs, nf, (dh,))
     down_sum = lax.psum_scatter(g_down.reshape(nf * 4 * part, width), "fsdp", scatter_dimension=0, tiled=True)
     final_down = lax.psum(down_sum, "rep").astype(F32)
-    dr1, do, da, sums_one = back_part(dh, dr, normed, inverse, vecs, full_out, got_up, ids, nb, (g_down,))
+    g_up = grad_cols([Job((yb, yb_sib), [(dh[None], dh_sib[None])])], jb, nf, 512, "grad_up", (g_down,))
+    chain_up = Chain(g_up, nf, nr, odd)
+    dr1, do, da, sums_one = back_part(dh, dr, normed, inverse, vecs, full_out, got_up, ids, nb, (g_up[0],))
     do_sib = sib_of(do)
-    (g_up,) = grad_cols(yb, yb_sib, [dh[None]], [dh_sib[None]], jb, nf, 512, "grad_up", deps=(da,), total=5 * width)
-    (g_up,) = grad_cols(a_all, a_sib, [do[None]], [do_sib[None]], jb, nf, 512, "grad_out", into=g_up, at=4 * width, total=5 * width)
-    chain_up = Chain(g_up, nf, nr)
+    output = unpair_up(core, out, out_sib, part_len, (da,))
+    vec_sums = jnp.concatenate([sums_one[2:3], sums_one[0:2], sums_two[2:3], sums_two[0:2], sum_up.reshape(4, width)], 0)
+    vec_sib = sib_of(vec_sums)
 
     def back(i, deps):
         return attn_bwd(q, k, v, da, a_all, fwd[i][1], kf, i * each, each, deps)
 
-    grads = [back(0, (g_up,))]
-    sibs = [sib_of(grads[0])]
-    grads.append(back(1, (grads[0],)))
-    sibs.append(sib_of(grads[1]))
-    grads.append(back(2, (grads[1],) + chain_up.plane()))
-    sibs.append(sib_of(grads[2]))
-    g_one, sum_one = grad_cols(x, x_sib, grads[:2], sibs[:2], jb, nf, each * LANES, "grad_qkv", True, (grads[2],) + chain_up.rest().cur_deps())
-    chain_one = Chain(g_one, nf, nr)
-    grads.append(back(3, (g_one,) + chain_up.rep_first()))
-    sibs.append(sib_of(grads[3]))
-    vec_sums = jnp.concatenate([sums_one[2:3], sums_one[0:2], sums_two[2:3], sums_two[0:2], sum_up.reshape(4, width)], 0)
-    vec_sums = vec_sums + sib_of(vec_sums)
-    deps = chain_one.plane() + chain_up.rep_middle()
-    g_two, sum_two = grad_cols(x, x_sib, grads[2:], sibs[2:], jb, nf, each * LANES, "grad_qkv", True, (grads[3],) + deps)
-
-    sums = jnp.concatenate([sum_one[0].reshape(2, 3, -1), sum_two[0].reshape(2, 3, -1)], 0)
-    bq, bv = sums[:, 0].reshape(-1), sums[:, 2].reshape(-1)
-    eight = jnp.concatenate([bq[None], bv[None], vec_sums[:6]], 0)
-    by_block = jnp.concatenate(
-        [eight.reshape(8, nb, part).transpose(1, 0, 2).reshape(nb, 8 * part), vec_sums[6:].reshape(nb, 4 * part)], 1
+    grads, sums, sibs = [], [], []
+
+    def run(i, deps):
+        d, sm = back(i, deps)
+        grads.append(d)
+        sums.append(sm)
+        sibs.append(sib_of(d))
+
+    run(0, (output,))
+    run(1, (grads[0],) + chain_up.plane())
+    run(2, (grads[1],) + chain_up.rest())
+    g_one = grad_cols(
+        [Job((a_all, a_sib), [(do[None], do_sib[None])]), Job((x, x_sib), [(grads[0], sibs[0]), (grads[1], sibs[1])])],
+        jb, nf, 256, "grad_out_qkv", (grads[2],) + chain_up.rep_first(),
     )
-    cols = g_two.shape[2]
-    lines16 = -(-12 * part // (cols * 16)) * 16
-    mine = jnp.pad(by_block[jb], ((0, 0), (0, lines16 * cols - 12 * part))).reshape(nf, lines16, cols).astype(BF)
-    chain_two = Chain(g_two, nf, nr, mine)
-    input_grad = unpair(input_part(dr1, grads, got_qkv, ids, nb, (g_two,)))
+    chain_one = Chain(g_one, nf, nr, odd)
+    run(3, (grads[2], g_one[0]))
+    chain_up.rep_middle()
+    g_two = grad_cols(
+        [Job((x, x_sib), [(grads[2], sibs[2]), (grads[3], sibs[3])])], jb, nf, 256, "grad_qkv", (grads[3],) + chain_one.plane()
+    )
+    bqv = jnp.concatenate([sm[:2] for sm in sums], 1)
+    bqv = bqv + sib_of(bqv)
+    vec_sums = vec_sums + vec_sib
+    eight = jnp.concatenate([bqv, vec_sums[:6]], 0)
+    small = jnp.concatenate([eight, vec_sums[6:].reshape(8, width // 2)], 1)
+    rows = 16
+    small = jnp.pad(small, ((0, rows - 8), (0, 0))).astype(BF)
+    small = jnp.broadcast_to(small[None], (nf // 2,) + small.shape)
+    g_two = [jnp.concatenate([z, small], 1) for z in g_two]
+    chain_two = Chain(g_two, nf, nr, odd)
+    send_half = input_part(dr1, grads, got_qkv, ids, 0, nb, (g_two[0],) + chain_up.kept_deps())
+    their_half = sib_of(send_half)
+    keep_half = input_part(dr1, grads, got_qkv, ids, 1, nb, (send_half,) + chain_two.plane() + chain_one.rest())
     chain_up.rep_last()
-    chain_one.rest().rep_first()
+    chain_one.rep_first()
     chain_one.rep_middle()
     chain_one.rep_last()
-    chain_two.rest().rep_first()
+    chain_two.rest()
+    chain_two.rep_first()
     chain_two.rep_middle()
     chain_two.rep_last()
-    both_up, _ = chain_up.result()
-    final_up, final_out = both_up[:, : 4 * width], both_up[:, 4 * width :]
-    one, _ = chain_one.result()
-    two, small = chain_two.result()
+    input_grad = unpair_up(core, keep_half, their_half, part_len)
+    final_up = chain_up.result()
+    one = chain_one.result()
+    two = chain_two.result()
+    half = part // 2
+    small = two[half : half + 8]
+    two = jnp.concatenate([two[:half], two[half + rows : 2 * half + rows]], 0)
+    final_out = one[:, :width]
     wide = each * LANES
-    pieces = [z[:, (3 * i + m) * wide : (3 * i + m + 1) * wide] for m in range(3) for z in (one, two) for i in range(2)]
-    final_q, final_k, final_v = (jnp.concatenate(pieces[4 * m : 4 * m + 4], 1) for m in range(3))
-    small = small.reshape(-1)
-    v8 = [small[i * part : (i + 1) * part] for i in range(8)]
-    final_bup = small[8 * part : 12 * part]
+    third = [one[:, width + k * wide : width + (k + 1) * wide] for k in range(6)] + [two[:, k * wide : (k + 1) * wide] for k in range(6)]
+    final_q, final_k, final_v = (jnp.concatenate([third[3 * i + m] for i in range(4)], 1) for m in range(3))
+    own_block = 2 * f + c
+    v8 = lax.dynamic_slice(small[:, :width], (0, own_block * part), (8, part))
+    final_bup = lax.dynamic_slice(small[:, width:].reshape(-1), (own_block * 4 * part,), (4 * part,))
     return (output, input_grad, final_q, final_k, final_v, final_out, v8[0], v8[1], v8[2], v8[3], v8[4],
             final_up, final_bup, final_down, v8[5], v8[6], v8[7])
 

time: 588 us -> 518 us (0.88)
  waiting for transfers between devices: 164 us -> 113 us
  Pallas kernels: 255 us -> 289 us
  other arithmetic: 48.2 us -> 20.6 us
  local copies, waits for them, and re-layouts: 47.8 us -> 29.5 us
  starting transfers between devices: 52.9 us -> 40 us
    ppermute x65 -> x56, waiting for transfers between devices: 163 us -> 112 us  [swap(): return lax.ppermute(x, axis, [(i, i ^ xor) for i in range(size)])]
    pallas_call x4 -> x12, Pallas kernels: 41.3 us -> 66.7 us  [the longest x3 44.1 us: grad_cols(): pl.pallas_call(functools.partial(grad_cols_kernel, spans, nl, nf, block,...]
    ppermute x65 -> x56, starting transfers between devices: 52.8 us -> 39.9 us  [swap(): return lax.ppermute(x, axis, [(i, i ^ xor) for i in range(size)])]
    slice x16 -> x12, local copies, waits for them, and re-layouts: 13.9 us -> 1.25 us  [the longest x2 1.1 us: gather_far(): first[1][half:]]
    another operation x6 -> x4, other arithmetic: 11.5 us -> 1.5 us  [the longest x2 1.48 us: body(): marks = jnp.stack([segment_ids, padding])]
    select_n x12 -> x6, other arithmetic: 12.2 us -> 2.35 us  [the longest x3 2.33 us: result(): jnp.where(odd, self.other, self.kept)]
    convert_element_type x18 -> x6, other arithmetic: 13.3 us -> 3.53 us  [add_low(): return lax.optimization_barrier((a.astype(F32) + b.astype(F32)).astype(BF))]
    squeeze x15 -> x1, local copies, waits for them, and re-layouts: 7.08 us -> 0.54 us  [body(): v8[7]]
  transfers between devices with their start and end apart: 69 -> 60, of which waited for: 24 -> 17; matrix products, arithmetic and copies ran while one was open for 12% -> 5% of each run, Pallas kernels for 42% -> 56%
where the time goes in v2:
time: 518 us; the launch traced here: 508 us
  Pallas kernels  289 us (56%)
  waiting for transfers between devices  113 us (22%)
  starting transfers between devices  40 us (8%)
  local copies, waits for them, and re-layouts  29.5 us (6%)
  other arithmetic  20.6 us (4%)
  between operations  15.4 us (3%)
    ppermute x56, waiting for transfers between devices, swap(): return lax.ppermute(x, axis, [(i, i ^ xor) for i in range(size)])  112 us
    pallas_call x4, Pallas kernels, attn_bwd(): pl.pallas_call(functools.partial(attn_bwd_kernel, qb), grid=(npair,), in_...  51 us
    pallas_call x3, Pallas kernels, grad_cols(): pl.pallas_call(functools.partial(grad_cols_kernel, spans, nl, nf, block,...  44.1 us
    ppermute x56, starting transfers between devices, swap(): return lax.ppermute(x, axis, [(i, i ^ xor) for i in range(size)])  39.9 us
    pallas_call x4, Pallas kernels, attn_fwd(): pl.pallas_call(functools.partial(attn_fwd_kernel, qb), grid=(npair,), in_...  32.5 us
    pallas_call x1, Pallas kernels, up_part(): pl.pallas_call(functools.partial(up_kernel, got, part), grid_spec=pltpu.P...  28.5 us
    unnamed x126, local copies, waits for them, and re-layouts  22.7 us
    pallas_call x1, Pallas kernels, back_part(): pl.pallas_call(functools.partial(back_kernel, up, part), grid_spec=pltpu....  22.1 us
  transfers between devices with their start and end apart: 60, of which 17 were waited for; matrix products, arithmetic and copies ran while one was open for 5% of the time, Pallas kernels for 56%

profile of v2, /device:TPU:0, one launch (start us, length us, event | category | flops | bytes accessed | tf_op | source)
XLA Modules:
  0.0 507.9 jit_solution(3581563592315088131)
XLA Ops:
  22.9 16.0 %collective-permute-done.3.rest_2_.refs_8_.rest_7_ = bf16[416,1024]{1,0:T(8,128)(2,1)S(1)} collective-permute-done((bf16[416,1024]{1,0:T(8,128)(2,1)}, bf16[416,1024]{1,0:T(8,128)(2,1)S(1)}, u32[]{:S(2)}, u32[]{:S(2)}) %collective-permute-start.3) | collective-permute-done | bytes 852000 | tf_op jit(solution)/shard_map/ppermute | solution.py:37
  63.3 13.1 %project.1 = (bf16[1024,1024]{1,0:T(8,128)(2,1)}, bf16[1024,1024]{1,0:T(8,128)(2,1)}, bf16[1024,1024]{1,0:T(8,128)(2,1)}, f32[8,1024]{1,0:T(8,128)}, f32[1,4096]{1,0:T(1,128)}) custom-call(s32[18]{0:T(128)} %stack.92.ids, bf16[1024,1024]{1,0:T(8,128)(2,1)} %get-tuple-element.91.x_ref.refs_3_.refs_9_.refs_10_.refs_11_.refs_12_.refs_1_.refs_2_.refs_4_, ...), custom_call_target="tpu_custom_call" | custom-call | flops 6442450944 | bytes 14680064 | tf_op jit(solution)/shard_map/project/pallas_call | solution.py:251
  76.4 14.7 %collective-permute-done.12.rest_1_.rest_6_ = bf16[128,4096]{1,0:T(8,128)(2,1)S(1)} collective-permute-done((bf16[128,4096]{1,0:T(8,128)(2,1)}, bf16[128,4096]{1,0:T(8,128)(2,1)S(1)}, u32[]{:S(2)}, u32[]{:S(2)}) %collective-permute-start.12) | collective-permute-done | bytes 1048608 | tf_op jit(solution)/shard_map/ppermute | solution.py:37
  115.9 8.1 %attend_forward.6 = (bf16[1024,256]{1,0:T(8,128)(2,1)S(1)}, bf16[1024,256]{1,0:T(8,128)(2,1)S(1)}) custom-call(bf16[1024,1024]{1,0:T(8,128)(2,1)} %get-tuple-element.94.q_ref, bf16[1024,1024]{1,0:T(8,128)(2,1)} %get-tuple-element.95.k_ref, bf16[1024,1024]{1,0:T(8,128)(2,1)} %get-tuple-element.96.v_ref, bf16[1024,128]{1,0:T(8,128)(2,1)S(1)} %copy-done.11, ...), custom_call_target="tpu_custom_call" | custom-call | flops 4294967296 | bytes 2621440 | tf_op jit(solution)/shard_map/attend_forward/pallas_call | solution.py:309
  124.1 8.5 %attend_forward.7 = (bf16[1024,256]{1,0:T(8,128)(2,1)S(1)}, bf16[1024,256]{1,0:T(8,128)(2,1)S(1)}) custom-call(bf16[1024,1024]{1,0:T(8,128)(2,1)} %get-tuple-element.94.q_ref, bf16[1024,1024]{1,0:T(8,128)(2,1)} %get-tuple-element.95.k_ref, bf16[1024,1024]{1,0:T(8,128)(2,1)} %get-tuple-element.96.v_ref, bf16[1024,128]{1,0:T(8,128)(2,1)S(1)} %copy-done.11, ...), custom_call_target="tpu_custom_call" | custom-call | flops 4294967296 | bytes 2621440 | tf_op jit(solution)/shard_map/attend_forward/pallas_call | solution.py:309
  136.6 28.5 %out_norm_up.1 = (bf16[1024,1024]{1,0:T(8,128)(2,1)}, f32[1024,1024]{1,0:T(8,128)}, bf16[1024,1024]{1,0:T(8,128)(2,1)}, bf16[1024,1024]{1,0:T(8,128)(2,1)}, f32[...) custom-call(s32[18]{0:T(128)} %stack.92.ids, ...), custom_call_target="tpu_custom_call" | custom-call | flops 10737418240 | bytes 39845888 | tf_op jit(solution)/shard_map/out_norm_up/pallas_call | solution.py:427
  165.2 19.1 %down_norm.1 = (bf16[1024,1024]{1,0:T(8,128)(2,1)}, bf16[1024,1024]{1,0:T(8,128)(2,1)}, f32[1024,1024]{1,0:T(8,128)}, f32[8,1024]{1,0:T(8,128)}) custom-call(bf16[1024,4096]{1,0:T(8,128)(2,1)} %get-tuple-element.104.g_ref.lo, f32[1024,1024]{1,0:T(8,128)} %get-tuple-element.105.y_ref, bf16[1024,1024]{1,0:T(8,128)(2,1)} %get-tuple-element.99.refs_4_.c_ref, ...), custom_call_target="tpu_custom_call" | custom-call | flops 8589934592 | bytes 31457280 | tf_op jit(solution)/shard_map/down_norm/pallas_call | solution.py:481
  184.4 16.3 %hidden_gradient.1 = (bf16[1024,4096]{1,0:T(8,128)(2,1)}, f32[1,4096]{1,0:T(1,128)}) custom-call(bf16[1024,1024]{1,0:T(8,128)(2,1)} %get-tuple-element.108.df_ref.ro, bf16[1024,4096]{1,0:T(8,128)(2,1)} %get-tuple-element.109.gp_ref, bf16[4096,1024]{1,0:T(8,128)(2,1)} %all-gather.5.cloned.1.call-done.wd), custom_call_target="tpu_custom_call" | custom-call | flops 8589934592 | bytes 27262976 | tf_op jit(solution)/shard_map/hidden_gradient/pallas_call | solution.py:510
  206.8 13.4 %collective-permute-done.25.rs = bf16[1024,1024]{1,0:T(8,128)(2,1)} collective-permute-done((bf16[1024,1024]{1,0:T(8,128)(2,1)}, bf16[1024,1024]{1,0:T(8,128)(2,1)}, u32[]{:S(2)}, u32[]{:S(2)}) %collective-permute-start.25) | collective-permute-done | bytes 2097184 | tf_op jit(solution)/shard_map/ppermute | solution.py:37
  220.2 14.1 %grad_down.1.refs_11_ = bf16[4,512,1024]{2,1,0:T(8,128)(2,1)} custom-call(s32[4]{0:T(128)} %pad_add_fusion.2.jb, bf16[1024,4096]{1,0:T(8,128)(2,1)} %get-tuple-element.104.g_ref.lo, bf16[1024,4096]{1,0:T(8,128)(2,1)} %collective-permute-done.24.ls, bf16[1024,1024]{1,0:T(8,128)(2,1)} %get-tuple-element.108.df_ref.ro, ...), custom_call_target="tpu_custom_call" | custom-call | flops 8589934592 | bytes 16777216 | tf_op jit(solution)/shard_map/grad_down/pallas_call | solution.py:583
  234.4 17.3 %grad_up.1 = (bf16[2,64,4096]{2,1,0:T(8,128)(2,1)}, bf16[2,64,4096]{2,1,0:T(8,128)(2,1)}, bf16[2,64,4096]{2,1,0:T(8,128)(2,1)}, bf16[2,64,4096]{2,1,0:T(8,128)(2,1)}) custom-call(s32[4]{0:T(128)} %pad_add_fusion.1.refs_0_, bf16[1024,1024]{1,0:T(8,128)(2,1)} %get-tuple-element.114.refs_1_.refs_2_.refs_3_.refs_4_, ...), custom_call_target="tpu_custom_call" | custom-call | flops 8589934592 | bytes 18874368 | tf_op jit(solution)/shard_map/grad_up/pallas_call | solution.py:678
  254.6 22.1 %norm_backward.1 = (f32[1024,1024]{1,0:T(8,128)}, bf16[1024,1024]{1,0:T(8,128)(2,1)}, bf16[1024,1024]{1,0:T(8,128)(2,1)}, f32[8,1024]{1,0:T(8,128)}) custom-call(s32[18]{0:T(128)} %stack.92.ids, bf16[1024,4096]{1,0:T(8,128)(2,1)} %get-tuple-element.110.rest_0_.dh_ref, f32[1024,1024]{1,0:T(8,128)} %get-tuple-element.111.dr_ref, ...), custom_call_target="tpu_custom_call" | custom-call | flops 10737418240 | bytes 33554432 | tf_op jit(solution)/shard_map/norm_backward/pallas_call | solution.py:556
  281.2 12.6 %attend_backward.4 = (bf16[3,1024,256]{2,1,0:T(8,128)(2,1)S(1)}, f32[8,256]{1,0:T(8,128)S(1)}) custom-call(bf16[1024,1024]{1,0:T(8,128)(2,1)} %get-tuple-element.94.q_ref, bf16[1024,1024]{1,0:T(8,128)(2,1)} %get-tuple-element.95.k_ref, bf16[1024,1024]{1,0:T(8,128)(2,1)} %get-tuple-element.96.v_ref, bf16[1024,1024]{1,0:T(8,128)(2,1)} %get-tuple-element.116.rest_0_.da_ref, ...), custom_call_target="tpu_custom_call" | custom-call | flops 10737418240 | bytes 4718592 | tf_op jit(solution)/shard_map/attend_backward/pallas_call | solution.py:365
  301.6 13.3 %attend_backward.5 = (bf16[3,1024,256]{2,1,0:T(8,128)(2,1)}, f32[8,256]{1,0:T(8,128)S(1)}) custom-call(bf16[1024,1024]{1,0:T(8,128)(2,1)} %get-tuple-element.94.q_ref, bf16[1024,1024]{1,0:T(8,128)(2,1)} %get-tuple-element.95.k_ref, bf16[1024,1024]{1,0:T(8,128)(2,1)} %get-tuple-element.96.v_ref, bf16[1024,1024]{1,0:T(8,128)(2,1)} %get-tuple-element.116.rest_0_.da_ref, ...), custom_call_target="tpu_custom_call" | custom-call | flops 10737418240 | bytes 4718592 | tf_op jit(solution)/shard_map/attend_backward/pallas_call | solution.py:365
  317.2 12.5 %attend_backward.6 = (bf16[3,1024,256]{2,1,0:T(8,128)(2,1)S(1)}, f32[8,256]{1,0:T(8,128)S(1)}) custom-call(bf16[1024,1024]{1,0:T(8,128)(2,1)} %get-tuple-element.94.q_ref, bf16[1024,1024]{1,0:T(8,128)(2,1)} %get-tuple-element.95.k_ref, bf16[1024,1024]{1,0:T(8,128)(2,1)} %get-tuple-element.96.v_ref, bf16[1024,1024]{1,0:T(8,128)(2,1)} %get-tuple-element.116.rest_0_.da_ref, ...), custom_call_target="tpu_custom_call" | custom-call | flops 10737418240 | bytes 4718592 | tf_op jit(solution)/shard_map/attend_backward/pallas_call | solution.py:365
  336.2 16.3 %grad_out_qkv.1 = (bf16[2,64,2560]{2,1,0:T(8,128)(2,1)}, bf16[2,64,2560]{2,1,0:T(8,128)(2,1)}, bf16[2,64,2560]{2,1,0:T(8,128)(2,1)}, bf16[2,64,2560]{2,1,0:T(8,128)(2,1)}) custom-call(s32[4]{0:T(128)} %pad_add_fusion.1.refs_0_, bf16[1024,1024]{1,0:T(8,128)(2,1)} %get-tuple-element.118.a_ref.refs_1_.refs_2_.refs_3_.refs_4_, ...), custom_call_target="tpu_custom_call" | custom-call | flops 5368709120 | bytes 12582912 | tf_op jit(solution)/shard_map/grad_out_qkv/pallas_call | solution.py:678
  356.2 12.6 %attend_backward.7 = (bf16[3,1024,256]{2,1,0:T(8,128)(2,1)S(1)}, f32[8,256]{1,0:T(8,128)S(1)}) custom-call(bf16[1024,1024]{1,0:T(8,128)(2,1)} %get-tuple-element.94.q_ref, bf16[1024,1024]{1,0:T(8,128)(2,1)} %get-tuple-element.95.k_ref, bf16[1024,1024]{1,0:T(8,128)(2,1)} %get-tuple-element.96.v_ref, bf16[1024,1024]{1,0:T(8,128)(2,1)} %get-tuple-element.116.rest_0_.da_ref, ...), custom_call_target="tpu_custom_call" | custom-call | flops 10737418240 | bytes 4718592 | tf_op jit(solution)/shard_map/attend_backward/pallas_call | solution.py:365
  379.6 8.3 %collective-permute-done.44.ra = bf16[1,64,2560]{2,1,0:T(8,128)(2,1)S(1)} collective-permute-done((bf16[1,64,2560]{2,1,0:T(8,128)(2,1)S(1)}, bf16[1,64,2560]{2,1,0:T(8,128)(2,1)S(1)}, u32[]{:S(2)}, u32[]{:S(2)}) %collective-permute-start.44) | collective-permute-done | bytes 327712 | tf_op jit(solution)/shard_map/ppermute | solution.py:37
  389.9 11.9 %collective-permute-done.55 = bf16[64,4096]{1,0:T(8,128)(2,1)} collective-permute-done((bf16[64,4096]{1,0:T(8,128)(2,1)}, bf16[64,4096]{1,0:T(8,128)(2,1)}, u32[]{:S(2)}, u32[]{:S(2)}) %collective-permute-start.55) | collective-permute-done | bytes 524320 | tf_op jit(solution)/shard_map/ppermute | solution.py:37
  409.5 10.4 %grad_qkv.1 = (bf16[2,64,1536]{2,1,0:T(8,128)(2,1)}, bf16[2,64,1536]{2,1,0:T(8,128)(2,1)}, bf16[2,64,1536]{2,1,0:T(8,128)(2,1)}, bf16[2,64,1536]{2,1,0:T(8,128)(2,1)}) custom-call(s32[4]{0:T(128)} %pad_add_fusion.1.refs_0_, bf16[1024,1024]{1,0:T(8,128)(2,1)} %get-tuple-element.91.x_ref.refs_3_.refs_9_.refs_10_.refs_11_.refs_12_.refs_1_.refs_2_.refs_4_, ...), custom_call_target="tpu_custom_call" | custom-call | flops 3221225472 | bytes 8388608 | tf_op jit(solution)/shard_map/grad_qkv/pallas_call | solution.py:678
  423.1 17.6 %collective-permute-done.48 = bf16[64,2560]{1,0:T(8,128)(2,1)S(1)} collective-permute-done((bf16[64,2560]{1,0:T(8,128)(2,1)S(1)}, bf16[64,2560]{1,0:T(8,128)(2,1)S(1)}, u32[]{:S(2)}, u32[]{:S(2)}) %collective-permute-start.48) | collective-permute-done | bytes 327712 | tf_op jit(solution)/shard_map/ppermute | solution.py:37
  447.5 10.2 %input_gradient.2.rest_15_ = f32[512,1024]{1,0:T(8,128)} custom-call(s32[18]{0:T(128)} %stack.92.ids, f32[1024,1024]{1,0:T(8,128)} %get-tuple-element.117.dr_ref.rest_0_, f32[1024,1024]{1,0:T(8,128)} %get-tuple-element.117.dr_ref.rest_0_, bf16[3,1024,256]{2,1,0:T(8,128)(2,1)} %copy-done.3, bf16[3,1024,256]{2,1,0:T(8,128)(2,1)} %get-tuple-element.129.rest_0_.refs_21_.rest_2_, ...), custom_call_target="tpu_custom_call" | custom-call | flops 3221225472 | bytes 13631488 | tf_op jit(solution)/shard_map/input_gradient/pallas_call | solution.py:721
  469.2 11.5 %collective-permute-done.53 = bf16[80,1536]{1,0:T(8,128)(2,1)S(1)} collective-permute-done((bf16[80,1536]{1,0:T(8,128)(2,1)S(1)}, bf16[80,1536]{1,0:T(8,128)(2,1)S(1)}, u32[]{:S(2)}, u32[]{:S(2)}) %collective-permute-start.53) | collective-permute-done | bytes 245792 | tf_op jit(solution)/shard_map/ppermute | solution.py:37
  480.9 10.3 %input_gradient.3.own = f32[512,1024]{1,0:T(8,128)} custom-call(s32[18]{0:T(128)} %stack.92.ids, f32[1024,1024]{1,0:T(8,128)} %get-tuple-element.117.dr_ref.rest_0_, f32[1024,1024]{1,0:T(8,128)} %get-tuple-element.117.dr_ref.rest_0_, bf16[3,1024,256]{2,1,0:T(8,128)(2,1)} %copy-done.3, bf16[3,1024,256]{2,1,0:T(8,128)(2,1)} %get-tuple-element.129.rest_0_.refs_21_.rest_2_, ...), custom_call_target="tpu_custom_call" | custom-call | flops 3221225472 | bytes 13631488 | tf_op jit(solution)/shard_map/input_gradient/pallas_call | solution.py:721
  (318 shorter events, 153.4 us)
Async XLA Ops:
  7.2 128.4 %all-gather.3.cloned.1.call-start = ((), (), s32[]{:S(2)}) async-start(), calls=%async_computation.1 | async-start | bytes 2359296 | tf_op jit(solution)/shard_map/all_gather | solution.py:863
  7.2 36.2 %collective-permute-start = (bf16[2,512,1024]{2,1,0:T(8,128)(2,1)}, bf16[2,512,1024]{2,1,0:T(8,128)(2,1)}, u32[]{:S(2)}, u32[]{:S(2)}) collective-permute-start(bf16[2,512,1024]{2,1,0:T(8,128)(2,1)} %refs_0_.4), channel_id=1, source_target_pairs={{0,1},{1,0},{2,3},{3,2},{4,5},{5,4},{6,7},{7,6},{8,9},{9,8},{10,11... | collective-permute-start | bytes 6291464 | tf_op jit(solution)/shard_map/ppermute | solution.py:37
  7.8 35.7 %collective-permute-start.1 = (bf16[2,512,1024]{2,1,0:T(8,128)(2,1)}, bf16[2,512,1024]{2,1,0:T(8,128)(2,1)}, u32[]{:S(2)}, u32[]{:S(2)}) collective-permute-start(bf16[2,512,1024]{2,1,0:T(8,128)(2,1)} %refs_2_.4), channel_id=1, source_target_pairs={{0,1},{1,0},{2,3},{3,2},{4,5},{5,4},{6,7},{7,6},{8,9},{9,8},{10,11... | collective-permute-start | bytes 6291464 | tf_op jit(solution)/shard_map/ppermute | solution.py:37
  55.5 109.7 %all-gather.5.cloned.1.call-start = ((), (), s32[]{:S(2)}) async-start(), calls=%async_computation.2 | async-start | bytes 9437184 | tf_op jit(solution)/shard_map/all_gather | solution.py:864
  56.2 315.8 %reduce-scatter.2.cloned.1.call-start = ((), (), s32[]{:S(2)}) async-start(), calls=%async_computation.3 | async-start | bytes 5242880 | tf_op jit(solution)/shard_map/reduce_scatter | solution.py:886
  57.4 33.8 %collective-permute-start.12 = (bf16[128,4096]{1,0:T(8,128)(2,1)}, bf16[128,4096]{1,0:T(8,128)(2,1)S(1)}, u32[]{:S(2)}, u32[]{:S(2)}) collective-permute-start(bf16[128,4096]{1,0:T(8,128)(2,1)} %get-tuple-element.100.rest_5_.rest_0_), channel_id=1, source_target_pairs={{0,2},{2,0},{4,6},{6,4},{1,3},{3,1},{5,7},{7,5},{8,10},{10,8},{12,... | collective-permute-start | bytes 3145736 | tf_op jit(solution)/shard_map/ppermute | solution.py:37
  59.5 34.7 %collective-permute-start.13 = (bf16[128,4096]{1,0:T(8,128)(2,1)}, bf16[128,4096]{1,0:T(8,128)(2,1)}, u32[]{:S(2)}, u32[]{:S(2)}) collective-permute-start(bf16[128,4096]{1,0:T(8,128)(2,1)} %get-tuple-element.100.rest_5_.rest_0_), channel_id=1, source_target_pairs={{0,4},{2,6},{4,0},{6,2},{1,5},{3,7},{5,1},{7,3},{8,12},{10,14},{12... | collective-permute-start | bytes 3145736 | tf_op jit(solution)/shard_map/ppermute | solution.py:37
  63.1 71.1 %collective-permute-start.16 = (bf16[128,4096]{1,0:T(8,128)(2,1)}, bf16[128,4096]{1,0:T(8,128)(2,1)S(1)}, u32[]{:S(2)}, u32[]{:S(2)}) collective-permute-start(bf16[128,4096]{1,0:T(8,128)(2,1)} %get-tuple-element.100.rest_5_.rest_0_), channel_id=1, source_target_pairs={{0,1},{1,0},{2,3},{3,2},{4,5},{5,4},{6,7},{7,6},{8,9},{9,8},{10,11... | collective-permute-start | bytes 3145736 | tf_op jit(solution)/shard_map/ppermute | solution.py:37
  165.1 41.2 %collective-permute-start.24 = (bf16[1024,4096]{1,0:T(8,128)(2,1)}, bf16[1024,4096]{1,0:T(8,128)(2,1)}, u32[]{:S(2)}, u32[]{:S(2)}) collective-permute-start(bf16[1024,4096]{1,0:T(8,128)(2,1)} %get-tuple-element.104.g_ref.lo), channel_id=1, source_target_pairs={{0,1},{1,0},{2,3},{3,2},{4,5},{5,4},{6,7},{7,6},{8,9},{9,8},{10,11... | collective-permute-start | bytes 25165832 | tf_op jit(solution)/shard_map/ppermute | solution.py:37
  200.6 33.8 %collective-permute-start.23 = (bf16[1024,4096]{1,0:T(8,128)(2,1)}, bf16[1024,4096]{1,0:T(8,128)(2,1)}, u32[]{:S(2)}, u32[]{:S(2)}) collective-permute-start(bf16[1024,4096]{1,0:T(8,128)(2,1)} %get-tuple-element.110.rest_0_.dh_ref), channel_id=1, source_target_pairs={{0,1},{1,0},{2,3},{3,2},{4,5},{5,4},{6,7},{7,6},{8,9},{9,8},{10,11... | collective-permute-start | bytes 25165832 | tf_op jit(solution)/shard_map/ppermute | solution.py:37
  201.1 33.2 %collective-permute-start.22 = (bf16[1024,1024]{1,0:T(8,128)(2,1)S(1)}, bf16[1024,1024]{1,0:T(8,128)(2,1)}, u32[]{:S(2)}, u32[]{:S(2)}) collective-permute-start(bf16[1024,1024]{1,0:T(8,128)(2,1)S(1)} %copy-done.46), channel_id=1, source_target_pairs={{0,1},{1,0},{2,3},{3,2},{4,5},{5,4},{6,7},{7,6},{8,9},{9,8},{10,11... | collective-permute-start | bytes 6291464 | tf_op jit(solution)/shard_map/ppermute | solution.py:37
  202.8 129.2 %collective-permute-start.30 = (bf16[1024,1024]{1,0:T(8,128)(2,1)}, bf16[1024,1024]{1,0:T(8,128)(2,1)}, u32[]{:S(2)}, u32[]{:S(2)}) collective-permute-start(bf16[1024,1024]{1,0:T(8,128)(2,1)} %get-tuple-element.118.a_ref.refs_1_.refs_2_.refs_3_.refs_4_), channel_id=1, source_target_pairs={{0,1},{1,0},{2,3},{3,2},{4,5},{5,4},{6,7},{7,6},{8,9},{9,8},{10,11... | collective-permute-start | bytes 6291464 | tf_op jit(solution)/shard_map/ppermute | solution.py:37
  206.3 71.9 %collective-permute-start.21 = (bf16[1024,1024]{1,0:T(8,128)(2,1)}, bf16[1024,1024]{1,0:T(8,128)(2,1)}, u32[]{:S(2)}, u32[]{:S(2)}) collective-permute-start(bf16[1024,1024]{1,0:T(8,128)(2,1)} %get-tuple-element.107.own), channel_id=1, source_target_pairs={{0,1},{1,0},{2,3},{3,2},{4,5},{5,4},{6,7},{7,6},{8,9},{9,8},{10,11... | collective-permute-start | bytes 6291464 | tf_op jit(solution)/shard_map/ppermute | solution.py:37
  234.3 208.2 %all-reduce.3.cloned.1.call-start = ((), (), s32[]{:S(2)}) async-start(), calls=%async_computation.4 | async-start | bytes 2097152 | tf_op jit(solution)/shard_map/psum | solution.py:887
  251.7 42.8 %collective-permute-start.26 = (bf16[2,64,4096]{2,1,0:T(8,128)(2,1)}, bf16[2,64,4096]{2,1,0:T(8,128)(2,1)}, u32[]{:S(2)}, u32[]{:S(2)}) collective-permute-start(bf16[2,64,4096]{2,1,0:T(8,128)(2,1)} %get-tuple-element.122), channel_id=1, source_target_pairs={{0,2},{2,0},{4,6},{6,4},{1,3},{3,1},{5,7},{7,5},{8,10},{10,8},{12,... | collective-permute-start | bytes 3145736 | tf_op jit(solution)/shard_map/ppermute | solution.py:37
  253.1 41.4 %collective-permute-start.27 = (bf16[2,64,4096]{2,1,0:T(8,128)(2,1)}, bf16[2,64,4096]{2,1,0:T(8,128)(2,1)}, u32[]{:S(2)}, u32[]{:S(2)}) collective-permute-start(bf16[2,64,4096]{2,1,0:T(8,128)(2,1)} %get-tuple-element.124), channel_id=1, source_target_pairs={{0,4},{2,6},{4,0},{6,2},{1,5},{3,7},{5,1},{7,3},{8,12},{10,14},{12... | collective-permute-start | bytes 3145736 | tf_op jit(solution)/shard_map/ppermute | solution.py:37
  293.8 41.2 %collective-permute-start.32 = (bf16[3,1024,256]{2,1,0:T(8,128)(2,1)S(1)}, bf16[3,1024,256]{2,1,0:T(8,128)(2,1)}, u32[]{:S(2)}, u32[]{:S(2)}) collective-permute-start(bf16[3,1024,256]{2,1,0:T(8,128)(2,1)S(1)} %get-tuple-element.120.rest_0_.refs_19_.rest_1_), channel_id=1, source_target_pairs={{0,1},{1,0},{2,3},{3,2},{4,5},{5,4},{6,7},{7,6},{8,9},{9,8},{10,11... | collective-permute-start | bytes 4718600 | tf_op jit(solution)/shard_map/ppermute | solution.py:37
  294.0 41.0 %collective-permute-start.31 = (bf16[1024,1024]{1,0:T(8,128)(2,1)}, bf16[1024,1024]{1,0:T(8,128)(2,1)}, u32[]{:S(2)}, u32[]{:S(2)}) collective-permute-start(bf16[1024,1024]{1,0:T(8,128)(2,1)} %get-tuple-element.136), channel_id=1, source_target_pairs={{0,1},{1,0},{2,3},{3,2},{4,5},{5,4},{6,7},{7,6},{8,9},{9,8},{10,11... | collective-permute-start | bytes 6291464 | tf_op jit(solution)/shard_map/ppermute | solution.py:37
  330.8 41.0 %collective-permute-start.40 = (f32[10,1024]{1,0:T(8,128)S(1)}, f32[10,1024]{1,0:T(8,128)S(1)}, u32[]{:S(2)}, u32[]{:S(2)}) collective-permute-start(f32[10,1024]{1,0:T(8,128)S(1)} %concatenate.56), channel_id=1, source_target_pairs={{0,1},{1,0},{2,3},{3,2},{4,5},{5,4},{6,7},{7,6},{8,9},{9,8},{10,11... | collective-permute-start | bytes 122888 | tf_op jit(solution)/shard_map/ppermute | solution.py:37
  332.0 37.0 %collective-permute-start.41 = (bf16[64,4096]{1,0:T(8,128)(2,1)}, bf16[64,4096]{1,0:T(8,128)(2,1)S(1)}, u32[]{:S(2)}, u32[]{:S(2)}) collective-permute-start(bf16[64,4096]{1,0:T(8,128)(2,1)} %fusion.refs_24_), channel_id=1, source_target_pairs={{0,16},{8,24},{16,0},{24,8},{1,17},{9,25},{17,1},{25,9},{2,18},{10... | collective-permute-start | bytes 1572872 | tf_op jit(solution)/shard_map/ppermute | solution.py:37
  371.9 37.6 %collective-permute-start.35 = (bf16[3,1024,256]{2,1,0:T(8,128)(2,1)S(1)}, bf16[3,1024,256]{2,1,0:T(8,128)(2,1)}, u32[]{:S(2)}, u32[]{:S(2)}) collective-permute-start(bf16[3,1024,256]{2,1,0:T(8,128)(2,1)S(1)} %copy-done.1), channel_id=1, source_target_pairs={{0,1},{1,0},{2,3},{3,2},{4,5},{5,4},{6,7},{7,6},{8,9},{9,8},{10,11... | collective-permute-start | bytes 4718600 | tf_op jit(solution)/shard_map/ppermute | solution.py:37
  372.1 37.4 %collective-permute-start.36 = (bf16[3,1024,256]{2,1,0:T(8,128)(2,1)S(1)}, bf16[3,1024,256]{2,1,0:T(8,128)(2,1)}, u32[]{:S(2)}, u32[]{:S(2)}) collective-permute-start(bf16[3,1024,256]{2,1,0:T(8,128)(2,1)S(1)} %get-tuple-element.138.refs_11_.refs_13_.rest_4_), channel_id=1, source_target_pairs={{0,1},{1,0},{2,3},{3,2},{4,5},{5,4},{6,7},{7,6},{8,9},{9,8},{10,11... | collective-permute-start | bytes 4718600 | tf_op jit(solution)/shard_map/ppermute | solution.py:37
  409.4 31.3 %collective-permute-start.48 = (bf16[64,2560]{1,0:T(8,128)(2,1)S(1)}, bf16[64,2560]{1,0:T(8,128)(2,1)S(1)}, u32[]{:S(2)}, u32[]{:S(2)}) collective-permute-start(bf16[64,2560]{1,0:T(8,128)(2,1)S(1)} %fusion.1), channel_id=1, source_target_pairs={{0,16},{8,24},{16,0},{24,8},{1,17},{9,25},{17,1},{25,9},{2,18},{10... | collective-permute-start | bytes 983048 | tf_op jit(solution)/shard_map/ppermute | solution.py:37
  457.8 37.6 %collective-permute-start.46 = (f32[512,1024]{1,0:T(8,128)}, f32[512,1024]{1,0:T(8,128)S(1)}, u32[]{:S(2)}, u32[]{:S(2)}) collective-permute-start(f32[512,1024]{1,0:T(8,128)} %input_gradient.2.rest_15_), channel_id=1, source_target_pairs={{0,1},{1,0},{2,3},{3,2},{4,5},{5,4},{6,7},{7,6},{8,9},{9,8},{10,11... | collective-permute-start | bytes 6291464 | tf_op jit(solution)/shard_map/ppermute | solution.py:37
  (98 other events, 1066.3 us)
Sparse Core Ops, SparseCore 0:
  55.6 36.8 all-gather.2
  94.4 56.9 all-gather.4
  234.5 67.4 reduce-scatter.1
  372.2 70.2 all-reduce.2

commit v3 on v2

--- a/solution.py
+++ b/solution.py
@@ -17,7 +17,9 @@
 NT = (((1,), (1,)), ((), ()))
 TN = (((0,), (0,)), ((), ()))
 NN = (((1,), (0,)), ((), ()))
-VMEM = 58 << 20
+VMEM = 48 << 20
+FULL = 58 << 20
+SHRINK = 1
 ANY = pl.BlockSpec(memory_space=pl.ANY)
 
 
@@ -30,11 +32,15 @@
 
 
 def cost(flops, bytes_accessed, trans=0):
-    return pl.CostEstimate(flops=flops, bytes_accessed=bytes_accessed, transcendentals=trans)
+    return pl.CostEstimate(flops=flops // SHRINK, bytes_accessed=bytes_accessed // SHRINK, transcendentals=trans // SHRINK)
 
 
 def swap(x, axis, size, xor):
     return lax.ppermute(x, axis, [(i, i ^ xor) for i in range(size)])
+
+
+def after(x, *deps):
+    return lax.optimization_barrier((x,) + deps)[0]
 
 
 class Gathered:
@@ -45,11 +51,14 @@
         out = []
         for which, index, base, half, slot in self.entries:
             low = half * self.half
-            for first, rows, dest, stride, offset in targets:
+            for first, rows, dest, stride, offset, *column in targets:
                 a, b = max(first, low), min(first + rows, low + self.half)
                 if a >= b:
                     continue
-                src = refs[which].at[(*index, pl.ds(base + a - low, b - a))]
+                place = (*index, pl.ds(base + a - low, b - a))
+                if column:
+                    place += (pl.ds(column[0], dest.shape[1]),)
+                src = refs[which].at[place]
                 start = pl.multiple_of(ids[slot] * stride + (offset + a - first), 16)
                 out.append(pltpu.make_async_copy(src, dest.at[pl.ds(start, b - a)], sems.at[len(out)]))
         return out
@@ -68,14 +77,16 @@
     return [lax.all_gather(shard, "fsdp", axis=0)]
 
 
-def gather_far(first, nf):
+def gather_far(first, nf, deps=()):
     if nf == 4:
         half = first[0].shape[0] // 2
-        return [swap(first[0][:half], "fsdp", nf, 2), swap(first[1][half:], "fsdp", nf, 1)]
+        shape = (half, first[0].shape[1])
+        one, two = split_rows(first, [(0, 0, half, 0, 0, 0), (1, half, half, 1, 0, 0)], [shape, shape], deps, "cut_halves")
+        return [swap(one, "fsdp", nf, 2), swap(two, "fsdp", nf, 1)]
     return []
 
 
-def gather_end(shard, first, far, nf, ns):
+def gather_end(shard, first, far, nf, ns, late=()):
     half = shard.shape[0] // 2
     if nf == 4:
         arrays = [shard, *first, *far]
@@ -85,9 +96,11 @@
         arrays = list(first)
         entries = [(0, (f,), h * half, h, 2 * nf + 2 * f) for f in range(nf) for h in range(2)]
     n = len(arrays)
-    arrays = arrays + [swap(a, "seq", ns, 1) for a in arrays]
+    swaps = [swap(a, "seq", ns, 1) for a in arrays[: n - len(far)]]
+    swaps += [swap(after(a, *late), "seq", ns, 1) for a in arrays[n - len(far) :]]
+    arrays = arrays + swaps
     entries = entries + [(w + n, i, r, h, s + 1) for w, i, r, h, s in entries]
-    return Gathered(arrays, entries, half)
+    return Gathered(arrays, entries, half), swaps
 
 
 BIAS_ROWS = 32
@@ -96,8 +109,8 @@
 def split_kernel(moves, nin, nout, *refs):
     ins, outs, sems = refs[:nin], refs[len(refs) - nout - 1 : -1], refs[-1]
     copies = [
-        pltpu.make_async_copy(ins[s].at[pl.ds(first, rows)], outs[d].at[pl.ds(to, rows)], sems.at[i])
-        for i, (s, first, rows, d, to) in enumerate(moves)
+        pltpu.make_async_copy(ins[s].at[pl.ds(first, rows)], outs[d].at[pl.ds(to, rows), pl.ds(col, ins[s].shape[1])], sems.at[i])
+        for i, (s, first, rows, d, to, col) in enumerate(moves)
     ]
     for m in copies:
         m.start()
@@ -112,31 +125,44 @@
         out_specs=[pl.BlockSpec(memory_space=pltpu.VMEM)] * len(out_shapes),
         out_shape=[jax.ShapeDtypeStruct(o, BF) for o in out_shapes],
         scratch_shapes=[pltpu.SemaphoreType.DMA((len(moves),))],
-        compiler_params=params(),
+        compiler_params=params(58 << 20),
+        cost_estimate=cost(0, 1 << 20),
         name=name,
     )(*ins, *deps)
 
 
 def bias_kernel(nvec, *refs):
-    vecs, out, tile = refs[:nvec], refs[nvec], refs[nvec + 1]
-    part = vecs[0].shape[-1]
+    vecs, mats, out = refs[:nvec], refs[nvec : nvec + 3], refs[nvec + 3]
+    held, tile, sems = refs[nvec + 4 : 2 * nvec + 4], refs[-2], refs[-1]
+    part = mats[0].shape[0]
+    moves = [pltpu.make_async_copy(m, out.at[pl.ds(i * part, part)], sems.at[i]) for i, m in enumerate(mats)]
+    small = [pltpu.make_async_copy(v, h, sems.at[3 + i]) for i, (v, h) in enumerate(zip(vecs, held))]
+    for m in small + moves:
+        m.start()
     tile[...] = jnp.zeros_like(tile)
+    for m in small:
+        m.wait()
     for i in range(8):
-        tile[0:1, i * part : (i + 1) * part] = vecs[i][...].astype(F32).reshape(1, part)
-    tile[1:2, 0 : 4 * part] = vecs[8][...].astype(F32).reshape(1, 4 * part)
-    out[...] = tile[...].astype(BF)
-
-
-def pack_bias(vecs, width):
-    return pl.pallas_call(
-        functools.partial(bias_kernel, len(vecs)),
-        in_specs=[pl.BlockSpec(memory_space=pltpu.VMEM)] * len(vecs),
+        tile[0:1, i * part : (i + 1) * part] = held[i][...].astype(F32).reshape(1, part)
+    tile[1:2, 0 : 4 * part] = held[8][...].astype(F32).reshape(1, 4 * part)
+    out[3 * part :, :] = tile[...].astype(BF)
+    for m in moves:
+        m.wait()
+
+
+def pack_first(vecs, mats):
+    part, width = mats[0].shape
+    n = len(vecs)
+    return pl.pallas_call(
+        functools.partial(bias_kernel, n),
+        in_specs=[ANY] * (n + 3),
         out_specs=pl.BlockSpec(memory_space=pltpu.VMEM),
-        out_shape=jax.ShapeDtypeStruct((BIAS_ROWS, width), BF),
-        scratch_shapes=[pltpu.VMEM((BIAS_ROWS, width), F32)],
-        compiler_params=params(4 << 20),
-        name="pack_bias",
-    )(*vecs)
+        out_shape=jax.ShapeDtypeStruct((3 * part + BIAS_ROWS, width), BF),
+        scratch_shapes=[pltpu.VMEM(v.shape, BF) for v in vecs] + [pltpu.VMEM((BIAS_ROWS, width), F32), pltpu.SemaphoreType.DMA((n + 3,))],
+        compiler_params=params(58 << 20),
+        cost_estimate=cost(0, 1 << 20),
+        name="pack_first",
+    )(*vecs, *mats)
 
 
 def pair_kernel(count, core, *refs):
@@ -172,7 +198,8 @@
             scratch_shapes=[pltpu.SemaphoreType.DMA((2 * len(shapes),))],
         ),
         out_shape=shapes,
-        compiler_params=params(),
+        compiler_params=params(58 << 20),
+        cost_estimate=cost(0, 1 << 20),
         name="pair_up",
     )(core, *flat, *deps)
 
@@ -203,14 +230,16 @@
             scratch_shapes=[pltpu.SemaphoreType.DMA((2,))],
         ),
         out_shape=jax.ShapeDtypeStruct((2, half, width), own.dtype),
-        compiler_params=params(),
+        compiler_params=params(58 << 20),
+        cost_estimate=cost(0, 1 << 20),
         name="unpair",
     )(core, own, theirs, *deps)
 
 
 def qkv_kernel(got, ids, x_ref, *rest):
     n = len(got.arrays)
-    pieces, (q_ref, k_ref, v_ref, p_ref, b_ref, wq, wk, wv, wb, sems) = rest[:n], rest[-10:]
+    pieces = rest[:n]
+    q_ref, k_ref, v_ref, p_ref, b_ref, wq, wk, wv, wb, sems = rest[-10:]
     width = x_ref.shape[1]
     nb = wb.shape[0] // BIAS_ROWS
     part = width // nb
@@ -235,11 +264,9 @@
     v_ref[...] = (dg(x, wv[...], NN) + p_ref[1:2, :]).astype(BF)
 
 
-def qkv_targets(part, wq, wk, wv, wb):
+def qkv_targets(part, wq, wk, wv, wb=None):
     t = [(0, part, wq, part, 0), (part, part, wk, part, 0), (2 * part, part, wv, part, 0)]
-    if wb is not None:
-        t.append((3 * part, BIAS_ROWS, wb, BIAS_ROWS, 0))
-    return t
+    return t if wb is None else t + [(3 * part, BIAS_ROWS, wb, BIAS_ROWS, 0)]
 
 
 def project(x, got, ids, nb, deps=(), block=256):
@@ -260,7 +287,7 @@
         ),
         out_shape=[jax.ShapeDtypeStruct((n, width), BF)] * 3
         + [jax.ShapeDtypeStruct((8, width), F32), jax.ShapeDtypeStruct((1, 4 * width), F32)],
-        compiler_params=params(),
+        compiler_params=params(FULL),
         cost_estimate=cost(6 * n * width * width, 2 * n * width * 4 + 6 * width * width),
         name="project",
     )(ids, x, *got.arrays, *deps)
@@ -309,11 +336,11 @@
     return pl.pallas_call(functools.partial(attn_fwd_kernel,qb),grid=(npair,),
         in_specs=[blk,blk,blk,whole,whole]+[ANY]*len(deps),out_specs=[out,out],
         out_shape=[jax.ShapeDtypeStruct((n,npair*LANES),BF)]*2,
-        compiler_params=pltpu.CompilerParams(vmem_limit_bytes=50<<20),
-        cost_estimate=pl.CostEstimate(flops=npair*2*2*2*n*n*256,bytes_accessed=npair*n*LANES*2*5,transcendentals=npair*2*n*n),
+        compiler_params=pltpu.CompilerParams(vmem_limit_bytes=VMEM),
+        cost_estimate=cost(npair*2*2*2*n*n*256,npair*n*LANES*2*5),
         name="attend_forward")(q,k,v,qf,kf,*deps)
 def attn_bwd_kernel(qb,q_ref,k_ref,v_ref,da_ref,a_ref,lf_ref,kf_ref,*rest):
-    d_ref,s_ref,dka,dva=rest[-4:]
+    d_ref,dka,dva=rest[-3:]
     n=q_ref.shape[0]
     lane=lax.broadcasted_iota(jnp.int32,(n,LANES),1)
     left=lane<HEAD_DIM
@@ -332,7 +359,6 @@
         sides.append((jnp.where(own,q,lf),jnp.where(own,k,kf),jnp.where(own,v,minus),jnp.where(own,da,df),
                       jnp.where(own,q,zero),jnp.where(own,da,zero)))
     kt=k.T
-    sq=jnp.zeros((1,LANES),F32)
     for c in range(n//qb):
         rows=slice(c*qb,(c+1)*qb)
         dqs=[]; dk=None; dv=None
@@ -346,28 +372,23 @@
             x=dg(pb,daz[rows],NN); dv=x if dv is None else dv+x
             y=dg(ds,qz[rows],NN); dk=y if dk is None else dk+y
             dqs.append(dg(kt[h*64:(h+1)*64],ds,NN))
-        dqb=(jnp.concatenate(dqs,0).T*0.125).astype(BF)
-        d_ref[0,rows,:]=dqb
-        sq=sq+jnp.sum(dqb.astype(F32),0,keepdims=True)
+        d_ref[0,rows,:]=(jnp.concatenate(dqs,0).T*0.125).astype(BF)
         if c==0: dka[...]=dk; dva[...]=dv
         else: dka[...]+=dk; dva[...]+=dv
     d_ref[1]=dka[...].astype(BF)
-    dvb=dva[...].astype(BF)
-    d_ref[2]=dvb
-    s_ref[0:1,:]=sq
-    s_ref[1:2,:]=jnp.sum(dvb.astype(F32),0,keepdims=True)
-def attn_bwd(q,k,v,da,a,lf,kf,first,npair,deps=(),qb=256):
+    d_ref[2]=dva[...].astype(BF)
+def attn_bwd(q,k,v,da,a,lf,kf,first,npair,skip=0,deps=(),qb=256):
     n=q.shape[0]
     blk=pl.BlockSpec((n,LANES),lambda i:(0,i+first))
     whole=pl.BlockSpec((n,LANES),lambda i:(0,0))
-    own=pl.BlockSpec((n,LANES),lambda i:(0,i))
+    own=pl.BlockSpec((n,LANES),lambda i:(0,i+skip))
     out=pl.BlockSpec((3,n,LANES),lambda i:(0,0,i))
     return pl.pallas_call(functools.partial(attn_bwd_kernel,qb),grid=(npair,),
-        in_specs=[blk]*5+[own,whole]+[ANY]*len(deps),out_specs=[out,pl.BlockSpec((8,LANES),lambda i:(0,i))],
-        out_shape=[jax.ShapeDtypeStruct((3,n,npair*LANES),BF),jax.ShapeDtypeStruct((8,npair*LANES),F32)],
+        in_specs=[blk]*5+[own,whole]+[ANY]*len(deps),out_specs=out,
+        out_shape=jax.ShapeDtypeStruct((3,n,npair*LANES),BF),
         scratch_shapes=[pltpu.VMEM((n,LANES),F32)]*2,
-        compiler_params=pltpu.CompilerParams(vmem_limit_bytes=50<<20),
-        cost_estimate=pl.CostEstimate(flops=npair*2*5*2*n*n*256,bytes_accessed=npair*n*LANES*2*9,transcendentals=npair*2*n*n),
+        compiler_params=pltpu.CompilerParams(vmem_limit_bytes=VMEM),
+        cost_estimate=cost(npair*2*5*2*n*n*256,npair*n*LANES*2*9),
         name="attend_backward")(q,k,v,da,a,lf,kf,*deps)
 def seg_features(seg,pad):
     n=seg.shape[0]
@@ -380,16 +401,19 @@
 
 def up_kernel(got, part, ids, x_ref, p_ref, bup_ref, *rest):
     n = len(got.arrays)
-    *a_refs, wo = rest[: len(rest) - n - 9]
-    pieces = rest[len(rest) - n - 9 : len(rest) - 9]
-    a_all, y_ref, yb_ref, n_ref, s_ref, g_ref, gp_ref, wu, sems = rest[-9:]
+    a_refs = rest[: len(rest) - n - 11]
+    pieces = rest[len(rest) - n - 11 : len(rest) - 11]
+    a_all, y_ref, yb_ref, n_ref, s_ref, g_ref, gp_ref, wu, wo, sems, sems_out = rest[-11:]
     width = x_ref.shape[1]
-    targets = [(0, part, wu, part, 0)]
+    targets = [(0, part, wu, part, 0, 0)]
 
     @pl.when(pl.program_id(0) == 0)
     def _():
-        for m in got.copies(pieces, ids, targets, sems):
+        moves = got.copies(pieces, ids, [(0, part, wo, part, 0, 4 * width)], sems_out)
+        for m in moves + got.copies(pieces, ids, targets, sems):
             m.start()
+        for m in moves:
+            m.wait()
 
     a = jnp.concatenate([r[...] for r in a_refs], 1)
     a_all[...] = a
@@ -417,7 +441,7 @@
         gp_ref[:, k : k + step] = (phi + h * (jnp.exp(-0.5 * h * h) * INV_ROOT_TAU)).astype(BF)
 
 
-def up_part(x, vecs, bup, a_parts, w_out, got, ids, nb, block=256):
+def up_part(x, vecs, bup, a_parts, got, ids, nb, block=256):
     n, width = x.shape
     part = width // nb
     rows = lambda w: pl.BlockSpec((block, w), lambda i, ids: (i, 0))
@@ -431,10 +455,9 @@
             grid=(n // block,),
             in_specs=[rows(width), whole((8, width)), whole((1, 4 * width))]
             + [rows(a.shape[1]) for a in a_parts]
-            + [whole((width, width))]
             + [ANY] * len(got.arrays),
             out_specs=[rows(width), rows(width), rows(width), rows(width), rows(1), rows(4 * width), rows(4 * width)],
-            scratch_shapes=[pltpu.VMEM((width, 4 * width), BF), pltpu.SemaphoreType.DMA((count,))],
+            scratch_shapes=[pltpu.VMEM((width, 4 * width), BF), pltpu.VMEM((width, width), BF)] + [pltpu.SemaphoreType.DMA((count,))] * 2,
         ),
         out_shape=[
             sds((n, width), BF),
@@ -445,10 +468,10 @@
             sds((n, 4 * width), BF),
             sds((n, 4 * width), BF),
         ],
-        compiler_params=params(),
+        compiler_params=params(FULL),
         cost_estimate=cost(10 * n * width * width, 28 * n * width + 10 * width * width, 8 * n * width),
         name="out_norm_up",
-    )(ids, x, vecs, bup, *a_parts, w_out, *got.arrays)
+    )(ids, x, vecs, bup, *a_parts, *got.arrays)
 
 
 def down_kernel(g_ref, y_ref, c_ref, p_ref, wd, o_ref, df_ref, dr_ref, sum_ref):
@@ -484,57 +507,63 @@
         in_specs=[rows(4 * width), rows(width), rows(width), whole((8, width)), whole((4 * width, width))],
         out_specs=[rows(width), rows(width), rows(width), whole((8, width))],
         out_shape=[sds((n, width), BF), sds((n, width), BF), sds((n, width), F32), sds((8, width), F32)],
-        compiler_params=params(),
+        compiler_params=params(FULL),
         cost_estimate=cost(8 * n * width * width, 22 * n * width + 8 * width * width),
         name="down_norm",
     )(g, y, ct, vecs, w_down)
 
 
-def hidden_kernel(df_ref, gp_ref, wd, dh_ref, bup_ref):
+def hidden_kernel(df_ref, gp_ref, wd, *rest):
+    dh_ref, bup_ref = rest[-2:]
+
     @pl.when(pl.program_id(0) == 0)
     def _():
         bup_ref[...] = jnp.zeros_like(bup_ref)
 
     df = df_ref[...]
+    width = df.shape[1]
     step = 512
     for k in range(0, dh_ref.shape[1], step):
         dh = (dg(df, wd[k : k + step, :], NT) * gp_ref[:, k : k + step].astype(F32)).astype(BF)
         dh_ref[:, k : k + step] = dh
-        bup_ref[:, k : k + step] += jnp.sum(dh.astype(F32), 0, keepdims=True)
-
-
-def hidden_part(df, gp, w_down, block=256):
+        row, col = k // width, k % width
+        bup_ref[row : row + 1, col : col + step] += jnp.sum(dh.astype(F32), 0, keepdims=True)
+
+
+def hidden_part(df, gp, w_down, which, deps=(), block=256):
     n, width = df.shape
-    rows = lambda w: pl.BlockSpec((block, w), lambda i: (i, 0))
-    whole = lambda shape: pl.BlockSpec(shape, lambda i: (0, 0))
+    cols = w_down.shape[0] // 2
+    rows = pl.BlockSpec((block, width), lambda i: (i, 0))
     return pl.pallas_call(
         hidden_kernel,
         grid=(n // block,),
-        in_specs=[rows(width), rows(4 * width), whole((4 * width, width))],
-        out_specs=[rows(4 * width), whole((1, 4 * width))],
-        out_shape=[jax.ShapeDtypeStruct((n, 4 * width), BF), jax.ShapeDtypeStruct((1, 4 * width), F32)],
-        compiler_params=params(),
-        cost_estimate=cost(8 * n * width * width, 18 * n * width + 8 * width * width),
+        in_specs=[rows, pl.BlockSpec((block, cols), lambda i: (i, which)), pl.BlockSpec((cols, width), lambda i: (which, 0))]
+        + [ANY] * len(deps),
+        out_specs=[pl.BlockSpec((block, cols), lambda i: (i, 0)), pl.BlockSpec((8, width), lambda i: (0, 0))],
+        out_shape=[jax.ShapeDtypeStruct((n, cols), BF), jax.ShapeDtypeStruct((8, width), F32)],
+        compiler_params=params(FULL),
+        cost_estimate=cost(2 * n * width * cols, n * (2 * width + 4 * cols) + 2 * width * cols),
         name="hidden_gradient",
-    )(df, gp, w_down)
-
-
-def back_kernel(up, part, ids, dh_ref, dr_ref, n_ref, s_ref, p_ref, wo, *rest):
+    )(df, gp, w_down, *deps)
+
+
+def back_kernel(up, part, ids, dh_ref, dh2_ref, dr_ref, n_ref, s_ref, p_ref, *rest):
     nu = len(up.arrays)
     pu = rest[:nu]
-    dr1_ref, do_ref, da_ref, sum_ref, wu, su = rest[-6:]
-    tu = [(0, part, wu, part, 0)]
+    dr1_ref, do_ref, da_ref, sum_ref, wu, wo, su, so = rest[-8:]
+    width = dr_ref.shape[1]
 
     @pl.when(pl.program_id(0) == 0)
     def _():
-        moves = up.copies(pu, ids, tu, su)
+        moves = up.copies(pu, ids, [(0, part, wu, part, 0, 0)], su) + up.copies(pu, ids, [(0, part, wo, part, 0, 4 * width)], so)
         for m in moves:
             m.start()
         sum_ref[...] = jnp.zeros_like(sum_ref)
         for m in moves:
             m.wait()
 
-    dy = dr_ref[...] + dg(dh_ref[...], wu[...], NT)
+    cut = dh_ref.shape[1]
+    dy = dr_ref[...] + dg(dh_ref[...], wu[:, :cut], NT) + dg(dh2_ref[...], wu[:, cut:], NT)
     normed = n_ref[...].astype(F32)
     e = dy * p_ref[3:4, :]
     dr = s_ref[...] * (e - jnp.mean(e, -1, keepdims=True) - normed * jnp.mean(e * normed, -1, keepdims=True))
@@ -547,7 +576,7 @@
     sum_ref[2:3, :] += jnp.sum(do.astype(F32), 0, keepdims=True)
 
 
-def back_part(dh, dr, normed, inverse, vecs, w_out, up, ids, nb, deps=(), block=256):
+def back_part(dh, dr, normed, inverse, vecs, up, ids, nb, deps=(), block=256):
     n, width = dr.shape
     part = width // nb
     rows = lambda w: pl.BlockSpec((block, w), lambda i, ids: (i, 0))
@@ -558,38 +587,86 @@
         grid_spec=pltpu.PrefetchScalarGridSpec(
             num_scalar_prefetch=1,
             grid=(n // block,),
-            in_specs=[rows(4 * width), rows(width), rows(width), rows(1), whole((8, width)), whole((width, width))]
+            in_specs=[rows(2 * width), rows(2 * width), rows(width), rows(width), rows(1), whole((8, width))]
             + [ANY] * (len(up.arrays) + len(deps)),
             out_specs=[rows(width), rows(width), rows(width), whole((8, width))],
-            scratch_shapes=[pltpu.VMEM((width, 4 * width), BF), pltpu.SemaphoreType.DMA((up.count([(0, part, 0, 0, 0)]),))],
+            scratch_shapes=[pltpu.VMEM((width, 4 * width), BF), pltpu.VMEM((width, width), BF)]
+            + [pltpu.SemaphoreType.DMA((up.count([(0, part, 0, 0, 0)]),))] * 2,
         ),
         out_shape=[sds((n, width), F32), sds((n, width), BF), sds((n, width), BF), sds((8, width), F32)],
-        compiler_params=params(),
+        compiler_params=params(FULL),
         cost_estimate=cost(10 * n * width * width, 22 * n * width + 10 * width * width),
         name="norm_backward",
-    )(ids, dh, dr, normed, inverse, vecs, w_out, *up.arrays, *deps)
-
-
-def grad_rows_kernel(jb, lo, ls, ro, rs, *rest):
-    rest[-1][0] = (dg(lo[...], ro[...], TN) + dg(ls[...], rs[...], TN)).astype(BF)
+    )(ids, *dh, dr, normed, inverse, vecs, *up.arrays, *deps)
+
+
+def sums_kernel(one, two, up0, up1, *rest):
+    out = rest[-1]
+    out[...] = jnp.zeros_like(out)
+    for r, (src, at) in enumerate(((one, 2), (one, 0), (one, 1), (two, 2), (two, 0), (two, 1))):
+        out[1 + r : 2 + r, :] = src[at : at + 1, :]
+    for r, (src, at) in enumerate(((up0, 0), (up0, 1), (up1, 0), (up1, 1))):
+        out[7 + r : 8 + r, :] = src[at : at + 1, :]
+
+
+def pack_sums(one, two, up0, up1):
+    return pl.pallas_call(
+        sums_kernel,
+        in_specs=[pl.BlockSpec(memory_space=pltpu.VMEM)] * 4,
+        out_specs=pl.BlockSpec(memory_space=pltpu.VMEM),
+        out_shape=jax.ShapeDtypeStruct((16, one.shape[1]), F32),
+        compiler_params=params(4 << 20),
+        cost_estimate=cost(0, 1 << 20),
+        name="pack_sums",
+    )(one, two, up0, up1)
+
+
+def grad_rows_kernel(top, jb, lo, ls, ro, rs, *rest):
+    ka, sa, kb, sb = rest[-4:]
+    j = pl.program_id(0)
+    half = ka.shape[1]
+    got = (dg(lo[...], ro[...], TN) + dg(ls[...], rs[...], TN)).astype(BF)
+
+    @pl.when(j % 2 == 0)
+    def _():
+        ka[0] = got[:half]
+
+    @pl.when(j % 2 == 1)
+    def _():
+        sa[0] = got[:half]
+
+    @pl.when(j < top)
+    def _():
+        kb[0] = got[half:]
+
+    @pl.when(j >= top)
+    def _():
+        sb[0] = got[half:]
 
 
 def grad_down(g_own, g_sib, df_own, df_sib, jb, nf, deps=()):
     n, hidden = g_own.shape
     width = df_own.shape[1]
     part = hidden // (2 * nf)
+    top = nf // 2
     left = pl.BlockSpec((n, part), lambda j, jb: (0, jb[j]))
     right = pl.BlockSpec((n, width), lambda j, jb: (0, 0))
-    return pl.pallas_call(
-        grad_rows_kernel,
+    out = lambda at: pl.BlockSpec((1, part // 2, width), lambda j, jb: (at(j), 0, 0))
+    return pl.pallas_call(
+        functools.partial(grad_rows_kernel, top),
         grid_spec=pltpu.PrefetchScalarGridSpec(
             num_scalar_prefetch=1,
             grid=(nf,),
             in_specs=[left, left, right, right] + [ANY] * len(deps),
-            out_specs=pl.BlockSpec((1, part, width), lambda j, jb: (j, 0, 0)),
+            out_specs=[
+                out(lambda j: j // 2),
+                out(lambda j: j // 2),
+                out(lambda j: jnp.minimum(j, top - 1)),
+                out(lambda j: jnp.maximum(j - top, 0)),
+            ],
         ),
-        out_shape=jax.ShapeDtypeStruct((nf, part, width), BF),
-        compiler_params=params(),
+        out_shape=[jax.ShapeDtypeStruct((top, part // 2, width), BF)] * 4,
+        compiler_params=params(FULL),
         cost_estimate=cost(2 * n * hidden * width, 2 * n * hidden + 4 * n * width + hidden * width),
         name="grad_down",
     )(jb, g_own, g_sib, df_own, df_sib, *deps)
@@ -600,7 +677,10 @@
         self.left, self.rights = left, rights
 
 
-def grad_cols_kernel(jobs, nl, nf, block, keeps, *refs):
+EXTRA = 16
+
+
+def grad_cols_kernel(jobs, nl, nf, block, keeps, extra, sum_blocks, *refs):
     pos = 1
     step = pl.program_id(0)
     lefts, rights = [], []
@@ -611,6 +691,8 @@
         for _ in spans:
             rights.append((refs[pos], refs[pos + 1]))
             pos += 2
+    if sum_blocks:
+        vec_own, vec_sib = refs[pos : pos + 2]
     outs = refs[len(refs) - len(jobs) - 4 : len(refs) - len(jobs)]
     lts = refs[len(refs) - len(jobs) :]
     n, wide = lefts[0][0][0].shape
@@ -636,9 +718,18 @@
                 for out, (which, side) in zip(outs, keeps):
                     for m, j in enumerate(which):
                         out[m, 0:half, :] = got[j * part + side * half : j * part + (side + 1) * half]
-
-
-def grad_cols(jobs, jb, nf, block, name, deps=()):
+                if extra:
+                    tile = jnp.zeros((EXTRA, block), F32)
+                    if sum_blocks:
+                        tile = jnp.where(step < sum_blocks, vec_own[...] + vec_sib[...], 0.0)
+                    columns = jnp.sum(both.astype(F32), 0, keepdims=True)
+                    tile = jnp.where(lax.broadcasted_iota(jnp.int32, (EXTRA, block), 0) == 0, columns, tile).astype(BF)
+                    for out in outs:
+                        for m in range(out.shape[0]):
+                            out[m, half : half + EXTRA, :] = tile
+
+
+def grad_cols(jobs, jb, nf, block, name, deps=(), extra=False, vecs=None):
     n, width = jobs[0].left[0].shape
     part = width // (2 * nf)
     spans, step = [], 0
@@ -670,13 +761,19 @@
             step += count
         spans.append(mine)
     half = part // 2
+    sum_blocks = 0
+    if vecs is not None:
+        sum_blocks = vecs[0].shape[1] // block
+        right_specs += [pl.BlockSpec((EXTRA, block), lambda i, jb: (0, jnp.minimum(i, sum_blocks - 1)))] * 2
+        right_ops += list(vecs)
     js = list(range(nf))
     top = nf // 2
     keeps = [([j for j in js if not j & 1], 0), ([j for j in js if j & 1], 0), ([j for j in js if j < top], 1), ([j for j in js if j >= top], 1)]
-    out_spec = pl.BlockSpec((nf // 2, half, block), lambda i, jb: (0, 0, i))
-    out_shape = jax.ShapeDtypeStruct((nf // 2, half, step * block), BF)
-    return pl.pallas_call(
-        functools.partial(grad_cols_kernel, spans, nl, nf, block, keeps),
+    lines = half + (EXTRA if extra else 0)
+    out_spec = pl.BlockSpec((nf // 2, lines, block), lambda i, jb: (0, 0, i))
+    out_shape = jax.ShapeDtypeStruct((nf // 2, lines, step * block), BF)
+    return pl.pallas_call(
+        functools.partial(grad_cols_kernel, spans, nl, nf, block, keeps, extra, sum_blocks),
         grid_spec=pltpu.PrefetchScalarGridSpec(
             num_scalar_prefetch=1,
             grid=(step,),
@@ -695,7 +792,7 @@
     n = len(got.arrays)
     d_refs, pieces = rest[1 : 1 + groups], rest[1 + groups : 1 + groups + n]
     out_ref, wq, wk, wv, sems = rest[-5:]
-    targets = qkv_targets(part, wq, wk, wv, None)
+    targets = qkv_targets(part, wq, wk, wv)
 
     @pl.when(pl.program_id(0) == 0)
     def _():
@@ -717,7 +814,7 @@
     steps = n // 2 // block
     rows = pl.BlockSpec((block, width), lambda i, ids: (i + ids[ids.shape[0] - 2 + place] * steps, 0))
     three = lambda w: pl.BlockSpec((3, block, w), lambda i, ids: (0, i + ids[ids.shape[0] - 2 + place] * steps, 0))
-    count = got.count(qkv_targets(width // nb, 0, 0, 0, None))
+    count = got.count(qkv_targets(width // nb, 0, 0, 0))
     return pl.pallas_call(
         functools.partial(input_kernel, got, width // nb, len(grads), place),
         grid_spec=pltpu.PrefetchScalarGridSpec(
@@ -728,19 +825,26 @@
             scratch_shapes=[pltpu.VMEM((width, width), BF)] * 3 + [pltpu.SemaphoreType.DMA((count,))],
         ),
         out_shape=jax.ShapeDtypeStruct((n // 2, width), F32),
-        compiler_params=params(),
+        compiler_params=params(FULL),
         cost_estimate=cost(3 * n * width * width, 7 * n * width + 6 * width * width),
         name="input_gradient",
     )(ids, dr, dr, *grads, *got.arrays, *deps)
 
 
 def add_low(a, b):
-    return lax.optimization_barrier((a.astype(F32) + b.astype(F32)).astype(BF))
-
-
-def stage_kernel(last, odd, ka, ra, kb, rb, *outs):
-    add = lambda a, b: (a[...].astype(F32) + b[...].astype(F32)).astype(BF)
-    a, b = add(ka, ra), add(kb, rb)
+    return (a[...].astype(F32) + b[...].astype(F32)).astype(BF)
+
+
+SMALL = 16 << 20
+
+
+def tile_of(cols):
+    return cols // 2 if cols % (2 * LANES) == 0 else cols
+
+
+def stage_kernel(last, odd, ka, ra, kb, rb, *rest):
+    outs = rest[len(rest) - (2 if last else 4) :]
+    a, b = add_low(ka, ra), add_low(kb, rb)
     m = a.shape[0]
     if last:
         swapped = odd[0] == 1
@@ -752,11 +856,9 @@
             outs[2][i], outs[3][i] = b[i], b[m // 2 + i]
 
 
-def stage(odd, ka, ra, kb, rb, name, block=512):
+def stage(odd, ka, ra, kb, rb, deps):
     m, rows, cols = ka.shape
-    block = min(block, cols)
-    while cols % block:
-        block //= 2
+    block = tile_of(cols)
     last = m == 1
     into = pl.BlockSpec((m, rows, block), lambda i, odd: (0, 0, i))
     mo = max(m // 2, 1)
@@ -766,60 +868,183 @@
         grid_spec=pltpu.PrefetchScalarGridSpec(
             num_scalar_prefetch=1,
             grid=(cols // block,),
-            in_specs=[into] * 4,
+            in_specs=[into] * 4 + [ANY] * len(deps),
             out_specs=[out] * (2 if last else 4),
         ),
         out_shape=[jax.ShapeDtypeStruct((mo, rows, cols), BF)] * (2 if last else 4),
-        compiler_params=params(16 << 20),
+        compiler_params=params(9 << 20),
         cost_estimate=cost(0, 12 * m * rows * cols),
-        name=name,
-    )(odd, ka, ra, kb, rb)
-
-
-class Chain:
+        name="sum_plane",
+    )(odd, ka, ra, kb, rb, *deps)
+
+
+def pair_sum_kernel(a, b, *rest):
+    rest[-1][...] = add_low(a, b)
+
+
+def pair_sum(a, b, deps):
+    rows, cols = a.shape
+    block = tile_of(cols)
+    spec = pl.BlockSpec((rows, block), lambda i: (0, i))
+    return pl.pallas_call(
+        pair_sum_kernel,
+        grid=(cols // block,),
+        in_specs=[spec] * 2 + [ANY] * len(deps),
+        out_specs=spec,
+        out_shape=jax.ShapeDtypeStruct((rows, cols), BF),
+        compiler_params=params(4 << 20),
+        cost_estimate=cost(0, 6 * rows * cols),
+        name="sum_rep",
+    )(a, b, *deps)
+
+
+def pick_kernel(odd, a, b, *rest):
+    rest[-2][...], rest[-1][...] = a[...], b[...]
+
+
+def pick(odd, v, deps=()):
+    rows, cols = v.shape
+    block = tile_of(cols)
+    spec = lambda flip: pl.BlockSpec((rows // 2, block), lambda i, odd: ((odd[0] + flip) % 2, i))
+    out = pl.BlockSpec((rows // 2, block), lambda i, odd: (0, i))
+    return pl.pallas_call(
+        pick_kernel,
+        grid_spec=pltpu.PrefetchScalarGridSpec(
+            num_scalar_prefetch=1, grid=(cols // block,), in_specs=[spec(0), spec(1)] + [ANY] * len(deps), out_specs=[out, out]
+        ),
+        out_shape=[jax.ShapeDtypeStruct((rows // 2, cols), BF)] * 2,
+        compiler_params=params(4 << 20),
+        cost_estimate=cost(0, 4 * rows * cols),
+        name="pick_half",
+    )(odd, v, v, *deps)
+
+
+class RepChain:
+    def __init__(self, kept, sent, nr, odd):
+        self.kept, self.sent, self.nr, self.odd = kept, sent, nr, odd
+
+    def rep_first(self, deps=()):
+        self.kept = pair_sum(self.kept, swap(self.sent, "rep", self.nr, 1), deps)
+        return (self.kept,)
+
+    def rep_middle(self, deps=()):
+        xor = 2
+        while xor < self.nr:
+            self.kept = pair_sum(self.kept, swap(self.kept, "rep", self.nr, xor), deps)
+            xor *= 2
+        return (self.kept,)
+
+    def rep_middle_part(self, which, deps=()):
+        if self.nr != 4:
+            return self.rep_middle(deps) if which == 1 else ()
+        rows = self.kept.shape[0] // 2
+        part = self.kept[:rows] if which == 0 else self.kept[rows:]
+        part = pair_sum(part, swap(part, "rep", self.nr, 2), deps)
+        if which == 0:
+            self.first_part = part
+        else:
+            self.kept = jnp.concatenate([self.first_part, part], 0)
+        return (part,)
+
+    def rep_last(self):
+        self.other = swap(self.kept, "rep", self.nr, 1)
+        return (self.other,)
+
+    def halves(self):
+        odd = self.odd[0] == 1
+        return jnp.where(odd, self.other, self.kept).astype(F32), jnp.where(odd, self.kept, self.other).astype(F32)
+
+    def result(self):
+        return jnp.concatenate(self.halves(), 0)
+
+
+class Chain(RepChain):
     def __init__(self, parts, nf, nr, odd):
         self.nf, self.nr, self.odd = nf, nr, odd
         self.ka, self.sa, self.kb, self.sb = parts
         self.level, self.bits = 0, nf.bit_length() - 1
 
-    def plane(self):
+    def plane(self, deps=()):
         a, b = self.level, self.bits - 1 - self.level
         ra, rb = swap(self.sa, "fsdp", self.nf, 1 << a), swap(self.sb, "fsdp", self.nf, 1 << b)
         self.level += 1
-        out = stage(self.odd, self.ka, ra, self.kb, rb, "sum_plane")
+        out = stage(self.odd, self.ka, ra, self.kb, rb, deps)
         if self.level == self.bits:
             self.kept, self.sent = out[0][0], out[1][0]
         else:
             self.ka, self.sa, self.kb, self.sb = out
         return tuple(out)
 
-    def kept_deps(self):
-        return (self.kept,)
-
-    def rest(self):
+    def rest(self, deps=()):
         out = ()
         while self.level < self.bits:
-            out = self.plane()
+            out = self.plane(deps)
         return out
 
-    def rep_first(self):
-        self.kept = add_low(self.kept, swap(self.sent, "rep", self.nr, 1))
-        return (self.kept,)
-
-    def rep_middle(self):
-        xor = 2
-        while xor < self.nr:
-            self.kept = add_low(self.kept, swap(self.kept, "rep", self.nr, xor))
-            xor *= 2
-        return (self.kept,)
-
-    def rep_last(self):
-        self.other = swap(self.kept, "rep", self.nr, 1)
-        return (self.other,)
-
-    def result(self):
-        odd = self.odd[0] == 1
-        return jnp.concatenate([jnp.where(odd, self.other, self.kept), jnp.where(odd, self.kept, self.other)], 0).astype(F32)
+
+def join_kernel(odd, kept, other, *rest):
+    out = rest[-1]
+    rows = kept.shape[0]
+    swapped = odd[0] == 1
+    out[:rows, :] = jnp.where(swapped, other[...], kept[...]).astype(F32)
+    out[rows:, :] = jnp.where(swapped, kept[...], other[...]).astype(F32)
+
+
+def join(chain, deps=()):
+    rows, cols = chain.kept.shape
+    block = cols // 2
+    spec = pl.BlockSpec((rows, block), lambda i, odd: (0, i))
+    return pl.pallas_call(
+        join_kernel,
+        grid_spec=pltpu.PrefetchScalarGridSpec(
+            num_scalar_prefetch=1,
+            grid=(2,),
+            in_specs=[spec] * 2 + [ANY] * len(deps),
+            out_specs=pl.BlockSpec((2 * rows, block), lambda i, odd: (0, i)),
+        ),
+        out_shape=jax.ShapeDtypeStruct((2 * rows, cols), F32),
+        compiler_params=params(8 << 20),
+        cost_estimate=cost(0, 12 * rows * cols),
+        name="join_halves",
+    )(chain.odd, chain.kept, chain.other, *deps)
+
+
+def finish_kernel(half, width, wide, counts, odd, *refs):
+    n = len(counts)
+    q, k, v, o, small, line = refs[2 * n :]
+    for at in range(2):
+        rows = slice(at * half, (at + 1) * half)
+        group, lines = 0, []
+        for i, count in enumerate(counts):
+            both = jnp.where(odd[0] == at, refs[2 * i][...], refs[2 * i + 1][...]).astype(F32)
+            col = 0
+            if i == 0:
+                o[rows, :] = both[:half, :width]
+                if at == 0:
+                    small[...] = both[half : half + EXTRA, :width]
+                col = width
+            lines.append(both[half : half + 8, col:])
+            for _ in range(count):
+                for out in (q, k, v):
+                    out[rows, group * wide : (group + 1) * wide] = both[:half, col : col + wide]
+                    col += wide
+                group += 1
+        if at == 0:
+            line[...] = jnp.concatenate(lines, 1)
+
+
+def finish(odd, chains, counts, half, width, wide):
+    spec = pl.BlockSpec(memory_space=pltpu.VMEM)
+    sds = jax.ShapeDtypeStruct
+    return pl.pallas_call(
+        functools.partial(finish_kernel, half, width, wide, counts),
+        in_specs=[pl.BlockSpec(memory_space=pltpu.SMEM)] + [spec] * (2 * len(chains)),
+        out_specs=[spec] * 6,
+        out_shape=[sds((2 * half, width), F32)] * 4 + [sds((EXTRA, width), F32), sds((8, 3 * wide * sum(counts)), F32)],
+        compiler_params=params(12 << 20),
+        cost_estimate=cost(0, 6 << 20),
+        name="finish",
+    )(odd, *[z for c in chains for z in (c.kept, c.other)])
 
 
 def body(tokens, segment_ids, padding, cotangent, w_query, w_key, w_value, w_out, b_query, b_value, b_out,
@@ -837,12 +1062,9 @@
     nb = 2 * nf
     part = width // nb
 
-    bias = pack_bias([b_query, b_value, b_out, gain_one, shift_one, b_down, gain_two, shift_two, b_up], width)
-    moves, at = [], 0
-    for src, rows in enumerate((part, part, part, BIAS_ROWS)):
-        moves.append((src, 0, rows, 0, at))
-        at += rows
-    (qkv_shard,) = split_rows([w_query, w_key, w_value, bias], moves, [(at, width)], (), "pack_projections")
+    qkv_shard = pack_first(
+        [b_query, b_value, b_out, gain_one, shift_one, b_down, gain_two, shift_two, b_up], [w_query, w_key, w_value]
+    )
     first = gather_start(qkv_shard, nf)
     x, x_sib, ct = pair_up(core, [(tokens, sib_of(tokens), 2), (cotangent, sib_of(cotangent), 1)])
     marks = jnp.stack([segment_ids, padding])
@@ -851,18 +1073,13 @@
     mine_m, their_m = jnp.where(own, marks[:, 0], marks[:, 1]), jnp.where(own, theirs[:, 0], theirs[:, 1])
     whole = jnp.where(own, jnp.concatenate([mine_m, their_m], 1), jnp.concatenate([their_m, mine_m], 1))
     qf, kf = seg_features(whole[0], whole[1])
-    far = gather_far(first, nf)
-    got_qkv = gather_end(qkv_shard, first, far, nf, ns)
-    up_shard, out_shard, down_shard = split_rows(
-        [w_up, w_out, w_down],
-        [(0, 0, part, 0, 0), (1, 0, part, 1, 0), (2, 0, 4 * part, 2, 0)],
-        [w_up.shape, w_out.shape, w_down.shape],
-        (x, ct, qf, kf) + tuple(first) + tuple(far),
-        "hold_weights",
+    (up_shard,) = split_rows(
+        [w_up, w_out], [(0, 0, part, 0, 0, 0), (1, 0, part, 0, 0, 4 * width)], [(part, 5 * width)], (), "pack_up"
     )
-    full_out = lax.all_gather(out_shard, ("fsdp", "seq"), axis=0, tiled=True)
-    full_down = lax.all_gather(down_shard, ("fsdp", "seq"), axis=0, tiled=True)
-    first_up = gather_start(up_shard, nf)
+    far = gather_far(first, nf, (x, qf, up_shard))
+    gate = tuple(far) or tuple(first)
+    got_qkv, _ = gather_end(qkv_shard, first, far, nf, ns)
+    first_up = gather_start(after(up_shard, *gate), nf)
     q, k, v, vecs, bup = project(x, got_qkv, ids, nb)
 
     pairs = width // LANES
@@ -870,88 +1087,95 @@
     each = pairs // groups
     fwd = [attn_fwd(q, k, v, qf, kf, 0, each)]
     fwd.append(attn_fwd(q, k, v, qf, kf, each, each, (fwd[0][0],)))
-    far_up = gather_far(first_up, nf)
-    got_up = gather_end(up_shard, first_up, far_up, nf, ns)
-    fwd.append(attn_fwd(q, k, v, qf, kf, 2 * each, each, (fwd[1][0],) + tuple(first_up)))
-    fwd.append(attn_fwd(q, k, v, qf, kf, 3 * each, each, (fwd[2][0],)))
-
-    a_all, y, yb, normed, inverse, g, gp = up_part(x, vecs, bup, [r[0] for r in fwd], full_out, got_up, ids, nb)
+    far_up = gather_far(first_up, nf, (fwd[1][0],))
+    full_down = lax.all_gather(after(w_down, fwd[1][0], *first_up), ("fsdp", "seq"), axis=0, tiled=True)
+    fwd.append(attn_fwd(q, k, v, qf, kf, 2 * each, 2 * each, (fwd[1][0],) + tuple(first_up)))
+    got_up, swaps = gather_end(up_shard, first_up, far_up, nf, ns, (fwd[2][0],))
+    lf = [(fwd[0][1], 0), (fwd[1][1], 0), (fwd[2][1], 0), (fwd[2][1], each)]
+
+    a_all, y, yb, normed, inverse, g, gp = up_part(x, vecs, bup, [r[0] for r in fwd], got_up, ids, nb)
     a_sib, yb_sib, g_sib = sib_of(a_all), sib_of(yb), sib_of(g)
     out, df, dr, sums_two = down_part(g, y, ct, vecs, full_down)
-    df_sib = sib_of(df)
-    dh, sum_up = hidden_part(df, gp, full_down)
-    dh_sib = sib_of(dh)
-    out_sib = sib_of(out)
-    g_down = grad_down(g, g_sib, df, df_sib, jb_abs, nf, (dh,))
-    down_sum = lax.psum_scatter(g_down.reshape(nf * 4 * part, width), "fsdp", scatter_dimension=0, tiled=True)
-    final_down = lax.psum(down_sum, "rep").astype(F32)
-    g_up = grad_cols([Job((yb, yb_sib), [(dh[None], dh_sib[None])])], jb, nf, 512, "grad_up", (g_down,))
+    df_sib = sib_of(after(df, yb_sib, a_sib))
+    dh0, sum_up0 = hidden_part(df, gp, full_down, 0, (yb_sib, a_sib))
+    dh0_sib = sib_of(after(dh0, df_sib, g_sib))
+    dh1, sum_up1 = hidden_part(df, gp, full_down, 1, (dh0, df_sib, g_sib))
+    dh1_sib = sib_of(after(dh1, dh0_sib))
+    g_down = grad_down(g, g_sib, df, df_sib, jb, nf, (dh1, dh0_sib))
+    chain_down = Chain(after(g_down, dh1_sib), nf, nr, odd)
+    g_up = grad_cols([Job((yb, yb_sib), [(dh0[None], dh0_sib[None]), (dh1[None], dh1_sib[None])])], jb, nf, 512, "grad_up", (g_down[0],))
+    now = chain_down.plane((g_up[0],))
+    g_up = after(g_up, *now)
+    out_sib = sib_of(after(out, *now))
     chain_up = Chain(g_up, nf, nr, odd)
-    dr1, do, da, sums_one = back_part(dh, dr, normed, inverse, vecs, full_out, got_up, ids, nb, (g_up[0],))
-    do_sib = sib_of(do)
-    output = unpair_up(core, out, out_sib, part_len, (da,))
-    vec_sums = jnp.concatenate([sums_one[2:3], sums_one[0:2], sums_two[2:3], sums_two[0:2], sum_up.reshape(4, width)], 0)
-    vec_sib = sib_of(vec_sums)
-
-    def back(i, deps):
-        return attn_bwd(q, k, v, da, a_all, fwd[i][1], kf, i * each, each, deps)
-
-    grads, sums, sibs = [], [], []
+    dr1, do, da, sums_one = back_part((dh0, dh1), dr, normed, inverse, vecs, got_up, ids, nb, now + (g_up[0],))
+    now = chain_up.plane((da,)) + chain_down.rest((da,))
+    do_sib = sib_of(after(do, *now))
+    sums = pack_sums(*after((sums_one, sums_two, sum_up0, sum_up1), *now))
+
+    grads, sibs = [], []
 
     def run(i, deps):
-        d, sm = back(i, deps)
-        grads.append(d)
-        sums.append(sm)
-        sibs.append(sib_of(d))
-
-    run(0, (output,))
-    run(1, (grads[0],) + chain_up.plane())
-    run(2, (grads[1],) + chain_up.rest())
+        grads.append(attn_bwd(q, k, v, da, a_all, lf[i][0], kf, i * each, each, lf[i][1], deps))
+        return (grads[-1],)
+
+    def send(i, deps):
+        sibs.append(sib_of(after(grads[i], *deps)))
+
+    dep = run(0, (da,) + now)
+    now = chain_up.rest(dep) + chain_down.rep_first(dep)
+    send(0, now)
+    output = unpair_up(core, *after((out, out_sib), *now), part_len)
+    sums_sib = sib_of(after(sums, *now))
+    dep = run(1, dep + now + (output, do_sib, sums_sib, sibs[0]))
+    now = chain_up.rep_first(dep) + chain_down.rep_middle(dep)
+    chain_down.rep_last()
+    send(1, now)
     g_one = grad_cols(
-        [Job((a_all, a_sib), [(do[None], do_sib[None])]), Job((x, x_sib), [(grads[0], sibs[0]), (grads[1], sibs[1])])],
-        jb, nf, 256, "grad_out_qkv", (grads[2],) + chain_up.rep_first(),
+        [Job((a_all, a_sib), [(do[None], do_sib[None])]), Job((x, x_sib), [(grads[0], sibs[0])])],
+        jb, nf, 256, "grad_out_qkv", dep + now, True, (sums, sums_sib),
     )
-    chain_one = Chain(g_one, nf, nr, odd)
-    run(3, (grads[2], g_one[0]))
-    chain_up.rep_middle()
-    g_two = grad_cols(
-        [Job((x, x_sib), [(grads[2], sibs[2]), (grads[3], sibs[3])])], jb, nf, 256, "grad_qkv", (grads[3],) + chain_one.plane()
-    )
-    bqv = jnp.concatenate([sm[:2] for sm in sums], 1)
-    bqv = bqv + sib_of(bqv)
-    vec_sums = vec_sums + vec_sib
-    eight = jnp.concatenate([bqv, vec_sums[:6]], 0)
-    small = jnp.concatenate([eight, vec_sums[6:].reshape(8, width // 2)], 1)
-    rows = 16
-    small = jnp.pad(small, ((0, rows - 8), (0, 0))).astype(BF)
-    small = jnp.broadcast_to(small[None], (nf // 2,) + small.shape)
-    g_two = [jnp.concatenate([z, small], 1) for z in g_two]
-    chain_two = Chain(g_two, nf, nr, odd)
-    send_half = input_part(dr1, grads, got_qkv, ids, 0, nb, (g_two[0],) + chain_up.kept_deps())
-    their_half = sib_of(send_half)
-    keep_half = input_part(dr1, grads, got_qkv, ids, 1, nb, (send_half,) + chain_two.plane() + chain_one.rest())
+    dep = (g_one[0],)
+    now = chain_up.rep_middle_part(0, dep)
+    chain_one = Chain(after(g_one, *now), nf, nr, odd)
+    dep = run(2, dep + now + (sibs[1],))
+    final_down = join(chain_down, dep)
+    now = chain_one.plane(dep) + chain_up.rep_middle_part(1, dep) + (final_down,)
+    send(2, now)
     chain_up.rep_last()
-    chain_one.rep_first()
-    chain_one.rep_middle()
+    g_two = grad_cols([Job((x, x_sib), [(grads[i], sibs[i]) for i in (1, 2)])], jb, nf, 256, "grad_qkv", dep + now, True)
+    dep = (g_two[0],)
+    now = chain_one.rest(dep)
+    chain_two = Chain(after(g_two, *now), nf, nr, odd)
+    dep = run(3, dep + now)
+    final_up = join(chain_up, dep)
+    now = chain_two.plane(dep) + chain_one.rep_first(dep) + (final_up,)
+    send(3, now)
+    g_three = grad_cols([Job((x, x_sib), [(grads[3], sibs[3])])], jb, nf, 256, "grad_qkv", dep + now, True)
+    dep = (g_three[0],)
+    now = chain_two.rest(dep)
+    chain_three = Chain(after(g_three, *now), nf, nr, odd)
+    send_half = input_part(dr1, grads, got_qkv, ids, 0, nb, dep + now)
+    dep = (send_half,)
+    now = chain_three.plane(dep) + chain_one.rep_middle(dep) + chain_two.rep_first(dep)
     chain_one.rep_last()
-    chain_two.rest()
-    chain_two.rep_first()
-    chain_two.rep_middle()
+    their_half = sib_of(after(send_half, *now))
+    keep_half = input_part(dr1, grads, got_qkv, ids, 1, nb, dep + now)
+    dep = (keep_half,)
+    now = chain_three.rest(dep) + chain_two.rep_middle(dep)
     chain_two.rep_last()
-    input_grad = unpair_up(core, keep_half, their_half, part_len)
-    final_up = chain_up.result()
-    one = chain_one.result()
-    two = chain_two.result()
+    input_grad = unpair_up(core, *after((keep_half, their_half), *now), part_len)
+    chain_three.rep_first()
+    chain_three.rep_middle((input_grad,))
+    chain_three.rep_last()
     half = part // 2
-    small = two[half : half + 8]
-    two = jnp.concatenate([two[:half], two[half + rows : 2 * half + rows]], 0)
-    final_out = one[:, :width]
     wide = each * LANES
-    third = [one[:, width + k * wide : width + (k + 1) * wide] for k in range(6)] + [two[:, k * wide : (k + 1) * wide] for k in range(6)]
-    final_q, final_k, final_v = (jnp.concatenate([third[3 * i + m] for i in range(4)], 1) for m in range(3))
+    final_q, final_k, final_v, final_out, small, line = finish(odd, (chain_one, chain_two, chain_three), (1, 2, 1), half, width, wide)
+    line = line[0].reshape(groups, 3, wide)
+    vectors = jnp.concatenate([line[:, 0].reshape(1, width), line[:, 2].reshape(1, width), small[1:7]], 0)
     own_block = 2 * f + c
-    v8 = lax.dynamic_slice(small[:, :width], (0, own_block * part), (8, part))
-    final_bup = lax.dynamic_slice(small[:, width:].reshape(-1), (own_block * 4 * part,), (4 * part,))
+    v8 = lax.dynamic_slice(vectors, (0, own_block * part), (8, part))
+    final_bup = lax.dynamic_slice(small[7:11].reshape(-1), (own_block * 4 * part,), (4 * part,))
     return (output, input_grad, final_q, final_k, final_v, final_out, v8[0], v8[1], v8[2], v8[3], v8[4],
             final_up, final_bup, final_down, v8[5], v8[6], v8[7])
 

time: 518 us -> 490 us (0.946)
  waiting for transfers between devices: 113 us -> 63.4 us
  starting transfers between devices: 40 us -> 62.1 us
  other arithmetic: 20.6 us -> 3.55 us
  Pallas kernels: 289 us -> 302 us
    ppermute x56 -> x71, waiting for transfers between devices: 112 us -> 63.3 us  [swap(): return lax.ppermute(x, axis, [(i, i ^ xor) for i in range(size)])]
    ppermute x56 -> x71, starting transfers between devices: 39.9 us -> 62.1 us  [swap(): return lax.ppermute(x, axis, [(i, i ^ xor) for i in range(size)])]
    pallas_call x3 -> x19, Pallas kernels: 30.4 us -> 46 us  [the longest x2 19.6 us: hidden_part(): pl.pallas_call(hidden_kernel, grid=(n // block,), in_specs=[rows, pl.Bloc...]
    unnamed x126 -> x151, local copies, waits for them, and re-layouts: 22.7 us -> 32.5 us
    convert_element_type x10 -> x0, other arithmetic: 8.79 us -> none  [the longest x6 3.53 us: add_low(): return lax.optimization_barrier((a.astype(F32) + b.astype(F32)).astype(BF))]
    pallas_call x3 -> x4, Pallas kernels: 44.1 us -> 42.5 us  [grad_cols(): pl.pallas_call(functools.partial(grad_cols_kernel, spans, nl, nf, block,...]
    pallas_call x4 -> x3, Pallas kernels: 32.5 us -> 31.4 us  [attn_fwd(): pl.pallas_call(functools.partial(attn_fwd_kernel, qb), grid=(npair,), in_...]
  transfers between devices with their start and end apart: 60 -> 72, of which waited for: 17 -> 16; matrix products, arithmetic and copies ran while one was open for 5% -> 1% of each run, Pallas kernels for 56% -> 62%
where the time goes in v3:
time: 490 us; the launch traced here: 481 us
  Pallas kernels  302 us (62%)
  waiting for transfers between devices  63.4 us (13%)
  starting transfers between devices  62.1 us (13%)
  local copies, waits for them, and re-layouts  34.5 us (7%)
  between operations  15.5 us (3%)
    ppermute x71, waiting for transfers between devices, swap(): return lax.ppermute(x, axis, [(i, i ^ xor) for i in range(size)])  63.3 us
    ppermute x71, starting transfers between devices, swap(): return lax.ppermute(x, axis, [(i, i ^ xor) for i in range(size)])  62.1 us
    pallas_call x4, Pallas kernels, attn_bwd(): pl.pallas_call(functools.partial(attn_bwd_kernel, qb), grid=(npair,), in_...  51.1 us
    pallas_call x4, Pallas kernels, grad_cols(): pl.pallas_call(functools.partial(grad_cols_kernel, spans, nl, nf, block,...  42.5 us
    unnamed x151, local copies, waits for them, and re-layouts  32.5 us
    pallas_call x3, Pallas kernels, attn_fwd(): pl.pallas_call(functools.partial(attn_fwd_kernel, qb), grid=(npair,), in_...  31.4 us
    pallas_call x1, Pallas kernels, up_part(): pl.pallas_call(functools.partial(up_kernel, got, part), grid_spec=pltpu.P...  29.5 us
    pallas_call x1, Pallas kernels, back_part(): pl.pallas_call(functools.partial(back_kernel, up, part), grid_spec=pltpu....  22.2 us
  transfers between devices with their start and end apart: 72, of which 16 were waited for; matrix products, arithmetic and copies ran while one was open for 1% of the time, Pallas kernels for 62%

profile of v3, /device:TPU:0, one launch (start us, length us, event | category | flops | bytes accessed | tf_op | source)
XLA Modules:
  0.0 480.6 jit_solution(15351056040473724507)
XLA Ops:
  20.2 12.3 %collective-permute-done.2.refs_0_.rest_1_.rest_6_ = bf16[416,1024]{1,0:T(8,128)(2,1)S(1)} collective-permute-done((bf16[416,1024]{1,0:T(8,128)(2,1)}, bf16[416,1024]{1,0:T(8,128)(2,1)S(1)}, u32[]{:S(2)}, u32[]{:S(2)}) %collective-permute-start.2) | collective-permute-done | bytes 852000 | tf_op jit(solution)/shard_map/ppermute | solution.py:39
  32.6 5.9 %pair_up.1 = (bf16[1024,1024]{1,0:T(8,128)(2,1)}, bf16[1024,1024]{1,0:T(8,128)(2,1)}, bf16[1024,1024]{1,0:T(8,128)(2,1)}) custom-call(s32[1]{0:T(128)} %bitcast.core, bf16[2,512,1024]{2,1,0:T(8,128)(2,1)} %refs_0_.3, bf16[2,512,1024]{2,1,0:T(8,128)(2,1)} %collective-permute-done.refs_1_, bf16[2,512,1024]{2,1,0:T(8,128)(2,1)} %refs_2_.2, ...), custom_call_target="tpu_custom_call" | custom-call | bytes 1048576 | tf_op jit(solution)/shard_map/pair_up/pallas_call | solution.py:191
  43.8 9.0 %collective-permute-done.5.rest_3_.rest_8_ = bf16[208,1024]{1,0:T(8,128)(2,1)} collective-permute-done((bf16[208,1024]{1,0:T(8,128)(2,1)}, bf16[208,1024]{1,0:T(8,128)(2,1)}, u32[]{:S(2)}, u32[]{:S(2)}) %collective-permute-start.5) | collective-permute-done | bytes 426016 | tf_op jit(solution)/shard_map/ppermute | solution.py:39
  57.6 13.1 %project.1 = (bf16[1024,1024]{1,0:T(8,128)(2,1)}, bf16[1024,1024]{1,0:T(8,128)(2,1)}, bf16[1024,1024]{1,0:T(8,128)(2,1)}, f32[8,1024]{1,0:T(8,128)}, f32[1,4096]{1,0:T(1,128)}) custom-call(s32[18]{0:T(128)} %stack.85.ids, bf16[1024,1024]{1,0:T(8,128)(2,1)} %get-tuple-element.153.refs_2_.x_ref.refs_9_.refs_10_.refs_11_.refs_12_.refs_1_.refs_3_.refs_4_, ...), custom_call_target="tpu_custom_call" | custom-call | flops 6442450944 | bytes 14680064 | tf_op jit(solution)/shard_map/project/pallas_call | solution.py:278
  73.9 7.9 %attend_forward.3 = (bf16[1024,256]{1,0:T(8,128)(2,1)S(1)}, bf16[1024,256]{1,0:T(8,128)(2,1)S(1)}) custom-call(bf16[1024,1024]{1,0:T(8,128)(2,1)S(1)} %copy-done.49, bf16[1024,1024]{1,0:T(8,128)(2,1)S(1)} %copy-done.51, bf16[1024,1024]{1,0:T(8,128)(2,1)} %get-tuple-element.160.v_ref, bf16[1024,128]{1,0:T(8,128)(2,1)S(1)} %copy-done.24, ...), custom_call_target="tpu_custom_call" | custom-call | flops 4294967296 | bytes 2621440 | tf_op jit(solution)/shard_map/attend_forward/pallas_call | solution.py:336
  81.8 8.2 %attend_forward.4 = (bf16[1024,256]{1,0:T(8,128)(2,1)S(1)}, bf16[1024,256]{1,0:T(8,128)(2,1)S(1)}) custom-call(bf16[1024,1024]{1,0:T(8,128)(2,1)S(1)} %copy-done.49, bf16[1024,1024]{1,0:T(8,128)(2,1)} %get-tuple-element.159.k_ref, bf16[1024,1024]{1,0:T(8,128)(2,1)} %get-tuple-element.160.v_ref, bf16[1024,128]{1,0:T(8,128)(2,1)S(1)} %copy-done.24, ...), custom_call_target="tpu_custom_call" | custom-call | flops 4294967296 | bytes 2621440 | tf_op jit(solution)/shard_map/attend_forward/pallas_call | solution.py:336
  101.1 15.3 %attend_forward.5 = (bf16[1024,512]{1,0:T(8,128)(2,1)S(1)}, bf16[1024,512]{1,0:T(8,128)(2,1)S(1)}) custom-call(bf16[1024,1024]{1,0:T(8,128)(2,1)} %get-tuple-element.158.q_ref, bf16[1024,1024]{1,0:T(8,128)(2,1)} %get-tuple-element.159.k_ref, bf16[1024,1024]{1,0:T(8,128)(2,1)} %get-tuple-element.160.v_ref, bf16[1024,128]{1,0:T(8,128)(2,1)S(1)} %copy-done.24, ...), custom_call_target="tpu_custom_call" | custom-call | flops 8589934592 | bytes 5242880 | tf_op jit(solution)/shard_map/attend_forward/pallas_call | solution.py:336
  127.8 29.5 %out_norm_up.1 = (bf16[1024,1024]{1,0:T(8,128)(2,1)}, f32[1024,1024]{1,0:T(8,128)}, bf16[1024,1024]{1,0:T(8,128)(2,1)}, bf16[1024,1024]{1,0:T(8,128)(2,1)}, f32[...) custom-call(s32[18]{0:T(128)} %stack.85.ids, ...), custom_call_target="tpu_custom_call" | custom-call | flops 10737418240 | bytes 39845888 | tf_op jit(solution)/shard_map/out_norm_up/pallas_call | solution.py:451
  158.2 19.0 %down_norm.1 = (bf16[1024,1024]{1,0:T(8,128)(2,1)}, bf16[1024,1024]{1,0:T(8,128)(2,1)}, f32[1024,1024]{1,0:T(8,128)}, f32[8,1024]{1,0:T(8,128)}) custom-call(bf16[1024,4096]{1,0:T(8,128)(2,1)} %get-tuple-element.169.g_ref.lo, f32[1024,1024]{1,0:T(8,128)} %get-tuple-element.170.y_ref, bf16[1024,1024]{1,0:T(8,128)(2,1)} %get-tuple-element.171.c_ref, ...), custom_call_target="tpu_custom_call" | custom-call | flops 8589934592 | bytes 31457280 | tf_op jit(solution)/shard_map/down_norm/pallas_call | solution.py:504
  178.5 9.9 %hidden_gradient.2 = (bf16[1024,2048]{1,0:T(8,128)(2,1)}, f32[8,1024]{1,0:T(8,128)}) custom-call(bf16[1024,1024]{1,0:T(8,128)(2,1)} %get-tuple-element.177.df_ref.ro, bf16[1024,4096]{1,0:T(8,128)(2,1)} %get-tuple-element.178.gp_ref, bf16[4096,1024]{1,0:T(8,128)(2,1)} %all-gather.2.cloned.1.call-done.wd, ...), custom_call_target="tpu_custom_call" | custom-call | flops 4294967296 | bytes 14680064 | tf_op jit(solution)/shard_map/hidden_gradient/pallas_call | solution.py:537
  190.0 9.7 %hidden_gradient.3 = (bf16[1024,2048]{1,0:T(8,128)(2,1)}, f32[8,1024]{1,0:T(8,128)}) custom-call(bf16[1024,1024]{1,0:T(8,128)(2,1)} %get-tuple-element.177.df_ref.ro, bf16[1024,4096]{1,0:T(8,128)(2,1)} %get-tuple-element.178.gp_ref, bf16[4096,1024]{1,0:T(8,128)(2,1)} %all-gather.2.cloned.1.call-done.wd, ...), custom_call_target="tpu_custom_call" | custom-call | flops 4294967296 | bytes 14680064 | tf_op jit(solution)/shard_map/hidden_gradient/pallas_call | solution.py:537
  201.8 15.2 %grad_down.1 = (bf16[2,256,1024]{2,1,0:T(8,128)(2,1)}, bf16[2,256,1024]{2,1,0:T(8,128)(2,1)}, bf16[2,256,1024]{2,1,0:T(8,128)(2,1)}, bf16[2,256,1024]{2,1,0:T(8,128)(2,1)}) custom-call(s32[4]{0:T(128)} %pad_add_fusion.1.jb.refs_0_, bf16[1024,4096]{1,0:T(8,128)(2,1)} %get-tuple-element.169.g_ref.lo, bf16[1024,4096]{1,0:T(8,128)(2,1)} %collective-permute-done.21.rest_2_.ls, ...), custom_call_target="tpu_custom_call" | custom-call | flops 8589934592 | bytes 16777216 | tf_op jit(solution)/shard_map/grad_down/pallas_call | solution.py:655
  220.5 16.6 %grad_up.1 = (bf16[2,64,4096]{2,1,0:T(8,128)(2,1)S(1)}, bf16[2,64,4096]{2,1,0:T(8,128)(2,1)}, bf16[2,64,4096]{2,1,0:T(8,128)(2,1)S(1)}, bf16[2,64,4096]{2,1,0:T(8,128)(2,1)}) custom-call(s32[4]{0:T(128)S(1)} %copy-done.47, bf16[1024,1024]{1,0:T(8,128)(2,1)} %get-tuple-element.175.refs_1_.refs_2_.refs_3_.refs_4_, ...), custom_call_target="tpu_custom_call" | custom-call | flops 8589934592 | bytes 18874368 | tf_op jit(solution)/shard_map/grad_up/pallas_call | solution.py:775
  237.1 5.5 %collective-permute-done.27.ra = bf16[2,256,1024]{2,1,0:T(8,128)(2,1)S(1)} collective-permute-done((bf16[2,256,1024]{2,1,0:T(8,128)(2,1)}, bf16[2,256,1024]{2,1,0:T(8,128)(2,1)S(1)}, u32[]{:S(2)}, u32[]{:S(2)}) %collective-permute-start.27) | collective-permute-done | bytes 1048608 | tf_op jit(solution)/shard_map/ppermute | solution.py:39
  250.5 22.2 %norm_backward.1 = (f32[1024,1024]{1,0:T(8,128)}, bf16[1024,1024]{1,0:T(8,128)(2,1)}, bf16[1024,1024]{1,0:T(8,128)(2,1)}, f32[8,1024]{1,0:T(8,128)}) custom-call(s32[18]{0:T(128)} %stack.85.ids, bf16[1024,2048]{1,0:T(8,128)(2,1)} %get-tuple-element.181.rest_0_.dh_ref, bf16[1024,2048]{1,0:T(8,128)(2,1)} %get-tuple-element.186.rest_0_.dh2_ref, ...), custom_call_target="tpu_custom_call" | custom-call | flops 10737418240 | bytes 33554432 | tf_op jit(solution)/shard_map/norm_backward/pallas_call | solution.py:585
  272.7 10.2 %collective-permute-done.34.ra = bf16[1,256,1024]{2,1,0:T(8,128)(2,1)S(1)} collective-permute-done((bf16[1,256,1024]{2,1,0:T(8,128)(2,1)}, bf16[1,256,1024]{2,1,0:T(8,128)(2,1)S(1)}, u32[]{:S(2)}, u32[]{:S(2)}) %collective-permute-start.34) | collective-permute-done | bytes 524320 | tf_op jit(solution)/shard_map/ppermute | solution.py:39
  289.8 12.8 %attend_backward.4.rest_0_.refs_19_.rest_1_ = bf16[3,1024,256]{2,1,0:T(8,128)(2,1)S(1)} custom-call(bf16[1024,1024]{1,0:T(8,128)(2,1)} %get-tuple-element.158.q_ref, bf16[1024,1024]{1,0:T(8,128)(2,1)} %get-tuple-element.159.k_ref, bf16[1024,1024]{1,0:T(8,128)(2,1)} %get-tuple-element.160.v_ref, bf16[1024,1024]{1,0:T(8,128)(2,1)} %get-tuple-element.207.rest_0_.da_ref, ...), custom_call_target="tpu_custom_call" | custom-call | flops 10737418240 | bytes 4718592 | tf_op jit(solution)/shard_map/attend_backward/pallas_call | solution.py:386
  313.2 12.5 %attend_backward.5.rest_0_.refs_23_.refs_9_.rest_2_ = bf16[3,1024,256]{2,1,0:T(8,128)(2,1)S(1)} custom-call(bf16[1024,1024]{1,0:T(8,128)(2,1)} %get-tuple-element.158.q_ref, bf16[1024,1024]{1,0:T(8,128)(2,1)} %get-tuple-element.159.k_ref, bf16[1024,1024]{1,0:T(8,128)(2,1)} %get-tuple-element.160.v_ref, bf16[1024,1024]{1,0:T(8,128)(2,1)} %get-tuple-element.207.rest_0_.da_ref, ...), custom_call_target="tpu_custom_call" | custom-call | flops 10737418240 | bytes 4718592 | tf_op jit(solution)/shard_map/attend_backward/pallas_call | solution.py:386
  336.3 11.7 %grad_out_qkv.1 = (bf16[2,80,1792]{2,1,0:T(8,128)(2,1)S(1)}, bf16[2,80,1792]{2,1,0:T(8,128)(2,1)S(1)}, bf16[2,80,1792]{2,1,0:T(8,128)(2,1)S(1)}, bf16[2,80,1792]{2,1,0:T(8,128)(2,1)S(1)}) custom-call(s32[4]{0:T(128)S(1)} %copy-done.47, bf16[1024,1024]{1,0:T(8,128)(2,1)} %get-tuple-element.176.a_ref.refs_1_.refs_2_.refs_3_.refs_4_, ...), custom_call_target="tpu_custom_call" | custom-call | flops 3758096384 | bytes 9437184 | tf_op jit(solution)/shard_map/grad_out_qkv/pallas_call | solution.py:775
  353.4 13.1 %attend_backward.6.rest_0_.refs_11_.refs_13_.rest_3_ = bf16[3,1024,256]{2,1,0:T(8,128)(2,1)S(1)} custom-call(bf16[1024,1024]{1,0:T(8,128)(2,1)} %get-tuple-element.158.q_ref, bf16[1024,1024]{1,0:T(8,128)(2,1)} %get-tuple-element.159.k_ref, bf16[1024,1024]{1,0:T(8,128)(2,1)} %get-tuple-element.160.v_ref, ...), custom_call_target="tpu_custom_call" | custom-call | flops 10737418240 | bytes 4718592 | tf_op jit(solution)/shard_map/attend_backward/pallas_call | solution.py:386
  375.5 8.9 %grad_qkv.2 = (bf16[2,80,1536]{2,1,0:T(8,128)(2,1)S(1)}, bf16[2,80,1536]{2,1,0:T(8,128)(2,1)S(1)}, bf16[2,80,1536]{2,1,0:T(8,128)(2,1)S(1)}, bf16[2,80,1536]{2,1,0:T(8,128)(2,1)S(1)}) custom-call(s32[4]{0:T(128)S(1)} %copy-done.47, bf16[1024,1024]{1,0:T(8,128)(2,1)} %get-tuple-element.153.refs_2_.x_ref.refs_9_.refs_10_.refs_11_.refs_12_.refs_1_.refs_3_.refs_4_, ...), custom_call_target="tpu_custom_call" | custom-call | flops 3221225472 | bytes 8388608 | tf_op jit(solution)/shard_map/grad_qkv/pallas_call | solution.py:775
  388.1 12.7 %attend_backward.7.rest_0_.refs_9_.refs_11_.rest_4_ = bf16[3,1024,256]{2,1,0:T(8,128)(2,1)S(1)} custom-call(bf16[1024,1024]{1,0:T(8,128)(2,1)S(1)} %copy-done.50, bf16[1024,1024]{1,0:T(8,128)(2,1)} %get-tuple-element.159.k_ref, bf16[1024,1024]{1,0:T(8,128)(2,1)} %get-tuple-element.160.v_ref, bf16[1024,1024]{1,0:T(8,128)(2,1)} %get-tuple-element.207.rest_0_.da_ref, ...), custom_call_target="tpu_custom_call" | custom-call | flops 10737418240 | bytes 4718592 | tf_op jit(solution)/shard_map/attend_backward/pallas_call | solution.py:386
  416.3 10.2 %input_gradient.2.rest_0_.rest_15_ = f32[512,1024]{1,0:T(8,128)} custom-call(s32[18]{0:T(128)} %stack.85.ids, f32[1024,1024]{1,0:T(8,128)} %get-tuple-element.219.dr_ref.rest_0_, f32[1024,1024]{1,0:T(8,128)} %get-tuple-element.219.dr_ref.rest_0_, bf16[3,1024,256]{2,1,0:T(8,128)(2,1)} %copy-done.6, bf16[3,1024,256]{2,1,0:T(8,128)(2,1)} %copy-done.2, ...), custom_call_target="tpu_custom_call" | custom-call | flops 3221225472 | bytes 13631488 | tf_op jit(solution)/shard_map/input_gradient/pallas_call | solution.py:818
  436.0 10.7 %input_gradient.3.rest_0_.own = f32[512,1024]{1,0:T(8,128)} custom-call(s32[18]{0:T(128)} %stack.85.ids, f32[1024,1024]{1,0:T(8,128)} %get-tuple-element.219.dr_ref.rest_0_, f32[1024,1024]{1,0:T(8,128)} %get-tuple-element.219.dr_ref.rest_0_, bf16[3,1024,256]{2,1,0:T(8,128)(2,1)} %copy-done.6, bf16[3,1024,256]{2,1,0:T(8,128)(2,1)} %copy-done.2, ...), custom_call_target="tpu_custom_call" | custom-call | flops 3221225472 | bytes 13631488 | tf_op jit(solution)/shard_map/input_gradient/pallas_call | solution.py:818
  (345 shorter events, 162.9 us)
Async XLA Ops:
  7.2 151.0 %all-gather.2.cloned.1.call-start = ((), (), s32[]{:S(2)}) async-start(), calls=%async_computation | async-start | bytes 9437184 | tf_op jit(solution)/shard_map/all_gather | solution.py:1091
  7.2 25.3 %collective-permute-start = (bf16[2,512,1024]{2,1,0:T(8,128)(2,1)}, bf16[2,512,1024]{2,1,0:T(8,128)(2,1)}, u32[]{:S(2)}, u32[]{:S(2)}) collective-permute-start(bf16[2,512,1024]{2,1,0:T(8,128)(2,1)} %refs_0_.3), channel_id=1, source_target_pairs={{0,1},{1,0},{2,3},{3,2},{4,5},{5,4},{6,7},{7,6},{8,9},{9,8},{10,11... | collective-permute-start | bytes 6291464 | tf_op jit(solution)/shard_map/ppermute | solution.py:39
  13.1 25.3 %collective-permute-start.3 = (bf16[416,1024]{1,0:T(8,128)(2,1)}, bf16[416,1024]{1,0:T(8,128)(2,1)}, u32[]{:S(2)}, u32[]{:S(2)}) collective-permute-start(bf16[416,1024]{1,0:T(8,128)(2,1)} %pack_first.1.rest_0_.rest_5_), channel_id=1, source_target_pairs={{0,4},{2,6},{4,0},{6,2},{1,5},{3,7},{5,1},{7,3},{8,12},{10,14},{12... | collective-permute-start | bytes 2555912 | tf_op jit(solution)/shard_map/ppermute | solution.py:39
  18.6 37.0 %collective-permute-start.7 = (bf16[416,1024]{1,0:T(8,128)(2,1)S(1)}, bf16[416,1024]{1,0:T(8,128)(2,1)}, u32[]{:S(2)}, u32[]{:S(2)}) collective-permute-start(bf16[416,1024]{1,0:T(8,128)(2,1)S(1)} %copy-done.61), channel_id=1, source_target_pairs={{0,1},{1,0},{2,3},{3,2},{4,5},{5,4},{6,7},{7,6},{8,9},{9,8},{10,11... | collective-permute-start | bytes 2555912 | tf_op jit(solution)/shard_map/ppermute | solution.py:39
  55.6 36.1 %collective-permute-start.12 = (bf16[128,5120]{1,0:T(8,128)(2,1)}, bf16[128,5120]{1,0:T(8,128)(2,1)S(1)}, u32[]{:S(2)}, u32[]{:S(2)}) collective-permute-start(bf16[128,5120]{1,0:T(8,128)(2,1)} %pack_up.1.refs_4_.rest_3_.rest_0_), channel_id=1, source_target_pairs={{0,2},{2,0},{4,6},{6,4},{1,3},{3,1},{5,7},{7,5},{8,10},{10,8},{12,... | collective-permute-start | bytes 3932168 | tf_op jit(solution)/shard_map/ppermute | solution.py:39
  57.1 34.6 %collective-permute-start.13 = (bf16[128,5120]{1,0:T(8,128)(2,1)}, bf16[128,5120]{1,0:T(8,128)(2,1)S(1)}, u32[]{:S(2)}, u32[]{:S(2)}) collective-permute-start(bf16[128,5120]{1,0:T(8,128)(2,1)} %pack_up.1.refs_4_.rest_3_.rest_0_), channel_id=1, source_target_pairs={{0,4},{2,6},{4,0},{6,2},{1,5},{3,7},{5,1},{7,3},{8,12},{10,14},{12... | collective-permute-start | bytes 3932168 | tf_op jit(solution)/shard_map/ppermute | solution.py:39
  91.7 33.2 %collective-permute-start.16 = (bf16[128,5120]{1,0:T(8,128)(2,1)}, bf16[128,5120]{1,0:T(8,128)(2,1)S(1)}, u32[]{:S(2)}, u32[]{:S(2)}) collective-permute-start(bf16[128,5120]{1,0:T(8,128)(2,1)} %pack_up.1.refs_4_.rest_3_.rest_0_), channel_id=1, source_target_pairs={{0,1},{1,0},{2,3},{3,2},{4,5},{5,4},{6,7},{7,6},{8,9},{9,8},{10,11... | collective-permute-start | bytes 3932168 | tf_op jit(solution)/shard_map/ppermute | solution.py:39
  95.5 27.2 %collective-permute-start.14 = (bf16[64,5120]{1,0:T(8,128)(2,1)}, bf16[64,5120]{1,0:T(8,128)(2,1)S(1)}, u32[]{:S(2)}, u32[]{:S(2)}) collective-permute-start(bf16[64,5120]{1,0:T(8,128)(2,1)} %get-tuple-element.165), channel_id=1, source_target_pairs={{0,4},{2,6},{4,0},{6,2},{1,5},{3,7},{5,1},{7,3},{8,12},{10,14},{12... | collective-permute-start | bytes 1966088 | tf_op jit(solution)/shard_map/ppermute | solution.py:39
  97.1 27.8 %collective-permute-start.15 = (bf16[64,5120]{1,0:T(8,128)(2,1)}, bf16[64,5120]{1,0:T(8,128)(2,1)S(1)}, u32[]{:S(2)}, u32[]{:S(2)}) collective-permute-start(bf16[64,5120]{1,0:T(8,128)(2,1)} %get-tuple-element.166), channel_id=1, source_target_pairs={{0,2},{2,0},{4,6},{6,4},{1,3},{3,1},{5,7},{7,5},{8,10},{10,8},{12,... | collective-permute-start | bytes 1966088 | tf_op jit(solution)/shard_map/ppermute | solution.py:39
  97.7 27.2 %collective-permute-start.17 = (bf16[128,5120]{1,0:T(8,128)(2,1)}, bf16[128,5120]{1,0:T(8,128)(2,1)S(1)}, u32[]{:S(2)}, u32[]{:S(2)}) collective-permute-start(bf16[128,5120]{1,0:T(8,128)(2,1)} %copy-done.19), channel_id=1, source_target_pairs={{0,1},{1,0},{2,3},{3,2},{4,5},{5,4},{6,7},{7,6},{8,9},{9,8},{10,11... | collective-permute-start | bytes 3932168 | tf_op jit(solution)/shard_map/ppermute | solution.py:39
  97.7 27.3 %collective-permute-start.18 = (bf16[128,5120]{1,0:T(8,128)(2,1)}, bf16[128,5120]{1,0:T(8,128)(2,1)S(1)}, u32[]{:S(2)}, u32[]{:S(2)}) collective-permute-start(bf16[128,5120]{1,0:T(8,128)(2,1)} %copy-done.21), channel_id=1, source_target_pairs={{0,1},{1,0},{2,3},{3,2},{4,5},{5,4},{6,7},{7,6},{8,9},{9,8},{10,11... | collective-permute-start | bytes 3932168 | tf_op jit(solution)/shard_map/ppermute | solution.py:39
  157.3 31.1 %collective-permute-start.21 = (bf16[1024,4096]{1,0:T(8,128)(2,1)}, bf16[1024,4096]{1,0:T(8,128)(2,1)}, u32[]{:S(2)}, u32[]{:S(2)}) collective-permute-start(bf16[1024,4096]{1,0:T(8,128)(2,1)} %get-tuple-element.169.g_ref.lo), channel_id=1, source_target_pairs={{0,1},{1,0},{2,3},{3,2},{4,5},{5,4},{6,7},{7,6},{8,9},{9,8},{10,11... | collective-permute-start | bytes 25165832 | tf_op jit(solution)/shard_map/ppermute | solution.py:39
  217.0 25.6 %collective-permute-start.27 = (bf16[2,256,1024]{2,1,0:T(8,128)(2,1)}, bf16[2,256,1024]{2,1,0:T(8,128)(2,1)S(1)}, u32[]{:S(2)}, u32[]{:S(2)}) collective-permute-start(bf16[2,256,1024]{2,1,0:T(8,128)(2,1)} %get-tuple-element.188), channel_id=1, source_target_pairs={{0,2},{2,0},{4,6},{6,4},{1,3},{3,1},{5,7},{7,5},{8,10},{10,8},{12,... | collective-permute-start | bytes 3145736 | tf_op jit(solution)/shard_map/ppermute | solution.py:39
  218.1 25.1 %collective-permute-start.28 = (bf16[2,256,1024]{2,1,0:T(8,128)(2,1)}, bf16[2,256,1024]{2,1,0:T(8,128)(2,1)S(1)}, u32[]{:S(2)}, u32[]{:S(2)}) collective-permute-start(bf16[2,256,1024]{2,1,0:T(8,128)(2,1)} %get-tuple-element.190), channel_id=1, source_target_pairs={{0,4},{2,6},{4,0},{6,2},{1,5},{3,7},{5,1},{7,3},{8,12},{10,14},{12... | collective-permute-start | bytes 3145736 | tf_op jit(solution)/shard_map/ppermute | solution.py:39
  246.4 40.4 %collective-permute-start.30 = (bf16[2,64,4096]{2,1,0:T(8,128)(2,1)}, bf16[2,64,4096]{2,1,0:T(8,128)(2,1)S(1)}, u32[]{:S(2)}, u32[]{:S(2)}) collective-permute-start(bf16[2,64,4096]{2,1,0:T(8,128)(2,1)} %get-tuple-element.201), channel_id=1, source_target_pairs={{0,2},{2,0},{4,6},{6,4},{1,3},{3,1},{5,7},{7,5},{8,10},{10,8},{12,... | collective-permute-start | bytes 3145736 | tf_op jit(solution)/shard_map/ppermute | solution.py:39
  247.6 39.3 %collective-permute-start.31 = (bf16[2,64,4096]{2,1,0:T(8,128)(2,1)}, bf16[2,64,4096]{2,1,0:T(8,128)(2,1)S(1)}, u32[]{:S(2)}, u32[]{:S(2)}) collective-permute-start(bf16[2,64,4096]{2,1,0:T(8,128)(2,1)} %get-tuple-element.203), channel_id=1, source_target_pairs={{0,4},{2,6},{4,0},{6,2},{1,5},{3,7},{5,1},{7,3},{8,12},{10,14},{12... | collective-permute-start | bytes 3145736 | tf_op jit(solution)/shard_map/ppermute | solution.py:39
  249.1 33.8 %collective-permute-start.34 = (bf16[1,256,1024]{2,1,0:T(8,128)(2,1)}, bf16[1,256,1024]{2,1,0:T(8,128)(2,1)S(1)}, u32[]{:S(2)}, u32[]{:S(2)}) collective-permute-start(bf16[1,256,1024]{2,1,0:T(8,128)(2,1)} %get-tuple-element.193.rest_11_), channel_id=1, source_target_pairs={{0,4},{2,6},{4,0},{6,2},{1,5},{3,7},{5,1},{7,3},{8,12},{10,14},{12... | collective-permute-start | bytes 1572872 | tf_op jit(solution)/shard_map/ppermute | solution.py:39
  249.6 33.3 %collective-permute-start.35 = (bf16[1,256,1024]{2,1,0:T(8,128)(2,1)S(1)}, bf16[1,256,1024]{2,1,0:T(8,128)(2,1)S(1)}, u32[]{:S(2)}, u32[]{:S(2)}) collective-permute-start(bf16[1,256,1024]{2,1,0:T(8,128)(2,1)S(1)} %get-tuple-element.195.rest_13_), channel_id=1, source_target_pairs={{0,2},{2,0},{4,6},{6,4},{1,3},{3,1},{5,7},{7,5},{8,10},{10,8},{12,... | collective-permute-start | bytes 1572872 | tf_op jit(solution)/shard_map/ppermute | solution.py:39
  250.5 56.5 %collective-permute-start.29 = (bf16[1024,1024]{1,0:T(8,128)(2,1)}, bf16[1024,1024]{1,0:T(8,128)(2,1)}, u32[]{:S(2)}, u32[]{:S(2)}) collective-permute-start(bf16[1024,1024]{1,0:T(8,128)(2,1)} %get-tuple-element.217.own), channel_id=1, source_target_pairs={{0,1},{1,0},{2,3},{3,2},{4,5},{5,4},{6,7},{7,6},{8,9},{9,8},{10,11... | collective-permute-start | bytes 6291464 | tf_op jit(solution)/shard_map/ppermute | solution.py:39
  304.4 26.4 %collective-permute-start.41 = (bf16[256,1024]{1,0:T(8,128)(2,1)S(1)}, bf16[256,1024]{1,0:T(8,128)(2,1)S(1)}, u32[]{:S(2)}, u32[]{:S(2)}) collective-permute-start(bf16[256,1024]{1,0:T(8,128)(2,1)S(1)} %sum_rep.11.rest_3_.a), channel_id=1, source_target_pairs={{0,16},{8,24},{16,0},{24,8},{1,17},{9,25},{17,1},{25,9},{2,18},{10... | collective-permute-start | bytes 1572872 | tf_op jit(solution)/shard_map/ppermute | solution.py:39
  332.2 34.6 %collective-permute-start.47 = (bf16[256,1024]{1,0:T(8,128)(2,1)S(1)}, bf16[256,1024]{1,0:T(8,128)(2,1)S(1)}, u32[]{:S(2)}, u32[]{:S(2)}) collective-permute-start(bf16[256,1024]{1,0:T(8,128)(2,1)S(1)} %sum_rep.13.refs_25_.kept), channel_id=1, source_target_pairs={{0,8},{8,0},{16,24},{24,16},{1,9},{9,1},{17,25},{25,17},{2,10},{10... | collective-permute-start | bytes 1572872 | tf_op jit(solution)/shard_map/ppermute | solution.py:39
  335.6 30.9 %collective-permute-start.46 = (bf16[32,4096]{1,0:T(8,128)(2,1)S(1)}, bf16[32,4096]{1,0:T(8,128)(2,1)S(1)}, u32[]{:S(2)}, u32[]{:S(2)}) collective-permute-start(bf16[32,4096]{1,0:T(8,128)(2,1)S(1)} %get-tuple-element.289.a), channel_id=1, source_target_pairs={{0,16},{8,24},{16,0},{24,8},{1,17},{9,25},{17,1},{25,9},{2,18},{10... | collective-permute-start | bytes 786440 | tf_op jit(solution)/shard_map/ppermute | solution.py:39
  371.4 29.4 %collective-permute-start.54 = (bf16[64,4096]{1,0:T(8,128)(2,1)S(1)}, bf16[64,4096]{1,0:T(8,128)(2,1)S(1)}, u32[]{:S(2)}, u32[]{:S(2)}) collective-permute-start(bf16[64,4096]{1,0:T(8,128)(2,1)S(1)} %pad_maximum_fusion.kept), channel_id=1, source_target_pairs={{0,8},{8,0},{16,24},{24,16},{1,9},{9,1},{17,25},{25,17},{2,10},{10... | collective-permute-start | bytes 1572872 | tf_op jit(solution)/shard_map/ppermute | solution.py:39
  432.3 26.2 %collective-permute-start.62 = (f32[512,1024]{1,0:T(8,128)S(1)}, f32[512,1024]{1,0:T(8,128)}, u32[]{:S(2)}, u32[]{:S(2)}) collective-permute-start(f32[512,1024]{1,0:T(8,128)S(1)} %copy-done.5), channel_id=1, source_target_pairs={{0,1},{1,0},{2,3},{3,2},{4,5},{5,4},{6,7},{7,6},{8,9},{9,8},{10,11... | collective-permute-start | bytes 6291464 | tf_op jit(solution)/shard_map/ppermute | solution.py:39
  (122 other events, 1118.0 us)
Sparse Core Ops, SparseCore 0:
  91.8 64.7 all-gather.1
